TPU v7x, 32 devices: a whole 2x2x4 slice. The times are simulated.
32 devices in a mesh: dp: 8 (over z, x), tensor: 4 (over y, core).
Axes of the slice: x: 2, y: 2, z: 4, core: 2. Of those that a mesh axis runs over, the one named last changes fastest.
Arguments:
- tokens_in: bfloat16 [4096, 768], P(('dp', 'tensor')), may hold values from -6 to 6
- out_grad: bfloat16 [4096, 768], P(('dp', 'tensor')), may hold values from -6 to 6
- lengths: int32 [8, 6], P('dp'), may hold values from 1 to 197, 512 in all within a row
- owners: int32 [72], replicated, may hold values from 0 to 7, as said below
- weight_store: float32 [80, 256, 768], P('dp', 'tensor'), may hold values from -1 to 1
- first_store: float32 [80, 256, 768], P('dp', 'tensor'), may hold values from -4096 to 4096
- second_store: float32 [80, 256, 768], P('dp', 'tensor'), may hold values from 512 to 8192
- shared_params: float32 [2, 8, 768], replicated, may hold values from -2 to 2, as said below
- shared_first: float32 [2, 8, 768], replicated, may hold values from -4096 to 4096
- shared_second: float32 [2, 8, 768], replicated, may hold values from 2048 to 32768
- split_params: float32 [2, 4, 3348], P(None, 'tensor'), may hold values from -3 to 3
- split_first: float32 [2, 4, 3348], P(None, 'tensor'), may hold values from -4096 to 4096
- split_second: float32 [2, 4, 3348], P(None, 'tensor'), may hold values from 512 to 8192
Outputs:
- block_out: bfloat16 [4096, 768], P(('dp', 'tensor'))
- input_grad: float32 [4096, 768], P(('dp', 'tensor'))
- matrix_grad: float32 [80, 256, 768], P('dp', 'tensor')
- matrix_first: float32 [80, 256, 768], P('dp', 'tensor')
- matrix_second: float32 [80, 256, 768], P('dp', 'tensor')
- matrix_weight: float32 [80, 256, 768], P('dp', 'tensor')
- shared_grad: float32 [2, 8, 768], replicated
- shared_moment: float32 [2, 8, 768], replicated
- shared_square: float32 [2, 8, 768], replicated
- shared_value: float32 [2, 8, 768], replicated
- split_grad: float32 [2, 4, 3348], P(None, 'tensor')
- split_moment: float32 [2, 4, 3348], P(None, 'tensor')
- split_square: float32 [2, 4, 3348], P(None, 'tensor')
- split_value: float32 [2, 4, 3348], P(None, 'tensor')
Inputs may be any that keep to these rules, and one draw needn't show every extreme that they name: `owners`: no owner holds more than 10 blocks and some owner holds exactly 10. `lengths`: each row sums to 512. `shared_params`: rows 0, 2, 4, 6 lie in 0.7 to 1.3.
All inputs are finite; a program needn't handle non-finite values.
Results may differ from a plain program's by a relative error of at most 0.025.
Values may be sent and summed in bfloat16 or wider, within the bound.
No kernel may reach another device: no remote copies, remote signals or barrier semaphores. Data moves between devices by JAX's collectives and lax.ppermute only.
A program may use at most 192 MiB of HBM per device.

v0:
```python
import functools

import jax
import jax.numpy as jnp
from jax import lax
from jax.experimental import pallas as pl
from jax.experimental.pallas import tpu as pltpu
from jax.sharding import Mesh
from jax.sharding import PartitionSpec as P

D = 768
HEADS = 12
HEAD = 64
FF = 3072
GRID = 14
LAYERS = 2
STEP = 10
RELS = 732
SIDE = 2 * GRID - 1

PITCH = 16
CODES = 256
CLASS_CODE = GRID * PITCH
SPREAD = 512

PACK_B1 = 5
PACK_TABLE = 11
PACK_ENDS = 43
PACKED = 48

norm_eps = 1e-06
beta_first = 0.5
beta_second = 0.5
adam_eps = 1e-08
rate_matrix = 0.05
rate_small = 0.3
weight_decay = 0.05
masked_score = -1e30

f32 = jnp.float32
bf16 = jnp.bfloat16
MIB = 1 << 20
SCALE = 1e9


def iota(shape, axis):
    return lax.broadcasted_iota(jnp.int32, shape, axis)


def matmul(a, b):
    return jnp.dot(a, b, preferred_element_type=f32)


def matmul_nt(a, b):
    return lax.dot_general(a, b, (((1,), (1,)), ((), ())), preferred_element_type=f32)


def matmul_tn(a, b):
    return lax.dot_general(a, b, (((0,), (0,)), ((), ())), preferred_element_type=f32)


def two_parts(v):
    high = v.astype(bf16)
    return high, (v - high.astype(f32)).astype(bf16)


VMEM, SMEM, STAY, FAR = "vmem", "smem", "stay", "far"


def call(kernel, outs, args, name, us, scratch=(), limit=16, alias=None, **options):
    args = [a if isinstance(a, tuple) else (a, VMEM) for a in args]
    spaces = {VMEM: pltpu.VMEM, SMEM: pltpu.SMEM, FAR: pltpu.HBM}
    colors = {STAY: pltpu.VMEM, FAR: pltpu.HBM, VMEM: jax.ShapeDtypeStruct}
    in_specs = [pl.BlockSpec(memory_space=spaces[place]) for _, place in args]
    args = [
        (pltpu.with_memory_space_constraint(a, pltpu.HBM) if place == FAR else a, place)
        for a, place in args
    ]
    outs = [out if len(out) == 3 else (*out, VMEM) for out in outs]
    shapes = [colors[place](shape, dtype) for shape, dtype, place in outs]
    return pl.pallas_call(
        functools.partial(kernel, **options),
        out_shape=shapes,
        in_specs=in_specs,
        out_specs=[
            pl.BlockSpec(memory_space=pltpu.HBM if place == FAR else pltpu.VMEM) for _, _, place in outs
        ],
        scratch_shapes=list(scratch),
        input_output_aliases={alias + i: i for i in range(len(outs))} if alias is not None else {},
        compiler_params=pltpu.CompilerParams(vmem_limit_bytes=limit * MIB),
        cost_estimate=pl.CostEstimate(flops=int(us * SCALE), bytes_accessed=1, transcendentals=0),
        name=name,
    )(*[a for a, _ in args])


def swap(v, axis):
    return lax.ppermute(v, axis, [(0, 1), (1, 0)])


class Line:
    def __init__(self, ahead=1):
        self.come, self.ahead = [], ahead

    def send(self, v, axis, perm):
        if len(self.come) >= self.ahead:
            v = after(v, self.come[-self.ahead])
        self.come.append(lax.ppermute(v, axis, perm))
        return self.come[-1]


SWAP = [(0, 1), (1, 0)]
AHEAD = 1


def spans(order, capacity):
    pieces = []
    for s, parts in order:
        cuts = [capacity * i // parts for i in range(parts + 1)]
        pieces += [(s, a, b) for a, b in zip(cuts, cuts[1:])]
    return pieces


def gather_order(nz, capacity):
    if nz != 4:
        return spans([(s, 1) for s in range(nz)], capacity)
    return spans([(0, 1), (1, 1), (2, 2), (3, 2)], capacity)


def scatter_order(nz, capacity):
    if nz != 4:
        return spans([(s, 1) for s in range(1, nz)] + [(0, 1)], capacity)
    return spans([(2, 2), (1, 1), (3, 1), (0, 1)], capacity)


def gather_stores(store, order):
    nz = lax.axis_size("z")
    along_z, along_x = Line(AHEAD), Line()
    near, far = [], []
    for s, start, stop in order:
        piece = store if stop - start == store.shape[0] else store[start:stop]
        if s:
            piece = along_z.send(piece, "z", [((i + s) % nz, i) for i in range(nz)])
        near.append(piece)
        far.append(along_x.send(piece, "x", SWAP))
    return near + far


class ScatterSums:
    def __init__(self, grads, order):
        self.grads, self.order = grads, order
        self.along_z, self.along_x = Line(AHEAD), Line()
        self.totals, self.part, self.next = {}, None, 0

    def step(self):
        nz = lax.axis_size("z")
        s, _, _ = self.order[self.next]
        ours, theirs = self.grads[self.next], self.grads[len(self.order) + self.next]
        got = self.along_x.send(theirs, "x", SWAP)
        if self.part is not None:
            ours = after(ours, self.part)
        self.part = ours.astype(f32) + got.astype(f32)
        term = self.part
        if s:
            self.part = self.part.astype(bf16)
            term = self.along_z.send(self.part, "z", [(k, (k + s) % nz) for k in range(nz)])
        self.totals.setdefault(s, []).append(term)
        self.next += 1

    def result(self):
        totals = [jnp.concatenate(v, axis=0) if len(v) > 1 else v[0] for v in self.totals.values()]
        return sum(v.astype(f32) for v in totals)


def after(v, *others):
    return lax.optimization_barrier((v,) + others)[0]


def sum_over(v, axis):
    size = lax.axis_size(axis)
    step = 1
    while step < size:
        v = v + lax.ppermute(v, axis, [(i, i ^ step) for i in range(size)])
        step *= 2
    return v


def deal_kernel(near_unit, *refs, low, order):
    *blocks, first, second, third, semaphores = refs
    nz = near_unit.shape[0] // 2
    group = first.shape[0]
    outs = (first, second, third)
    for i, block in enumerate(blocks):
        s, start, stop = order[i % len(order)]
        owner = s + nz * (i // len(order))
        for k in range(stop - start):
            unit = near_unit[owner, start + k] - low
            for j, out in enumerate(outs):

                @pl.when((unit >= j * group) & (unit < (j + 1) * group))
                def _():
                    pltpu.make_async_copy(block.at[k], out.at[unit - j * group], semaphores.at[j]).start()

    for j, out in enumerate(outs):
        pltpu.make_async_copy(out, out, semaphores.at[j]).wait()


def lifting(rows):
    return jnp.where(
        SIDE - 1 - iota((rows, SPREAD), 1) // PITCH == iota((rows, SPREAD), 0), 1.0, 0.0
    ).astype(bf16)


def column_offset():
    return iota((32, SPREAD), 0) + (iota((32, SPREAD), 1) % PITCH) - (GRID - 1)


def prepare_kernel(
    table, ends, code_c, seg_c, code_r, seg_r, hot, hot_t, *rest
):
    *biases, spread, tile = rest
    heads = table.shape[0] // len(biases)
    tokens = code_c.shape[0]
    hot[...] = jnp.where(code_c[...] == iota((tokens, CODES), 1), 1.0, 0.0).astype(bf16)
    hot_t[...] = jnp.where(code_r[...] == iota((CODES, tokens), 0), 1.0, 0.0).astype(bf16)
    lift = lifting(32)
    offset = column_offset()
    spread[...] = jnp.zeros(spread.shape, f32)
    for h in range(table.shape[0]):
        high, low = two_parts(table[h])
        lifted = matmul_tn(high, lift) + matmul_tn(low, lift)
        for c in range(GRID):
            line = jnp.sum(jnp.where(offset == c, lifted, 0.0), axis=0, keepdims=True)
            spread[h, c : c + 1, :] = line
    row = iota((CODES, CODES), 0)
    col = iota((CODES, CODES), 1)
    for level, bias in enumerate(biases):

        def one(head, carry):
            h = level * heads + head
            lines = spread[h]
            for r in range(GRID):
                back = (GRID - 1 - r) * PITCH
                moved = pltpu.roll(lines, (SPREAD - back) % SPREAD, 1) if back else lines
                tile[r * PITCH : (r + 1) * PITCH, :] = moved[:, :CODES]
            tile[CLASS_CODE:, :] = jnp.zeros((CODES - CLASS_CODE, CODES), f32)
            full = jnp.where(row == CLASS_CODE, ends[h, 0], tile[...])
            full = jnp.where(col == CLASS_CODE, ends[h, 1], full)
            full = jnp.where((col == CLASS_CODE) & (row == CLASS_CODE), ends[h, 2], full)
            high, low = two_parts(full)
            left_high = matmul(hot[...], high).astype(bf16)
            left_low = matmul(hot[...], low).astype(bf16)
            values = matmul(left_high, hot_t[...]) + matmul(left_low, hot_t[...])
            bias[head] = jnp.where(seg_c[...] == seg_r[...], values, masked_score)
            return carry

        lax.fori_loop(0, heads, one, 0)


def normed(v):
    center = v - jnp.mean(v, axis=-1, keepdims=True)
    inverse = lax.rsqrt(jnp.mean(center * center, axis=-1, keepdims=True) + norm_eps)
    return center * inverse, inverse


def start_kernel(tokens, grads, near, shared, x, low, x_saved, upper, e):
    rows = tokens.shape[0]
    x[:rows, :] = tokens[...].astype(f32)
    x[rows:, :] = near[:rows, :].astype(f32)
    x_saved[...] = x[...]
    hat, _ = normed(x[...])
    low[...] = (hat * shared[0, 0:1, :] + shared[0, 1:2, :]).astype(bf16)
    upper[:rows, :] = grads[...].astype(f32)
    upper[rows:, :] = near[rows:, :].astype(f32)
    e[...] = (shared[LAYERS - 1, 6:7, :] * upper[...]).astype(bf16)


def attention_kernel(a0, a1, vector, bias, w, qkv, mixed, logs, a0_saved, a1_saved, keep, send):
    a0_saved[...] = a0[...]
    a1_saved[...] = a1[...]
    half = a0.shape[0]
    heads = bias.shape[0]
    width = heads * HEAD
    out = qkv
    for i, a in enumerate((a0, a1)):
        rows = pl.ds(i * half, half)
        proj = matmul_nt(a[...], w[: 3 * width, :]) + vector[:, : 3 * width]
        out[rows, :] = proj.astype(bf16)
    bias = bias
    parts = []
    for h in range(heads):
        q = out[:, h * HEAD : (h + 1) * HEAD] * jnp.asarray(HEAD**-0.5, bf16)
        k = out[:, width + h * HEAD : width + (h + 1) * HEAD]
        v = out[:, 2 * width + h * HEAD : 2 * width + (h + 1) * HEAD]
        s = matmul_nt(q, k) + bias[h]
        top = jnp.max(s, axis=-1, keepdims=True)
        e = jnp.exp(s - top)
        total = jnp.sum(e, axis=-1, keepdims=True)
        p = (e * (1.0 / total)).astype(bf16)
        parts.append(matmul(p, v))
        logs[:, h : h + 1] = top + jnp.log(total)
    mixed[...] = jnp.concatenate(parts, axis=1).astype(bf16)
    w_out = w[3 * width :, :]
    keep[...] = matmul(mixed[:half, :], w_out).astype(bf16)
    send[...] = matmul(mixed[half:, :], w_out).astype(bf16)


def attention_back_kernel(
    e0, e1, w_true, qkv, logs, bias, d_qkv, d_scores, e0_saved, e1_saved, keep, send
):
    e0_saved[...] = e0[...]
    e1_saved[...] = e1[...]
    half = e0.shape[0]
    heads = bias.shape[0]
    width = heads * HEAD
    scale = HEAD**-0.5
    w = w_true
    w_out = w[3 * width :, :]
    d_mixed = jnp.concatenate(
        [matmul_nt(e0[...], w_out), matmul_nt(e1[...], w_out)], axis=0
    ).astype(bf16)
    qkv, logs, bias = qkv, logs, bias
    dq, dk, dv = [], [], []
    for h in range(heads):
        q = qkv[:, h * HEAD : (h + 1) * HEAD] * jnp.asarray(scale, bf16)
        k = qkv[:, width + h * HEAD : width + (h + 1) * HEAD]
        v = qkv[:, 2 * width + h * HEAD : 2 * width + (h + 1) * HEAD]
        g = d_mixed[:, h * HEAD : (h + 1) * HEAD]
        p = jnp.exp(matmul_nt(q, k) + bias[h] - logs[:, h : h + 1])
        dp = matmul_nt(g, v)
        pdp = p * dp
        ds = (pdp - p * jnp.sum(pdp, axis=-1, keepdims=True)).astype(bf16)
        d_scores[h] = ds
        dq.append(matmul(ds, k) * scale)
        dk.append(matmul_tn(ds, q))
        dv.append(matmul_tn(p.astype(bf16), g))
    out = d_qkv
    out[...] = jnp.concatenate(dq + dk + dv, axis=1).astype(bf16)
    keep[...] = matmul(out[:half, :], w[: 3 * width, :]).astype(bf16)
    send[...] = matmul(out[half:, :], w[: 3 * width, :]).astype(bf16)


def table_kernel(d_qkv, d_b1, scores, hot, hot_t, packed):
    heads = scores.shape[0]
    width = heads * HEAD
    packed[...] = jnp.zeros(packed.shape, f32)
    line = jnp.sum(d_qkv[...].astype(f32), axis=0, keepdims=True)
    for start in range(0, 3 * width, 128):
        stop = min(start + 128, 3 * width)
        packed[start // 128 : start // 128 + 1, : stop - start] = line[:, start:stop]
    line = d_b1[...]
    for start in range(0, line.shape[1], 128):
        at = PACK_B1 + start // 128
        packed[at : at + 1, :] = line[:, start : start + 128]
    lift = lifting(32)
    offset = column_offset()
    row = iota((CODES, CODES), 0)
    col = iota((CODES, CODES), 1)
    for h in range(heads):
        high, low = two_parts(matmul(hot_t[...], scores[h]))
        tile = matmul(high, hot[...]) + matmul(low, hot[...])
        class_row = jnp.where(row == CLASS_CODE, tile, 0.0)
        class_col = jnp.where(col == CLASS_CODE, tile, 0.0)
        both = jnp.where(col == CLASS_CODE, class_row, 0.0)
        both_sum = jnp.sum(both, keepdims=True)
        row_sum = jnp.sum(class_row, keepdims=True) - both_sum
        col_sum = jnp.sum(class_col, keepdims=True) - both_sum
        lane = iota((1, 128), 1)
        packed[PACK_ENDS + h : PACK_ENDS + h + 1, :] = jnp.where(
            lane == 0, row_sum, jnp.where(lane == 1, col_sum, jnp.where(lane == 2, both_sum, 0.0))
        )
        inner = jnp.where((row < CLASS_CODE) & (col < CLASS_CODE), tile, 0.0)
        lines = jnp.zeros((PITCH, SPREAD), f32)
        for r in range(GRID):
            wide = jnp.concatenate(
                [inner[r * PITCH : (r + 1) * PITCH, :], jnp.zeros((PITCH, SPREAD - CODES), f32)],
                axis=1,
            )
            shift = (GRID - 1 - r) * PITCH
            lines = lines + (pltpu.roll(wide, shift, 1) if shift else wide)
        spread = jnp.zeros((32, SPREAD), f32)
        for c in range(GRID):
            spread = spread + jnp.where(offset == c, lines[c : c + 1, :], 0.0)
        high, low = two_parts(spread)
        packed[PACK_TABLE : PACK_TABLE + 32, 32 * h : 32 * h + 32] = matmul_nt(
            lift, high
        ) + matmul_nt(lift, low)


def gelu_parts(z):
    cdf = 0.5 * (1.0 + lax.erf(z * (0.5**0.5)))
    density = jnp.exp(-0.5 * z * z) * 0.3989422804014327
    return z * cdf, cdf + z * density


def hidden_kernel(c0, c1, b1, w1, w2, u, slope, c0_saved, c1_saved, keep, send):
    c0_saved[...] = c0[...]
    c1_saved[...] = c1[...]
    rows = c0.shape[0]
    cols = w1.shape[0] // 2
    for i, (c, out) in ((1, (c1, send)), (0, (c0, keep))):
        span = pl.ds(i * rows, rows)
        total = None
        for j in range(2):
            lanes = slice(j * cols, (j + 1) * cols)
            z = matmul_nt(c[...], w1[lanes, :]) + b1[:, lanes]
            value, grade = gelu_parts(z)
            value = value.astype(bf16)
            u[span, lanes] = value
            slope[span, lanes] = grade
            part = matmul(value, w2[lanes, :])
            total = part if total is None else total + part
        out[...] = total.astype(bf16)


def hidden_back_kernel(e0, e1, w1, w2, slope, dz, e0_saved, e1_saved, d_b1, keep, send):
    e0_saved[...] = e0[...]
    e1_saved[...] = e1[...]
    rows = e0.shape[0]
    cols = w1.shape[0] // 2
    w2, slope, w1 = w2, slope, w1
    sums = [None, None]
    for i, (e, out) in ((1, (e1, send)), (0, (e0, keep))):
        span = pl.ds(i * rows, rows)
        total = None
        for j in range(2):
            lanes = slice(j * cols, (j + 1) * cols)
            grad = matmul_nt(e[...], w2[lanes, :]) * slope[span, lanes]
            line = jnp.sum(grad, axis=0, keepdims=True)
            sums[j] = line if sums[j] is None else sums[j] + line
            grad = grad.astype(bf16)
            dz[span, lanes] = grad
            part = matmul(grad, w1[lanes, :])
            total = part if total is None else total + part
        out[...] = total.astype(bf16)
    d_b1[...] = jnp.concatenate(sums, axis=1)


def put_blocks(blocks, near_slot, first, outs, capacity, semaphore):
    for u in range(blocks.shape[0]):
        place = near_slot[first + u]
        if len(outs) == 1:
            pltpu.make_async_copy(blocks.at[u], outs[0].at[place], semaphore).start()
            continue
        for j, out in enumerate(outs):

            @pl.when((place >= j * capacity) & (place < (j + 1) * capacity))
            def _():
                pltpu.make_async_copy(blocks.at[u], out.at[place - j * capacity], semaphore).start()


def weights_kernel(near_slot, left0, right00, right01, left1, right10, right11, *refs, first, count, capacity):
    *refs, blocks, semaphore = refs
    outs = refs[-count:]
    half = right00.shape[0]
    at = 0
    for left, right0, right1 in ((left0, right00, right01), (left1, right10, right11)):
        grad = matmul_tn(left[:half, :], right0[...]) + matmul_tn(left[half:, :], right1[...])
        stop = at + grad.shape[0] // HEAD
        blocks[at:stop] = grad.astype(bf16).reshape(stop - at, HEAD, grad.shape[1])
        put_blocks(blocks.at[at:stop], near_slot, first + at, outs, capacity, semaphore)
        at = stop
    pltpu.make_async_copy(blocks, blocks, semaphore).wait()


def both_sums(ours, theirs):
    rows = ours.shape[0] // 2
    return jnp.concatenate(
        [
            ours[:rows, :].astype(f32) + theirs[rows:, :].astype(f32),
            ours[rows:, :].astype(f32) + theirs[:rows, :].astype(f32),
        ],
        axis=0,
    )


def join(level, kind):
    def kernel(ours, theirs, x, shared, x_next, low, branch, x_saved):
        rows = branch.shape[0]
        here = (level, 2, 3) if kind == 0 else (level, 6, 7)
        then = (level, 4, 5) if kind == 0 else (level + 1, 0, 1)
        y = both_sums(ours, theirs) + shared[here[0], here[2] : here[2] + 1, :]
        branch[...] = y[:rows, :]
        value = x[...] + shared[here[0], here[1] : here[1] + 1, :] * y
        x_next[...] = value
        x_saved[...] = x_next[...]
        hat, _ = normed(value)
        gain, shift = (shared[then[0], i : i + 1, :] for i in then[1:])
        low[...] = (hat * gain + shift).astype(bf16)

    return kernel


def through_norm(d_normed, x, upper, gain):
    hat, inverse = normed(x)
    d_hat = d_normed * gain
    mean_a = jnp.mean(d_hat, axis=-1, keepdims=True)
    mean_b = jnp.mean(d_hat * hat, axis=-1, keepdims=True)
    return upper + inverse * (d_hat - mean_a - hat * mean_b), d_normed * hat


def join_back(gain_at, scale_at):
    def kernel(ours, theirs, x, upper, branch, shared, dx, low, sums):
        rows = branch.shape[0]
        gain, scale = (shared[i, j : j + 1, :] for i, j in (gain_at, scale_at))
        d_normed = both_sums(ours, theirs)
        value, product = through_norm(d_normed, x[...], upper[...], gain)
        dx[...] = value
        e = scale * value
        low[...] = e.astype(bf16)
        sums[0:1, :] = jnp.sum(product[:rows, :], axis=0, keepdims=True)
        sums[1:2, :] = jnp.sum(d_normed[:rows, :], axis=0, keepdims=True)
        sums[2:3, :] = jnp.sum(value[:rows, :] * branch[...], axis=0, keepdims=True)
        sums[3:4, :] = jnp.sum(e[:rows, :], axis=0, keepdims=True)

    return kernel


def last_back_kernel(ours, theirs, x, upper, shared, dx, sums):
    rows = dx.shape[0]
    d_normed = ours[:rows, :].astype(f32) + theirs[...].astype(f32)
    value, product = through_norm(d_normed, x[:rows, :], upper[:rows, :], shared[0, 0:1, :])
    dx[...] = value
    sums[0:1, :] = jnp.sum(product, axis=0, keepdims=True)
    sums[1:2, :] = jnp.sum(d_normed, axis=0, keepdims=True)


def adam_step(weight, first, second, grad, rate, decay):
    first_new = beta_first * first + (1.0 - beta_first) * grad
    second_new = beta_second * second + (1.0 - beta_second) * grad * grad
    fix_first = 1.0 - beta_first**STEP
    fix_second = 1.0 - beta_second**STEP
    weight_new = weight - rate * (
        first_new / fix_first / (jnp.sqrt(second_new / fix_second) + adam_eps) + decay * weight
    )
    return (first_new, second_new, weight_new)


def image_layout(row_lengths, count):
    endings = jnp.cumsum(row_lengths)
    openings = endings - row_lengths
    places = jnp.arange(count, dtype=jnp.int32)
    inside = places[:, None] >= openings[None, :]
    segment = jnp.sum(inside.astype(jnp.int32), axis=1) - 1
    opening = jnp.max(jnp.where(inside, openings[None, :], 0), axis=1)
    return (segment, places - opening)


def unit_slots(owners, capacity):
    count = owners.shape[0]
    order = jnp.arange(count, dtype=jnp.int32)
    same_owner = owners[:, None] == owners[None, :]
    earlier = order[None, :] < order[:, None]
    rank = jnp.sum((same_owner & earlier).astype(jnp.int32), axis=1)
    return owners * capacity + rank


def per_device(
    tokens_in,
    out_grad,
    lengths,
    owners,
    weight_store,
    first_store,
    second_store,
    shared_params,
    shared_first,
    shared_second,
    split_params,
    split_first,
    split_second,
):
    nz = lax.axis_size("z")
    owners_all = nz * 2
    parts = 4
    heads_here = HEADS // parts
    width = heads_here * HEAD
    hidden = FF // parts
    rows = tokens_in.shape[0]
    tokens = rows * parts
    half = tokens // 2
    capacity = weight_store.shape[0]
    my_z, my_x = lax.axis_index("z"), lax.axis_index("x")
    my_y, my_c = lax.axis_index("y"), lax.axis_index("core")

    slots = unit_slots(owners, capacity)
    order = gather_order(nz, capacity)
    blocks = gather_stores(weight_store.astype(bf16), order)

    group = hidden // HEAD
    near_x = (my_x + jnp.arange(2, dtype=jnp.int32)) % 2
    near_z = (my_z + jnp.arange(nz, dtype=jnp.int32)) % nz
    owner_of = (near_z[None, :] * 2 + near_x[:, None]).reshape(-1)
    unit_ids = jnp.arange(slots.shape[0], dtype=jnp.int32)
    near_slots = owner_of[:, None] * capacity + jnp.arange(capacity, dtype=jnp.int32)[None, :]
    near_match = near_slots[:, :, None] == slots[None, None, :]
    near_unit = jnp.sum(jnp.where(near_match, unit_ids, 0), axis=2)
    near_unit = jnp.where(jnp.any(near_match, axis=2), near_unit, slots.shape[0])
    back_order = scatter_order(nz, capacity)
    in_pieces = owners_all == 8
    near_ids = [[0] * capacity for _ in range(owners_all)]
    for i, (s, start, stop) in enumerate(back_order):
        for x in range(2):
            for k in range(start, stop):
                near_ids[x * nz + s][k] = (x * len(back_order) + i) * capacity + k - start
    if not in_pieces:
        near_ids = [[p * capacity + k for k in range(capacity)] for p in range(owners_all)]
    near_ids = jnp.asarray(near_ids, jnp.int32)[:, :, None]
    near_slot = jnp.sum(jnp.where(near_match, near_ids, 0), axis=(0, 1))

    segment, position = image_layout(lengths[0], tokens)
    patch = position - 1
    code = jnp.where(position == 0, CLASS_CODE, (patch // GRID) * PITCH + patch % GRID)

    def local(v):
        v = jnp.roll(v.reshape(2, 2, rows), (-my_y, -my_c), (0, 1))
        return v.transpose(1, 0, 2).reshape(tokens)

    code, segment = local(code), local(segment)
    split = split_params[:, 0, :]
    bias_qv = jnp.concatenate(
        [split[:, :width], jnp.zeros((LAYERS, width), f32), split[:, width : 2 * width]], axis=1
    )
    bias_1 = split[:, 2 * width : 2 * width + hidden]
    table = split[:, 2 * width + hidden :].reshape(LAYERS * heads_here, RELS)
    inner = table[:, : SIDE * SIDE].reshape(-1, SIDE, SIDE)
    inner = jnp.pad(inner, ((0, 0), (0, 32 - SIDE), (0, 32 - SIDE)))
    hot, hot_t, *bias = call(
        prepare_kernel,
        [
            ((tokens, CODES), bf16, STAY),
            ((CODES, tokens), bf16, STAY),
        ]
        + [((heads_here, tokens, tokens), f32, STAY)] * LAYERS,
        [
            inner,
            (table[:, SIDE * SIDE :], SMEM),
            code[:, None],
            segment[:, None],
            code[None, :],
            segment[None, :],
        ],
        "prepare",
        6,
        scratch=[
            pltpu.VMEM((LAYERS * heads_here, PITCH, SPREAD), f32),
            pltpu.VMEM((CODES, CODES), f32),
        ],
    )
    def weights_of(level, *others):
        shape = (group, HEAD, D)
        low = 3 * group * level
        if in_pieces:
            taken = call(
                deal_kernel,
                [(shape, bf16, STAY)] * 3,
                [(after(near_unit, *others) if others else near_unit, SMEM)]
                + [(b, FAR) for b in blocks],
                "deal",
                2,
                scratch=[pltpu.SemaphoreType.DMA((3,))],
                low=low,
                order=order,
            )
        else:
            whole = jnp.concatenate(blocks, axis=0)
            place = jnp.sum(
                jnp.where(near_unit.reshape(-1)[None, :] == unit_ids[:, None], jnp.arange(whole.shape[0])[None, :], 0),
                axis=1,
            )
            whole = jnp.take(whole, place, axis=0)
            taken = [whole[low + i * group : low + (i + 1) * group] for i in range(3)]
        return [v.reshape(-1, D) for v in taken]

    both = jnp.concatenate([tokens_in, out_grad], axis=0)
    x, a0, x_far, upper, e0 = call(
        start_kernel,
        [
            ((half, D), f32),
            ((half, D), bf16),
            ((half, D), f32, STAY),
            ((half, D), f32, STAY),
            ((half, D), bf16),
        ],
        [tokens_in, out_grad, swap(both, "y"), shared_params],
        "start",
        0,
    )
    a1 = swap(a0, "core")

    def chip_sum(keep, send):
        return (keep.astype(f32) + swap(send, "core").astype(f32)).astype(bf16)

    def joined(level, kind, ours, theirs, x):
        return call(
            join(level, kind),
            [
                ((half, D), f32),
                ((half, D), bf16),
                ((rows, D), f32, STAY),
                ((half, D), f32, STAY),
            ],
            [ours, theirs, x, shared_params],
            "join",
            0,
        )

    saved = []
    for level in range(LAYERS):
        if level == 0:
            weights = [weights_of(0)]
        w_head, w1, w2 = weights[level]
        qkv, mixed, logs, a0_far, a1_far, keep, send = call(
            attention_kernel,
            [
                ((tokens, 3 * width), bf16, STAY),
                ((tokens, width), bf16, STAY),
                ((tokens, 128), f32, STAY),
                ((half, D), bf16, STAY),
                ((half, D), bf16, STAY),
                ((half, D), bf16),
                ((half, D), bf16),
            ],
            [a0, a1, bias_qv[level : level + 1], bias[level], w_head],
            "attention",
            0,
        )
        ours = chip_sum(keep, send)
        theirs = swap(ours, "y")
        if level == 0:
            weights.append(weights_of(1, ours))
            x = after(x, *weights[1])
        else:
            e0 = after(e0, ours)
            e1 = swap(e0, "core")
        x_mid, c0, branch, x_mid_far = joined(level, 0, ours, theirs, x)
        c1 = swap(c0, "core")
        u, slope, c0_far, c1_far, keep, send = call(
            hidden_kernel,
            [
                ((tokens, hidden), bf16, STAY),
                ((tokens, hidden), f32, STAY),
                ((half, D), bf16, STAY),
                ((half, D), bf16, STAY),
                ((half, D), bf16),
                ((half, D), bf16),
            ],
            [c0, c1, bias_1[level : level + 1], w1, w2],
            "hidden",
            0,
        )
        state = (x_far, a0_far, a1_far, qkv, mixed, logs, w_head, branch)
        state += (x_mid_far, c0_far, c1_far, u, slope, w1, w2)
        if level + 1 < LAYERS:
            ours = chip_sum(keep, send)
            theirs = swap(ours, "y")
            x, a0, branch_two, x_far = joined(level, 1, ours, theirs, x_mid)
            a1 = swap(a0, "core")
        else:
            final_parts = (keep, send)
            branch_two = None
        saved.append(state + (branch_two,))

    grads = None
    sizes = [stop - start for _, start, stop in back_order] * 2 if in_pieces else [owners_all * capacity]
    buffers = [((size, HEAD, D), bf16, FAR) for size in sizes]
    norm_sums, table_args = [], []
    for level in reversed(range(LAYERS)):
        x_far, a0_far, a1_far, qkv, mixed, logs, w_head, branch = saved[level][:8]
        x_mid_far, c0_far, c1_far, u, slope, w1, w2 = saved[level][8:15]
        dz, e0_far, e1_far, d_b1, keep, send = call(
            hidden_back_kernel,
            [
                ((tokens, hidden), bf16, STAY),
                ((half, D), bf16, STAY),
                ((half, D), bf16, STAY),
                ((1, hidden), f32),
                ((half, D), bf16),
                ((half, D), bf16),
            ],
            [e0, e1, w1, w2, slope],
            "hidden_back",
            0,
        )
        ours = chip_sum(keep, send)
        theirs = swap(ours, "y")
        first = 3 * group * level
        args = [(near_slot, SMEM), after(dz, ours), c0_far, c1_far, u, e0_far, e1_far]
        grads = call(
            weights_kernel,
            buffers,
            args + [(v, FAR) for v in grads or ()],
            "hidden_weights",
            2.5,
            scratch=[pltpu.VMEM((2 * group, HEAD, D), bf16), pltpu.SemaphoreType.DMA],
            alias=len(args) if grads else None,
            first=first + group,
            count=len(buffers),
            capacity=capacity,
        )
        d_mid, e0, sums_two = call(
            join_back((level, 4), (level, 2)),
            [((half, D), f32), ((half, D), bf16), ((4, D), f32)],
            [
                ours,
                theirs,
                after(x_mid_far, grads[0]),
                upper,
                branch,
                shared_params,
            ],
            "join_back",
            0,
        )
        e1 = swap(e0, "core")
        d_qkv, d_scores, e0_far, e1_far, keep, send = call(
            attention_back_kernel,
            [
                ((tokens, 3 * width), bf16, STAY),
                ((heads_here, tokens, tokens), bf16, STAY),
                ((half, D), bf16, STAY),
                ((half, D), bf16, STAY),
                ((half, D), bf16),
                ((half, D), bf16),
            ],
            [e0, e1, w_head, qkv, logs, bias[level]],
            "attention_back",
            0,
        )
        if level > 0:
            ours = chip_sum(keep, send)
            theirs = swap(ours, "y")
            d_qkv = after(d_qkv, ours)
        args = [(near_slot, SMEM), d_qkv, a0_far, a1_far, mixed, e0_far, e1_far]
        grads = call(
            weights_kernel,
            buffers,
            args + [(v, FAR) for v in grads],
            "attention_weights",
            2,
            scratch=[pltpu.VMEM((group, HEAD, D), bf16), pltpu.SemaphoreType.DMA],
            alias=len(args),
            first=first,
            count=len(buffers),
            capacity=capacity,
        )
        table_args.append([d_qkv, d_b1, d_scores, hot, hot_t])
        if level > 0:
            x_far = after(x_far, grads[0])
            upper, e0, sums_one = call(
                join_back((level, 0), (level - 1, 6)),
                [((half, D), f32), ((half, D), bf16), ((4, D), f32)],
                [ours, theirs, x_far, d_mid, saved[level - 1][-1], shared_params],
                "join_back",
                0,
                )
            e1 = swap(e0, "core")
        else:
            if not in_pieces:
                grads = [
                    grads[0][p * capacity + start : p * capacity + stop]
                    for x in range(2)
                    for s, start, stop in back_order
                    for p in [x * nz + s]
                ]
            scatter = ScatterSums(grads, back_order)
            scatter.step()
            last = scatter.part
            ours = chip_sum(keep, after(send, last))
            input_grad, sums_one = call(
                last_back_kernel,
                [((rows, D), f32), ((2, D), f32)],
                [ours, swap(ours[rows:], "y"), x_far, d_mid, shared_params],
                "last_back",
                0,
                )
        norm_sums.append((sums_one, sums_two))

    keep, send = after(final_parts, last)
    ours = chip_sum(keep, send)
    final_branch = (
        ours[:rows].astype(f32) + swap(ours[rows:], "y").astype(f32) + shared_params[LAYERS - 1, 7]
    )
    last_scale = shared_params[LAYERS - 1, 6]
    block_out = (x_mid[:rows] + last_scale * final_branch).astype(bf16)
    own_grad = out_grad.astype(f32)
    branch_sums = jnp.stack(
        [jnp.sum(own_grad * final_branch, axis=0), jnp.sum(last_scale * own_grad, axis=0)]
    )
    shared_grads, packed = [], []
    for sums, args in zip(norm_sums, table_args):
        sums_one, sums_two = sums
        shared_grads = [sums_one[0:2], sums_two[2:4], sums_two[0:2], branch_sums] + shared_grads
        branch_sums = sums_one[2:4]
        table = call(
            table_kernel, [((PACKED, 128), f32)], [after(args[0], last)] + args[1:], "table", 3
        )[0]
        packed.insert(0, table)

    shared_part = jnp.concatenate(shared_grads, axis=0)
    shared_part = sum_over(sum_over(shared_part, "core"), "y")
    small = jnp.concatenate([shared_part.reshape(-1, 128)] + packed, axis=0)
    scatter.step()
    scatter.step()
    small = small + scatter.along_x.send(small, "x", SWAP)
    while scatter.next < len(back_order) - 1:
        scatter.step()
    small = sum_over(small, "z")
    small = after(small, scatter.part)
    scatter.step()
    mine = scatter.result()
    lines = shared_part.size // 128
    shared_total = small[:lines].reshape(shared_params.shape)
    split_grads = []
    for level in range(LAYERS):
        part = small[lines + level * PACKED : lines + (level + 1) * PACKED]
        flat = part[: 3 * width // 128 + hidden // 128 + 1].reshape(-1)
        d_bias, d_b1 = flat[: 3 * width], flat[PACK_B1 * 128 : PACK_B1 * 128 + hidden]
        d_rel = jnp.concatenate(
            [
                part[PACK_TABLE : PACK_TABLE + SIDE, : 32 * heads_here]
                .reshape(SIDE, heads_here, 32)[:, :, :SIDE]
                .transpose(1, 0, 2)
                .reshape(heads_here, -1),
                part[PACK_ENDS : PACK_ENDS + heads_here, :3],
            ],
            axis=1,
        )
        split_grads.append(
            jnp.concatenate([d_bias[:width], d_bias[2 * width :], d_b1, d_rel.reshape(-1)])
        )
    split_total = jnp.stack(split_grads)[:, None, :]

    my_ids = (my_z * 2 + my_x) * capacity + jnp.arange(capacity, dtype=jnp.int32)
    used = jnp.any(my_ids[:, None] == slots[None, :], axis=1)[:, None, None]
    zeros = jnp.zeros_like(weight_store)
    mine = jnp.where(used, mine, zeros)
    matrix_first, matrix_second, matrix_weight = adam_step(
        weight_store, first_store, second_store, mine, rate_matrix, weight_decay
    )
    shared_moment, shared_square, shared_value = adam_step(
        shared_params, shared_first, shared_second, shared_total, rate_small, 0.0
    )
    split_moment, split_square, split_value = adam_step(
        split_params, split_first, split_second, split_total, rate_small, 0.0
    )
    return (
        block_out,
        input_grad,
        mine,
        jnp.where(used, matrix_first, zeros),
        jnp.where(used, matrix_second, zeros),
        jnp.where(used, matrix_weight, zeros),
        shared_total,
        shared_moment,
        shared_square,
        shared_value,
        split_total,
        split_moment,
        split_square,
        split_value,
    )


def solution(mesh):
    dp, tensor = mesh.shape["dp"], mesh.shape["tensor"]
    fine = Mesh(mesh.devices.reshape(dp // 2, 2, tensor // 2, 2), ("z", "x", "y", "core"))
    data, split = ("z", "x"), ("y", "core")
    tokens = P(data + split, None)
    store = P(data, split, None)
    shards = P(None, split, None)
    return jax.shard_map(
        per_device,
        mesh=fine,
        in_specs=(tokens, tokens, P(data, None), P(), store, store, store, P(), P(), P())
        + (shards,) * 3,
        out_specs=(tokens, tokens) + (store,) * 4 + (P(),) * 4 + (shards,) * 4,
        check_vma=False,
    )
```

profile of v0, /device:TPU:0, one launch (start us, length us, event | category | flops | bytes accessed | tf_op | source)
XLA Modules:
  0.0 375.1 jit_solution(6494983442529577701)
XLA Ops:
  0.7 1.7 convert_element_type.148.refs_0_
  2.4 5.1 %collective-permute-start.2 = (bf16[10,64,768]{2,1,0:T(8,128)(2,1)S(1)}, bf16[10,64,768]{2,1,0:T(8,128)(2,1)S(1)}, u32[]{:S(2)}, u32[]{:S(2)}) collective-permute-start(bf16[10,64,768]{2,1,0:T(8,128)(2,1)S(1)} %convert_element_type.148.refs_0_), channel_id=1, source_target_pairs={{8,0},{16,8},{24,16},{0,24},{9,1},{17,9},{25,17},{1,25},{10,2},{18... | collective-permute-start | bytes 2949128 | tf_op jit(solution)/shard_map/ppermute | solution.py:107
  11.6 16.9 %collective-permute-done.2.refs_1_ = bf16[10,64,768]{2,1,0:T(8,128)(2,1)S(1)} collective-permute-done((bf16[10,64,768]{2,1,0:T(8,128)(2,1)S(1)}, bf16[10,64,768]{2,1,0:T(8,128)(2,1)S(1)}, u32[]{:S(2)}, u32[]{:S(2)}) %collective-permute-start.2) | collective-permute-done | bytes 983072 | tf_op jit(solution)/shard_map/ppermute | solution.py:107
  28.5 2.2 collective-permute-done.7.refs_6_
  33.6 22.7 %collective-permute-done.3.refs_2_ = bf16[5,64,768]{2,1,0:T(8,128)(2,1)} collective-permute-done((bf16[5,64,768]{2,1,0:T(8,128)(2,1)}, bf16[5,64,768]{2,1,0:T(8,128)(2,1)}, u32[]{:S(2)}, u32[]{:S(2)}) %collective-permute-start.3) | collective-permute-done | bytes 491552 | tf_op jit(solution)/shard_map/ppermute | solution.py:107
  59.5 20.5 %collective-permute-done.4.refs_3_ = bf16[5,64,768]{2,1,0:T(8,128)(2,1)} collective-permute-done((bf16[5,64,768]{2,1,0:T(8,128)(2,1)}, bf16[5,64,768]{2,1,0:T(8,128)(2,1)}, u32[]{:S(2)}, u32[]{:S(2)}) %collective-permute-start.4) | collective-permute-done | bytes 491552 | tf_op jit(solution)/shard_map/ppermute | solution.py:107
  82.4 5.8 %prepare.1 = (bf16[512,256]{1,0:T(8,128)(2,1)S(1)}, bf16[256,512]{1,0:T(8,128)(2,1)S(1)}, f32[3,512,512]{2,1,0:T(8,128)S(1)}, f32[3,512,512]{2,1,0:T(8,128)S(1)}) custom-call(f32[6,32,32]{2,1,0:T(8,128)S(1)} %pad.4.table, f32[6,3]{1,0:T(8,128)S(1)} %slice.186.ends, s32[512,1]{1,0:T(8,128)S(1)} %copy-done.10, s32[512,1]{1,0:T(8,128)S(1)} %copy-done.11, ...), custom_call_target="tpu_custom_call" | custom-call | flops 6000000000 | bytes 1 | tf_op jit(solution)/shard_map/prepare/pallas_call | solution.py:81
  88.2 1.6 copy-done
  91.3 3.8 %collective-permute-done.5.refs_4_ = bf16[5,64,768]{2,1,0:T(8,128)(2,1)S(1)} collective-permute-done((bf16[5,64,768]{2,1,0:T(8,128)(2,1)}, bf16[5,64,768]{2,1,0:T(8,128)(2,1)S(1)}, u32[]{:S(2)}, u32[]{:S(2)}) %collective-permute-start.5) | collective-permute-done | bytes 491552 | tf_op jit(solution)/shard_map/ppermute | solution.py:107
  96.3 13.2 %collective-permute-done.6.refs_5_ = bf16[5,64,768]{2,1,0:T(8,128)(2,1)} collective-permute-done((bf16[5,64,768]{2,1,0:T(8,128)(2,1)S(1)}, bf16[5,64,768]{2,1,0:T(8,128)(2,1)}, u32[]{:S(2)}, u32[]{:S(2)}) %collective-permute-start.6) | collective-permute-done | bytes 491552 | tf_op jit(solution)/shard_map/ppermute | solution.py:107
  113.3 7.9 %collective-permute-done.12.refs_11_ = bf16[5,64,768]{2,1,0:T(8,128)(2,1)} collective-permute-done((bf16[5,64,768]{2,1,0:T(8,128)(2,1)}, bf16[5,64,768]{2,1,0:T(8,128)(2,1)}, u32[]{:S(2)}, u32[]{:S(2)}) %collective-permute-start.12) | collective-permute-done | bytes 491552 | tf_op jit(solution)/shard_map/ppermute | solution.py:107
  121.3 2.8 deal.2
  124.1 2.7 attention.2
  126.9 1.7 collective-permute-done.13
  128.7 1.6 collective-permute-start.14
  130.3 2.8 deal.3
  133.1 6.8 %collective-permute-done.14.theirs = bf16[256,768]{1,0:T(8,128)(2,1)S(1)} collective-permute-done((bf16[256,768]{1,0:T(8,128)(2,1)S(1)}, bf16[256,768]{1,0:T(8,128)(2,1)S(1)}, u32[]{:S(2)}, u32[]{:S(2)}) %collective-permute-start.14) | collective-permute-done | bytes 393248 | tf_op jit(solution)/shard_map/ppermute | solution.py:97
  140.4 1.7 collective-permute-done.15.c1
  142.1 2.2 hidden.2
  144.5 1.6 collective-permute-done.16
  146.2 1.6 collective-permute-start.17
  147.8 9.6 %collective-permute-done.17.theirs = bf16[256,768]{1,0:T(8,128)(2,1)S(1)} collective-permute-done((bf16[256,768]{1,0:T(8,128)(2,1)S(1)}, bf16[256,768]{1,0:T(8,128)(2,1)S(1)}, u32[]{:S(2)}, u32[]{:S(2)}) %collective-permute-start.17) | collective-permute-done | bytes 393248 | tf_op jit(solution)/shard_map/ppermute | solution.py:97
  157.9 1.7 collective-permute-done.18.a1
  159.6 2.8 attention.3
  164.3 1.6 collective-permute-start.20
  165.9 9.6 %collective-permute-done.20.theirs = bf16[256,768]{1,0:T(8,128)(2,1)S(1)} collective-permute-done((bf16[256,768]{1,0:T(8,128)(2,1)S(1)}, bf16[256,768]{1,0:T(8,128)(2,1)S(1)}, u32[]{:S(2)}, u32[]{:S(2)}) %collective-permute-start.20) | collective-permute-done | bytes 393248 | tf_op jit(solution)/shard_map/ppermute | solution.py:97
  177.7 2.4 hidden.3
  180.2 2.1 hidden_back.2
  185.7 3.2 hidden_weights.2
  188.9 6.5 %collective-permute-done.24.theirs = bf16[256,768]{1,0:T(8,128)(2,1)S(1)} collective-permute-done((bf16[256,768]{1,0:T(8,128)(2,1)S(1)}, bf16[256,768]{1,0:T(8,128)(2,1)S(1)}, u32[]{:S(2)}, u32[]{:S(2)}) %collective-permute-start.24) | collective-permute-done | bytes 393248 | tf_op jit(solution)/shard_map/ppermute | solution.py:97
  196.2 1.7 collective-permute-done.25.e1
  197.9 4.1 %attention_back.2 = (bf16[512,576]{1,0:T(8,128)(2,1)S(1)}, bf16[3,512,512]{2,1,0:T(8,128)(2,1)S(1)}, bf16[256,768]{1,0:T(8,128)(2,1)S(1)}, bf16[256,768]{1,0:T(8...) custom-call(bf16[256,768]{1,0:T(8,128)(2,1)S(1)} %get-tuple-element.231.e0, ...), custom_call_target="tpu_custom_call" | custom-call | bytes 1 | tf_op jit(solution)/shard_map/attention_back/pallas_call | solution.py:81
  202.3 1.6 collective-permute-done.26
  205.5 2.4 attention_weights.2
  207.9 7.3 %collective-permute-done.27.theirs = bf16[256,768]{1,0:T(8,128)(2,1)S(1)} collective-permute-done((bf16[256,768]{1,0:T(8,128)(2,1)S(1)}, bf16[256,768]{1,0:T(8,128)(2,1)S(1)}, u32[]{:S(2)}, u32[]{:S(2)}) %collective-permute-start.27) | collective-permute-done | bytes 393248 | tf_op jit(solution)/shard_map/ppermute | solution.py:97
  216.0 1.7 collective-permute-done.28.e1
  217.7 2.5 hidden_back.3
  220.4 1.6 collective-permute-done.29
  223.7 3.1 hidden_weights.3
  226.8 6.5 %collective-permute-done.30.theirs = bf16[256,768]{1,0:T(8,128)(2,1)S(1)} collective-permute-done((bf16[256,768]{1,0:T(8,128)(2,1)S(1)}, bf16[256,768]{1,0:T(8,128)(2,1)S(1)}, u32[]{:S(2)}, u32[]{:S(2)}) %collective-permute-start.30) | collective-permute-done | bytes 393248 | tf_op jit(solution)/shard_map/ppermute | solution.py:97
  234.1 1.7 collective-permute-done.31.e1
  235.9 4.1 %attention_back.3 = (bf16[512,576]{1,0:T(8,128)(2,1)S(1)}, bf16[3,512,512]{2,1,0:T(8,128)(2,1)S(1)}, bf16[256,768]{1,0:T(8,128)(2,1)S(1)}, bf16[256,768]{1,0:T(8...) custom-call(bf16[256,768]{1,0:T(8,128)(2,1)S(1)} %get-tuple-element.282.e0, ...), custom_call_target="tpu_custom_call" | custom-call | bytes 1 | tf_op jit(solution)/shard_map/attention_back/pallas_call | solution.py:81
  240.0 2.4 attention_weights.3
  243.0 12.9 %collective-permute-done.32 = bf16[5,64,768]{2,1,0:T(8,128)(2,1)S(1)} collective-permute-done((bf16[5,64,768]{2,1,0:T(8,128)(2,1)}, bf16[5,64,768]{2,1,0:T(8,128)(2,1)S(1)}, u32[]{:S(2)}, u32[]{:S(2)}) %collective-permute-start.32) | collective-permute-done | bytes 491552 | tf_op jit(solution)/shard_map/ppermute | solution.py:107
  256.4 1.9 add_convert_fusion.3
  260.2 1.6 collective-permute-start.34
  261.8 6.8 %collective-permute-done.38 = bf16[5,64,768]{2,1,0:T(8,128)(2,1)S(1)} collective-permute-done((bf16[5,64,768]{2,1,0:T(8,128)(2,1)}, bf16[5,64,768]{2,1,0:T(8,128)(2,1)S(1)}, u32[]{:S(2)}, u32[]{:S(2)}) %collective-permute-start.38) | collective-permute-done | bytes 491552 | tf_op jit(solution)/shard_map/ppermute | solution.py:107
  269.2 1.6 collective-permute-start.36
  271.7 3.3 collective-permute-done.36.theirs
  277.7 2.8 table.2
  280.5 1.6 collective-permute-start.43
  282.1 3.0 table.3
  285.2 5.9 %collective-permute-done.40 = bf16[10,64,768]{2,1,0:T(8,128)(2,1)} collective-permute-done((bf16[10,64,768]{2,1,0:T(8,128)(2,1)}, bf16[10,64,768]{2,1,0:T(8,128)(2,1)}, u32[]{:S(2)}, u32[]{:S(2)}) %collective-permute-start.40) | collective-permute-done | bytes 983072 | tf_op jit(solution)/shard_map/ppermute | solution.py:107
  291.6 4.9 %collective-permute-done.44 = f32[192,128]{1,0:T(8,128)S(1)} collective-permute-done((f32[192,128]{1,0:T(8,128)S(1)}, f32[192,128]{1,0:T(8,128)S(1)}, u32[]{:S(2)}, u32[]{:S(2)}) %collective-permute-start.44) | collective-permute-done | bytes 98336 | tf_op jit(solution)/shard_map/ppermute | solution.py:107
  298.4 1.9 collective-permute-start.48
  300.5 7.4 %collective-permute-done.48 = f32[192,128]{1,0:T(8,128)S(1)} collective-permute-done((f32[192,128]{1,0:T(8,128)S(1)}, f32[192,128]{1,0:T(8,128)S(1)}, u32[]{:S(2)}, u32[]{:S(2)}) %collective-permute-start.48) | collective-permute-done | bytes 98336 | tf_op jit(solution)/shard_map/ppermute | solution.py:182
  307.8 2.4 collective-permute-start.49
  310.2 2.4 add_convert_fusion.1
  312.6 7.4 %collective-permute-done.39 = bf16[5,64,768]{2,1,0:T(8,128)(2,1)S(1)} collective-permute-done((bf16[5,64,768]{2,1,0:T(8,128)(2,1)S(1)}, bf16[5,64,768]{2,1,0:T(8,128)(2,1)S(1)}, u32[]{:S(2)}, u32[]{:S(2)}) %collective-permute-start.39) | collective-permute-done | bytes 491552 | tf_op jit(solution)/shard_map/ppermute | solution.py:107
  323.6 20.3 %collective-permute-done.41 = bf16[10,64,768]{2,1,0:T(8,128)(2,1)S(1)} collective-permute-done((bf16[10,64,768]{2,1,0:T(8,128)(2,1)}, bf16[10,64,768]{2,1,0:T(8,128)(2,1)S(1)}, u32[]{:S(2)}, u32[]{:S(2)}) %collective-permute-start.41) | collective-permute-done | bytes 983072 | tf_op jit(solution)/shard_map/ppermute | solution.py:107
  349.0 16.4 %collective-permute-done.46 = bf16[10,64,768]{2,1,0:T(8,128)(2,1)S(1)} collective-permute-done((bf16[10,64,768]{2,1,0:T(8,128)(2,1)}, bf16[10,64,768]{2,1,0:T(8,128)(2,1)S(1)}, u32[]{:S(2)}, u32[]{:S(2)}) %collective-permute-start.46) | collective-permute-done | bytes 983072 | tf_op jit(solution)/shard_map/ppermute | solution.py:107
  365.3 1.9 collective-permute-done.47
  367.2 5.1 %subtract_select_fusion = (f32[10,64,768]{2,1,0:T(8,128)}, f32[10,64,768]{2,1,0:T(8,128)S(1)}) fusion(f32[10,64,768]{2,1,0:T(8,128)} %param.20, pred[10]{0:T(512)(128)(4,1)S(1)} %compare_reduce_fusion.1, f32[10,64,768]{2,1,0:T(8,128)} %param.21, f32[10,64,768]{2,1,0:T(8,128)} %param.22, bf16[10,64,768]{2,1,0:T(8,128)(2,1)S(1)} %collective-permute-done.47, ...), kind=kLoop, calls=%fused_computation.3 | loop fusion | flops 12779520 | bytes 14745610 | tf_op jit(solution)/shard_map/jit(_where)/select_n | solution.py:952
  372.4 2.5 broadcast_select_fusion
  (253 shorter events, 52.1 us)
Async XLA Ops:
  2.4 78.1 %copy-start.20 = (bf16[10,64,768]{2,1,0:T(8,128)(2,1)}, bf16[10,64,768]{2,1,0:T(8,128)(2,1)S(1)}, u32[]{:S(2)}) copy-start(bf16[10,64,768]{2,1,0:T(8,128)(2,1)S(1)} %convert_element_type.148.refs_0_) | copy-start | bytes 2949124
  2.4 31.0 %copy-start.44 = (s32[72]{0:T(128)S(1)}, s32[72]{0:T(128)}, u32[]{:S(2)}) copy-start(s32[72]{0:T(128)} %param.19) | copy-start | bytes 868
  2.4 56.5 %copy-start.37 = (f32[2,1,3348]{2,1,0:T(1,128)S(1)}, f32[2,1,3348]{2,1,0:T(1,128)}, u32[]{:S(2)}) copy-start(f32[2,1,3348]{2,1,0:T(1,128)} %param.26) | copy-start | bytes 80356
  2.4 26.1 %collective-permute-start.2 = (bf16[10,64,768]{2,1,0:T(8,128)(2,1)S(1)}, bf16[10,64,768]{2,1,0:T(8,128)(2,1)S(1)}, u32[]{:S(2)}, u32[]{:S(2)}) collective-permute-start(bf16[10,64,768]{2,1,0:T(8,128)(2,1)S(1)} %convert_element_type.148.refs_0_), channel_id=1, source_target_pairs={{8,0},{16,8},{24,16},{0,24},{9,1},{17,9},{25,17},{1,25},{10,2},{18... | collective-permute-start | bytes 2949128 | tf_op jit(solution)/shard_map/ppermute | solution.py:107
  7.5 23.2 %collective-permute-start.7 = (bf16[10,64,768]{2,1,0:T(8,128)(2,1)S(1)}, bf16[10,64,768]{2,1,0:T(8,128)(2,1)S(1)}, u32[]{:S(2)}, u32[]{:S(2)}) collective-permute-start(bf16[10,64,768]{2,1,0:T(8,128)(2,1)S(1)} %convert_element_type.148.refs_0_), channel_id=1, source_target_pairs={{0,4},{4,0},{1,5},{5,1},{2,6},{6,2},{3,7},{7,3},{8,12},{12,8},{9,1... | collective-permute-start | bytes 2949128 | tf_op jit(solution)/shard_map/ppermute | solution.py:107
  9.8 101.0 %collective-permute-start = (bf16[256,768]{1,0:T(8,128)(2,1)}, bf16[256,768]{1,0:T(8,128)(2,1)}, u32[]{:S(2)}, u32[]{:S(2)}) collective-permute-start(bf16[256,768]{1,0:T(8,128)(2,1)} %pad_maximum_fusion), channel_id=1, source_target_pairs={{0,2},{2,0},{1,3},{3,1},{4,6},{6,4},{5,7},{7,5},{8,10},{10,8},{9,1... | collective-permute-start | bytes 1179656 | tf_op jit(solution)/shard_map/ppermute | solution.py:97
  28.5 52.0 %copy-start.28 = (bf16[10,64,768]{2,1,0:T(8,128)(2,1)}, bf16[10,64,768]{2,1,0:T(8,128)(2,1)S(1)}, u32[]{:S(2)}) copy-start(bf16[10,64,768]{2,1,0:T(8,128)(2,1)S(1)} %collective-permute-done.2.refs_1_) | copy-start | bytes 2949124
  30.7 49.8 %copy-start.29 = (bf16[10,64,768]{2,1,0:T(8,128)(2,1)}, bf16[10,64,768]{2,1,0:T(8,128)(2,1)S(1)}, u32[]{:S(2)}) copy-start(bf16[10,64,768]{2,1,0:T(8,128)(2,1)S(1)} %collective-permute-done.7.refs_6_) | copy-start | bytes 2949124
  30.7 25.6 %collective-permute-start.8 = (bf16[10,64,768]{2,1,0:T(8,128)(2,1)S(1)}, bf16[10,64,768]{2,1,0:T(8,128)(2,1)}, u32[]{:S(2)}, u32[]{:S(2)}) collective-permute-start(bf16[10,64,768]{2,1,0:T(8,128)(2,1)S(1)} %collective-permute-done.2.refs_1_), channel_id=1, source_target_pairs={{0,4},{4,0},{1,5},{5,1},{2,6},{6,2},{3,7},{7,3},{8,12},{12,8},{9,1... | collective-permute-start | bytes 2949128 | tf_op jit(solution)/shard_map/ppermute | solution.py:107
  33.3 23.1 %collective-permute-start.3 = (bf16[5,64,768]{2,1,0:T(8,128)(2,1)}, bf16[5,64,768]{2,1,0:T(8,128)(2,1)}, u32[]{:S(2)}, u32[]{:S(2)}) collective-permute-start(bf16[5,64,768]{2,1,0:T(8,128)(2,1)} %get-tuple-element.183), channel_id=1, source_target_pairs={{16,0},{24,8},{0,16},{8,24},{17,1},{25,9},{1,17},{9,25},{18,2},{26... | collective-permute-start | bytes 1474568 | tf_op jit(solution)/shard_map/ppermute | solution.py:107
  56.4 23.6 %collective-permute-start.4 = (bf16[5,64,768]{2,1,0:T(8,128)(2,1)}, bf16[5,64,768]{2,1,0:T(8,128)(2,1)}, u32[]{:S(2)}, u32[]{:S(2)}) collective-permute-start(bf16[5,64,768]{2,1,0:T(8,128)(2,1)} %get-tuple-element.184), channel_id=1, source_target_pairs={{16,0},{24,8},{0,16},{8,24},{17,1},{25,9},{1,17},{9,25},{18,2},{26... | collective-permute-start | bytes 1474568 | tf_op jit(solution)/shard_map/ppermute | solution.py:107
  56.4 23.6 %collective-permute-start.9 = (bf16[5,64,768]{2,1,0:T(8,128)(2,1)}, bf16[5,64,768]{2,1,0:T(8,128)(2,1)}, u32[]{:S(2)}, u32[]{:S(2)}) collective-permute-start(bf16[5,64,768]{2,1,0:T(8,128)(2,1)} %collective-permute-done.3.refs_2_), channel_id=1, source_target_pairs={{0,4},{4,0},{1,5},{5,1},{2,6},{6,2},{3,7},{7,3},{8,12},{12,8},{9,1... | collective-permute-start | bytes 1474568 | tf_op jit(solution)/shard_map/ppermute | solution.py:107
  80.0 15.2 %collective-permute-start.5 = (bf16[5,64,768]{2,1,0:T(8,128)(2,1)}, bf16[5,64,768]{2,1,0:T(8,128)(2,1)S(1)}, u32[]{:S(2)}, u32[]{:S(2)}) collective-permute-start(bf16[5,64,768]{2,1,0:T(8,128)(2,1)} %get-tuple-element.183), channel_id=1, source_target_pairs={{24,0},{0,8},{8,16},{16,24},{25,1},{1,9},{9,17},{17,25},{26,2},{2,... | collective-permute-start | bytes 1474568 | tf_op jit(solution)/shard_map/ppermute | solution.py:107
  80.0 15.3 %collective-permute-start.10 = (bf16[5,64,768]{2,1,0:T(8,128)(2,1)}, bf16[5,64,768]{2,1,0:T(8,128)(2,1)S(1)}, u32[]{:S(2)}, u32[]{:S(2)}) collective-permute-start(bf16[5,64,768]{2,1,0:T(8,128)(2,1)} %collective-permute-done.4.refs_3_), channel_id=1, source_target_pairs={{0,4},{4,0},{1,5},{5,1},{2,6},{6,2},{3,7},{7,3},{8,12},{12,8},{9,1... | collective-permute-start | bytes 1474568 | tf_op jit(solution)/shard_map/ppermute | solution.py:107
  82.4 28.4 %copy-start.2 = (f32[2,8,768]{2,1,0:T(8,128)S(1)}, f32[2,8,768]{2,1,0:T(8,128)}, u32[]{:S(2)}) copy-start(f32[2,8,768]{2,1,0:T(8,128)} %shared.15) | copy-start | bytes 147460
  95.1 14.4 %collective-permute-start.6 = (bf16[5,64,768]{2,1,0:T(8,128)(2,1)S(1)}, bf16[5,64,768]{2,1,0:T(8,128)(2,1)}, u32[]{:S(2)}, u32[]{:S(2)}) collective-permute-start(bf16[5,64,768]{2,1,0:T(8,128)(2,1)S(1)} %copy-done.35), channel_id=1, source_target_pairs={{24,0},{0,8},{8,16},{16,24},{25,1},{1,9},{9,17},{17,25},{26,2},{2,... | collective-permute-start | bytes 1474568 | tf_op jit(solution)/shard_map/ppermute | solution.py:107
  95.3 14.2 %collective-permute-start.11 = (bf16[5,64,768]{2,1,0:T(8,128)(2,1)S(1)}, bf16[5,64,768]{2,1,0:T(8,128)(2,1)S(1)}, u32[]{:S(2)}, u32[]{:S(2)}) collective-permute-start(bf16[5,64,768]{2,1,0:T(8,128)(2,1)S(1)} %collective-permute-done.5.refs_4_), channel_id=1, source_target_pairs={{0,4},{4,0},{1,5},{5,1},{2,6},{6,2},{3,7},{7,3},{8,12},{12,8},{9,1... | collective-permute-start | bytes 1474568 | tf_op jit(solution)/shard_map/ppermute | solution.py:107
  109.5 11.8 %collective-permute-start.12 = (bf16[5,64,768]{2,1,0:T(8,128)(2,1)}, bf16[5,64,768]{2,1,0:T(8,128)(2,1)}, u32[]{:S(2)}, u32[]{:S(2)}) collective-permute-start(bf16[5,64,768]{2,1,0:T(8,128)(2,1)} %collective-permute-done.6.refs_5_), channel_id=1, source_target_pairs={{0,4},{4,0},{1,5},{5,1},{2,6},{6,2},{3,7},{7,3},{8,12},{12,8},{9,1... | collective-permute-start | bytes 1474568 | tf_op jit(solution)/shard_map/ppermute | solution.py:107
  113.3 10.8 %collective-permute-start.1 = (bf16[256,768]{1,0:T(8,128)(2,1)S(1)}, bf16[256,768]{1,0:T(8,128)(2,1)S(1)}, u32[]{:S(2)}, u32[]{:S(2)}) collective-permute-start(bf16[256,768]{1,0:T(8,128)(2,1)S(1)} %get-tuple-element.179.a0), channel_id=1, source_target_pairs={{0,1},{1,0},{2,3},{3,2},{4,5},{5,4},{6,7},{7,6},{8,9},{9,8},{10,11... | collective-permute-start | bytes 1179656 | tf_op jit(solution)/shard_map/ppermute | solution.py:97
  126.8 1.8 collective-permute-start.13
  128.7 11.2 %collective-permute-start.14 = (bf16[256,768]{1,0:T(8,128)(2,1)S(1)}, bf16[256,768]{1,0:T(8,128)(2,1)S(1)}, u32[]{:S(2)}, u32[]{:S(2)}) collective-permute-start(bf16[256,768]{1,0:T(8,128)(2,1)S(1)} %add_convert_fusion.11.ours), channel_id=1, source_target_pairs={{0,2},{2,0},{1,3},{3,1},{4,6},{6,4},{5,7},{7,5},{8,10},{10,8},{9,1... | collective-permute-start | bytes 1179656 | tf_op jit(solution)/shard_map/ppermute | solution.py:97
  140.3 1.8 collective-permute-start.15
  144.3 1.8 collective-permute-start.16
  146.2 11.2 %collective-permute-start.17 = (bf16[256,768]{1,0:T(8,128)(2,1)S(1)}, bf16[256,768]{1,0:T(8,128)(2,1)S(1)}, u32[]{:S(2)}, u32[]{:S(2)}) collective-permute-start(bf16[256,768]{1,0:T(8,128)(2,1)S(1)} %add_convert_fusion.10.ours), channel_id=1, source_target_pairs={{0,2},{2,0},{1,3},{3,1},{4,6},{6,4},{5,7},{7,5},{8,10},{10,8},{9,1... | collective-permute-start | bytes 1179656 | tf_op jit(solution)/shard_map/ppermute | solution.py:97
  157.8 1.8 collective-permute-start.18
  162.4 1.8 collective-permute-start.19
  164.3 11.2 %collective-permute-start.20 = (bf16[256,768]{1,0:T(8,128)(2,1)S(1)}, bf16[256,768]{1,0:T(8,128)(2,1)S(1)}, u32[]{:S(2)}, u32[]{:S(2)}) collective-permute-start(bf16[256,768]{1,0:T(8,128)(2,1)S(1)} %add_convert_fusion.9.ours), channel_id=1, source_target_pairs={{0,2},{2,0},{1,3},{3,1},{4,6},{6,4},{5,7},{7,5},{8,10},{10,8},{9,1... | collective-permute-start | bytes 1179656 | tf_op jit(solution)/shard_map/ppermute | solution.py:97
  175.9 1.8 collective-permute-start.21
  176.0 4.2 %collective-permute-start.22 = (bf16[256,768]{1,0:T(8,128)(2,1)S(1)}, bf16[256,768]{1,0:T(8,128)(2,1)S(1)}, u32[]{:S(2)}, u32[]{:S(2)}) collective-permute-start(bf16[256,768]{1,0:T(8,128)(2,1)S(1)} %get-tuple-element.215.e0), channel_id=1, source_target_pairs={{0,1},{1,0},{2,3},{3,2},{4,5},{5,4},{6,7},{7,6},{8,9},{9,8},{10,11... | collective-permute-start | bytes 1179656 | tf_op jit(solution)/shard_map/ppermute | solution.py:97
  182.3 1.8 collective-permute-start.23
  184.1 11.2 %collective-permute-start.24 = (bf16[256,768]{1,0:T(8,128)(2,1)S(1)}, bf16[256,768]{1,0:T(8,128)(2,1)S(1)}, u32[]{:S(2)}, u32[]{:S(2)}) collective-permute-start(bf16[256,768]{1,0:T(8,128)(2,1)S(1)} %add_convert_fusion.8.ours), channel_id=1, source_target_pairs={{0,2},{2,0},{1,3},{3,1},{4,6},{6,4},{5,7},{7,5},{8,10},{10,8},{9,1... | collective-permute-start | bytes 1179656 | tf_op jit(solution)/shard_map/ppermute | solution.py:97
  196.1 1.8 collective-permute-start.25
  202.1 1.8 collective-permute-start.26
  203.9 11.2 %collective-permute-start.27 = (bf16[256,768]{1,0:T(8,128)(2,1)S(1)}, bf16[256,768]{1,0:T(8,128)(2,1)S(1)}, u32[]{:S(2)}, u32[]{:S(2)}) collective-permute-start(bf16[256,768]{1,0:T(8,128)(2,1)S(1)} %add_convert_fusion.7.ours), channel_id=1, source_target_pairs={{0,2},{2,0},{1,3},{3,1},{4,6},{6,4},{5,7},{7,5},{8,10},{10,8},{9,1... | collective-permute-start | bytes 1179656 | tf_op jit(solution)/shard_map/ppermute | solution.py:97
  215.9 1.8 collective-permute-start.28
  220.2 1.8 collective-permute-start.29
  222.1 11.2 %collective-permute-start.30 = (bf16[256,768]{1,0:T(8,128)(2,1)S(1)}, bf16[256,768]{1,0:T(8,128)(2,1)S(1)}, u32[]{:S(2)}, u32[]{:S(2)}) collective-permute-start(bf16[256,768]{1,0:T(8,128)(2,1)S(1)} %add_convert_fusion.6.ours), channel_id=1, source_target_pairs={{0,2},{2,0},{1,3},{3,1},{4,6},{6,4},{5,7},{7,5},{8,10},{10,8},{9,1... | collective-permute-start | bytes 1179656 | tf_op jit(solution)/shard_map/ppermute | solution.py:97
  234.1 1.8 collective-permute-start.31
  242.4 13.5 %collective-permute-start.32 = (bf16[5,64,768]{2,1,0:T(8,128)(2,1)}, bf16[5,64,768]{2,1,0:T(8,128)(2,1)S(1)}, u32[]{:S(2)}, u32[]{:S(2)}) collective-permute-start(bf16[5,64,768]{2,1,0:T(8,128)(2,1)} %get-tuple-element.301), channel_id=1, source_target_pairs={{0,4},{4,0},{1,5},{5,1},{2,6},{6,2},{3,7},{7,3},{8,12},{12,8},{9,1... | collective-permute-start | bytes 1474568 | tf_op jit(solution)/shard_map/ppermute | solution.py:107
  255.9 12.6 %collective-permute-start.38 = (bf16[5,64,768]{2,1,0:T(8,128)(2,1)}, bf16[5,64,768]{2,1,0:T(8,128)(2,1)S(1)}, u32[]{:S(2)}, u32[]{:S(2)}) collective-permute-start(bf16[5,64,768]{2,1,0:T(8,128)(2,1)} %get-tuple-element.313), channel_id=1, source_target_pairs={{0,4},{4,0},{1,5},{5,1},{2,6},{6,2},{3,7},{7,3},{8,12},{12,8},{9,1... | collective-permute-start | bytes 1474568 | tf_op jit(solution)/shard_map/ppermute | solution.py:107
  258.4 1.7 collective-permute-start.33
  258.4 10.7 %collective-permute-start.35 = (bf16[256,768]{1,0:T(8,128)(2,1)S(1)}, bf16[256,768]{1,0:T(8,128)(2,1)S(1)}, u32[]{:S(2)}, u32[]{:S(2)}) collective-permute-start(bf16[256,768]{1,0:T(8,128)(2,1)S(1)} %get-tuple-element.306), channel_id=1, source_target_pairs={{0,1},{1,0},{2,3},{3,2},{4,5},{5,4},{6,7},{7,6},{8,9},{9,8},{10,11... | collective-permute-start | bytes 1179656 | tf_op jit(solution)/shard_map/ppermute | solution.py:97
  258.9 39.4 %collective-permute-start.37 = (bf16[5,64,768]{2,1,0:T(8,128)(2,1)}, bf16[5,64,768]{2,1,0:T(8,128)(2,1)}, u32[]{:S(2)}, u32[]{:S(2)}) collective-permute-start(bf16[5,64,768]{2,1,0:T(8,128)(2,1)} %add_convert_fusion.3), channel_id=1, source_target_pairs={{0,16},{8,24},{16,0},{24,8},{1,17},{9,25},{17,1},{25,9},{2,18},{10... | collective-permute-start | bytes 1474568 | tf_op jit(solution)/shard_map/ppermute | solution.py:107
  260.2 10.6 %collective-permute-start.34 = (bf16[128,768]{1,0:T(8,128)(2,1)S(1)}, bf16[128,768]{1,0:T(8,128)(2,1)S(1)}, u32[]{:S(2)}, u32[]{:S(2)}) collective-permute-start(bf16[128,768]{1,0:T(8,128)(2,1)S(1)} %slice.193), channel_id=1, source_target_pairs={{0,2},{2,0},{1,3},{3,1},{4,6},{6,4},{5,7},{7,5},{8,10},{10,8},{9,1... | collective-permute-start | bytes 589832 | tf_op jit(solution)/shard_map/ppermute | solution.py:97
  268.6 22.5 %collective-permute-start.40 = (bf16[10,64,768]{2,1,0:T(8,128)(2,1)}, bf16[10,64,768]{2,1,0:T(8,128)(2,1)}, u32[]{:S(2)}, u32[]{:S(2)}) collective-permute-start(bf16[10,64,768]{2,1,0:T(8,128)(2,1)} %get-tuple-element.318), channel_id=1, source_target_pairs={{0,4},{4,0},{1,5},{5,1},{2,6},{6,2},{3,7},{7,3},{8,12},{12,8},{9,1... | collective-permute-start | bytes 2949128 | tf_op jit(solution)/shard_map/ppermute | solution.py:107
  269.2 5.7 %collective-permute-start.36 = (bf16[128,768]{1,0:T(8,128)(2,1)S(1)}, bf16[128,768]{1,0:T(8,128)(2,1)S(1)}, u32[]{:S(2)}, u32[]{:S(2)}) collective-permute-start(bf16[128,768]{1,0:T(8,128)(2,1)S(1)} %slice.194), channel_id=1, source_target_pairs={{0,2},{2,0},{1,3},{3,1},{4,6},{6,4},{5,7},{7,5},{8,10},{10,8},{9,1... | collective-permute-start | bytes 589832 | tf_op jit(solution)/shard_map/ppermute | solution.py:97
  276.2 4.3 %collective-permute-start.42 = (f32[16,768]{1,0:T(8,128)S(1)}, f32[16,768]{1,0:T(8,128)S(1)}, u32[]{:S(2)}, u32[]{:S(2)}) collective-permute-start(f32[16,768]{1,0:T(8,128)S(1)} %concatenate.58), channel_id=1, source_target_pairs={{0,1},{1,0},{2,3},{3,2},{4,5},{5,4},{6,7},{7,6},{8,9},{9,8},{10,11... | collective-permute-start | bytes 147464 | tf_op jit(solution)/shard_map/ppermute | solution.py:182
  280.5 4.6 %collective-permute-start.43 = (f32[16,768]{1,0:T(8,128)S(1)}, f32[16,768]{1,0:T(8,128)S(1)}, u32[]{:S(2)}, u32[]{:S(2)}) collective-permute-start(f32[16,768]{1,0:T(8,128)S(1)} %add.288), channel_id=1, source_target_pairs={{0,2},{2,0},{1,3},{3,1},{4,6},{6,4},{5,7},{7,5},{8,10},{10,8},{9,1... | collective-permute-start | bytes 147464 | tf_op jit(solution)/shard_map/ppermute | solution.py:182
  285.1 25.1 %copy-start.21 = (bf16[10,64,768]{2,1,0:T(8,128)(2,1)S(1)}, bf16[10,64,768]{2,1,0:T(8,128)(2,1)}, u32[]{:S(2)}) copy-start(bf16[10,64,768]{2,1,0:T(8,128)(2,1)} %get-tuple-element.316) | copy-start | bytes 2949124
  291.0 5.4 %collective-permute-start.44 = (f32[192,128]{1,0:T(8,128)S(1)}, f32[192,128]{1,0:T(8,128)S(1)}, u32[]{:S(2)}, u32[]{:S(2)}) collective-permute-start(f32[192,128]{1,0:T(8,128)S(1)} %pad_maximum_fusion.1), channel_id=1, source_target_pairs={{0,4},{4,0},{1,5},{5,1},{2,6},{6,2},{3,7},{7,3},{8,12},{12,8},{9,1... | collective-permute-start | bytes 294920 | tf_op jit(solution)/shard_map/ppermute | solution.py:107
  296.4 24.8 %collective-permute-start.45 = (bf16[10,64,768]{2,1,0:T(8,128)(2,1)}, bf16[10,64,768]{2,1,0:T(8,128)(2,1)S(1)}, u32[]{:S(2)}, u32[]{:S(2)}) collective-permute-start(bf16[10,64,768]{2,1,0:T(8,128)(2,1)} %get-tuple-element.336), channel_id=1, source_target_pairs={{0,4},{4,0},{1,5},{5,1},{2,6},{6,2},{3,7},{7,3},{8,12},{12,8},{9,1... | collective-permute-start | bytes 2949128 | tf_op jit(solution)/shard_map/ppermute | solution.py:107
  298.3 21.7 %collective-permute-start.39 = (bf16[5,64,768]{2,1,0:T(8,128)(2,1)S(1)}, bf16[5,64,768]{2,1,0:T(8,128)(2,1)S(1)}, u32[]{:S(2)}, u32[]{:S(2)}) collective-permute-start(bf16[5,64,768]{2,1,0:T(8,128)(2,1)S(1)} %add_convert_fusion.2), channel_id=1, source_target_pairs={{0,16},{8,24},{16,0},{24,8},{1,17},{9,25},{17,1},{25,9},{2,18},{10... | collective-permute-start | bytes 1474568 | tf_op jit(solution)/shard_map/ppermute | solution.py:107
  298.4 9.5 %collective-permute-start.48 = (f32[192,128]{1,0:T(8,128)S(1)}, f32[192,128]{1,0:T(8,128)S(1)}, u32[]{:S(2)}, u32[]{:S(2)}) collective-permute-start(f32[192,128]{1,0:T(8,128)S(1)} %fusion.18), channel_id=1, source_target_pairs={{0,8},{8,0},{16,24},{24,16},{1,9},{9,1},{17,25},{25,17},{2,10},{10... | collective-permute-start | bytes 294920 | tf_op jit(solution)/shard_map/ppermute | solution.py:182
  307.8 13.3 %collective-permute-start.49 = (f32[192,128]{1,0:T(8,128)S(1)}, f32[192,128]{1,0:T(8,128)S(1)}, u32[]{:S(2)}, u32[]{:S(2)}) collective-permute-start(f32[192,128]{1,0:T(8,128)S(1)} %add.300), channel_id=1, source_target_pairs={{0,16},{8,24},{16,0},{24,8},{1,17},{9,25},{17,1},{25,9},{2,18},{10... | collective-permute-start | bytes 294920 | tf_op jit(solution)/shard_map/ppermute | solution.py:182
  320.0 23.8 %collective-permute-start.41 = (bf16[10,64,768]{2,1,0:T(8,128)(2,1)}, bf16[10,64,768]{2,1,0:T(8,128)(2,1)S(1)}, u32[]{:S(2)}, u32[]{:S(2)}) collective-permute-start(bf16[10,64,768]{2,1,0:T(8,128)(2,1)} %add_convert_fusion.1), channel_id=1, source_target_pairs={{0,8},{8,16},{16,24},{24,0},{1,9},{9,17},{17,25},{25,1},{2,10},{10... | collective-permute-start | bytes 2949128 | tf_op jit(solution)/shard_map/ppermute | solution.py:107
  321.1 24.1 %copy-start.24 = (bf16[10,64,768]{2,1,0:T(8,128)(2,1)S(1)}, bf16[10,64,768]{2,1,0:T(8,128)(2,1)}, u32[]{:S(2)}) copy-start(bf16[10,64,768]{2,1,0:T(8,128)(2,1)} %get-tuple-element.341) | copy-start | bytes 2949124
  321.1 25.7 %copy-start.38 = (f32[2,8,768]{2,1,0:T(8,128)S(1)}, f32[2,8,768]{2,1,0:T(8,128)}, u32[]{:S(2)}) copy-start(f32[2,8,768]{2,1,0:T(8,128)} %param.25) | copy-start | bytes 147460
  321.2 25.7 %copy-start.39 = (f32[2,8,768]{2,1,0:T(8,128)S(1)}, f32[2,8,768]{2,1,0:T(8,128)}, u32[]{:S(2)}) copy-start(f32[2,8,768]{2,1,0:T(8,128)} %param.24) | copy-start | bytes 147460
  321.2 27.0 %copy-start.40 = (f32[2,1,3348]{2,1,0:T(1,128)S(1)}, f32[2,1,3348]{2,1,0:T(1,128)}, u32[]{:S(2)}) copy-start(f32[2,1,3348]{2,1,0:T(1,128)} %param.28) | copy-start | bytes 80356
  321.2 27.0 %copy-start.41 = (f32[2,1,3348]{2,1,0:T(1,128)S(1)}, f32[2,1,3348]{2,1,0:T(1,128)}, u32[]{:S(2)}) copy-start(f32[2,1,3348]{2,1,0:T(1,128)} %param.27) | copy-start | bytes 80356
  321.2 46.0 %copy-start.23 = (bf16[10,64,768]{2,1,0:T(8,128)(2,1)S(1)}, bf16[10,64,768]{2,1,0:T(8,128)(2,1)}, u32[]{:S(2)}) copy-start(bf16[10,64,768]{2,1,0:T(8,128)(2,1)} %get-tuple-element.339) | copy-start | bytes 2949124
  323.5 48.9 %copy-start.36 = (f32[2,8,768]{2,1,0:T(8,128)}, f32[2,8,768]{2,1,0:T(8,128)S(1)}, u32[]{:S(2)}) copy-start(f32[2,8,768]{2,1,0:T(8,128)S(1)} %reshape.263) | copy-start | bytes 147460
  343.8 21.5 %collective-permute-start.46 = (bf16[10,64,768]{2,1,0:T(8,128)(2,1)}, bf16[10,64,768]{2,1,0:T(8,128)(2,1)S(1)}, u32[]{:S(2)}, u32[]{:S(2)}) collective-permute-start(bf16[10,64,768]{2,1,0:T(8,128)(2,1)} %add_convert_fusion), channel_id=1, source_target_pairs={{0,24},{8,0},{16,8},{24,16},{1,25},{9,1},{17,9},{25,17},{2,26},{10... | collective-permute-start | bytes 2949128 | tf_op jit(solution)/shard_map/ppermute | solution.py:107
  345.2 22.0 %collective-permute-start.47 = (bf16[10,64,768]{2,1,0:T(8,128)(2,1)S(1)}, bf16[10,64,768]{2,1,0:T(8,128)(2,1)S(1)}, u32[]{:S(2)}, u32[]{:S(2)}) collective-permute-start(bf16[10,64,768]{2,1,0:T(8,128)(2,1)S(1)} %copy-done.24), channel_id=1, source_target_pairs={{0,4},{4,0},{1,5},{5,1},{2,6},{6,2},{3,7},{7,3},{8,12},{12,8},{9,1... | collective-permute-start | bytes 2949128 | tf_op jit(solution)/shard_map/ppermute | solution.py:107
  (31 other events, 223.2 us)
where the time goes:
time: 379 us; the launch traced here: 375 us
  waiting for transfers between devices  242 us (64%)
  Pallas kernels  57.2 us (15%)
  starting transfers between devices  39.2 us (10%)
  other arithmetic  21.7 us (6%)
  local copies, waits for them, and re-layouts  12.8 us (3%)
    ppermute x21, waiting for transfers between devices, send(): self.come.append(lax.ppermute(v, axis, perm))  164 us
    ppermute x25, waiting for transfers between devices, swap(): return lax.ppermute(v, axis, [(0, 1), (1, 0)])  70.2 us
    pallas_call x25, Pallas kernels, call(): pl.pallas_call(functools.partial(kernel, **options), out_shape=shapes, in...  57.2 us
    ppermute x25, starting transfers between devices, swap(): return lax.ppermute(v, axis, [(0, 1), (1, 0)])  16.8 us
    ppermute x21, starting transfers between devices, send(): self.come.append(lax.ppermute(v, axis, perm))  16.5 us
    ppermute x4, waiting for transfers between devices, sum_over(): v = v + lax.ppermute(v, axis, [(i, i ^ step) for i in range(size)])  8.5 us
    unnamed x92, local copies, waits for them, and re-layouts  7.7 us
  transfers between devices with their start and end apart: 50, of which 37 were waited for; matrix products, arithmetic and copies ran while one was open for 5% of the time, Pallas kernels for 8%

commit v1 on v0

--- a/solution.py
+++ b/solution.py
@@ -109,66 +109,44 @@
 
 
 SWAP = [(0, 1), (1, 0)]
-AHEAD = 1
-
-
-def spans(order, capacity):
-    pieces = []
-    for s, parts in order:
-        cuts = [capacity * i // parts for i in range(parts + 1)]
-        pieces += [(s, a, b) for a, b in zip(cuts, cuts[1:])]
-    return pieces
-
-
-def gather_order(nz, capacity):
-    if nz != 4:
-        return spans([(s, 1) for s in range(nz)], capacity)
-    return spans([(0, 1), (1, 1), (2, 2), (3, 2)], capacity)
-
-
-def scatter_order(nz, capacity):
-    if nz != 4:
-        return spans([(s, 1) for s in range(1, nz)] + [(0, 1)], capacity)
-    return spans([(2, 2), (1, 1), (3, 1), (0, 1)], capacity)
-
-
-def gather_stores(store, order):
+
+
+def low_bit(s):
+    return s & -s
+
+
+def gather_stores(store, near):
     nz = lax.axis_size("z")
-    along_z, along_x = Line(AHEAD), Line()
-    near, far = [], []
-    for s, start, stop in order:
-        piece = store if stop - start == store.shape[0] else store[start:stop]
+    along_z, along_x = Line(2), Line()
+    blocks = [store]
+    for s in range(1, nz):
+        perm = [(i, i ^ low_bit(s)) for i in range(nz)]
+        sent = blocks[s - low_bit(s)]
+        blocks.append(along_z.send(after(sent, near) if s == 2 else sent, "z", perm))
+    return blocks + [along_x.send(v, "x", SWAP) for v in blocks]
+
+
+class ScatterSums:
+    def __init__(self, grads):
+        self.grads, self.count = grads, len(grads) // 2
+        self.along_z, self.along_x = Line(), Line()
+        self.come = [[] for _ in range(self.count)]
+        self.parts = []
+
+    def step(self):
+        s = self.count - 1 - len(self.parts)
+        got = self.along_x.send(self.grads[self.count + s], "x", SWAP)
+        ours = self.grads[s]
+        if self.parts:
+            ours = after(ours, self.parts[-1])
+        part = sum(v.astype(f32) for v in [ours, got] + self.come[s])
         if s:
-            piece = along_z.send(piece, "z", [((i + s) % nz, i) for i in range(nz)])
-        near.append(piece)
-        far.append(along_x.send(piece, "x", SWAP))
-    return near + far
-
-
-class ScatterSums:
-    def __init__(self, grads, order):
-        self.grads, self.order = grads, order
-        self.along_z, self.along_x = Line(AHEAD), Line()
-        self.totals, self.part, self.next = {}, None, 0
-
-    def step(self):
-        nz = lax.axis_size("z")
-        s, _, _ = self.order[self.next]
-        ours, theirs = self.grads[self.next], self.grads[len(self.order) + self.next]
-        got = self.along_x.send(theirs, "x", SWAP)
-        if self.part is not None:
-            ours = after(ours, self.part)
-        self.part = ours.astype(f32) + got.astype(f32)
-        term = self.part
-        if s:
-            self.part = self.part.astype(bf16)
-            term = self.along_z.send(self.part, "z", [(k, (k + s) % nz) for k in range(nz)])
-        self.totals.setdefault(s, []).append(term)
-        self.next += 1
-
-    def result(self):
-        totals = [jnp.concatenate(v, axis=0) if len(v) > 1 else v[0] for v in self.totals.values()]
-        return sum(v.astype(f32) for v in totals)
+            part = part.astype(bf16)
+            perm = [(i, i ^ low_bit(s)) for i in range(self.count)]
+            if s == 1:
+                self.along_z.ahead = 2
+            self.come[s - low_bit(s)].append(self.along_z.send(part, "z", perm))
+        self.parts.append(part)
 
 
 def after(v, *others):
@@ -184,16 +162,13 @@
     return v
 
 
-def deal_kernel(near_unit, *refs, low, order):
+def deal_kernel(near_unit, *refs, low):
     *blocks, first, second, third, semaphores = refs
-    nz = near_unit.shape[0] // 2
     group = first.shape[0]
     outs = (first, second, third)
-    for i, block in enumerate(blocks):
-        s, start, stop = order[i % len(order)]
-        owner = s + nz * (i // len(order))
-        for k in range(stop - start):
-            unit = near_unit[owner, start + k] - low
+    for owner, block in enumerate(blocks):
+        for k in range(block.shape[0]):
+            unit = near_unit[owner, k] - low
             for j, out in enumerate(outs):
 
                 @pl.when((unit >= j * group) & (unit < (j + 1) * group))
@@ -583,28 +558,20 @@
     my_y, my_c = lax.axis_index("y"), lax.axis_index("core")
 
     slots = unit_slots(owners, capacity)
-    order = gather_order(nz, capacity)
-    blocks = gather_stores(weight_store.astype(bf16), order)
+    both = swap(jnp.concatenate([tokens_in, out_grad], axis=0), "y")
+    blocks = gather_stores(weight_store.astype(bf16), both)
 
     group = hidden // HEAD
     near_x = (my_x + jnp.arange(2, dtype=jnp.int32)) % 2
-    near_z = (my_z + jnp.arange(nz, dtype=jnp.int32)) % nz
+    near_z = my_z ^ jnp.arange(nz, dtype=jnp.int32)
     owner_of = (near_z[None, :] * 2 + near_x[:, None]).reshape(-1)
     unit_ids = jnp.arange(slots.shape[0], dtype=jnp.int32)
     near_slots = owner_of[:, None] * capacity + jnp.arange(capacity, dtype=jnp.int32)[None, :]
     near_match = near_slots[:, :, None] == slots[None, None, :]
     near_unit = jnp.sum(jnp.where(near_match, unit_ids, 0), axis=2)
     near_unit = jnp.where(jnp.any(near_match, axis=2), near_unit, slots.shape[0])
-    back_order = scatter_order(nz, capacity)
     in_pieces = owners_all == 8
-    near_ids = [[0] * capacity for _ in range(owners_all)]
-    for i, (s, start, stop) in enumerate(back_order):
-        for x in range(2):
-            for k in range(start, stop):
-                near_ids[x * nz + s][k] = (x * len(back_order) + i) * capacity + k - start
-    if not in_pieces:
-        near_ids = [[p * capacity + k for k in range(capacity)] for p in range(owners_all)]
-    near_ids = jnp.asarray(near_ids, jnp.int32)[:, :, None]
+    near_ids = jnp.arange(owners_all * capacity, dtype=jnp.int32).reshape(owners_all, capacity, 1)
     near_slot = jnp.sum(jnp.where(near_match, near_ids, 0), axis=(0, 1))
 
     segment, position = image_layout(lengths[0], tokens)
@@ -659,7 +626,6 @@
                 2,
                 scratch=[pltpu.SemaphoreType.DMA((3,))],
                 low=low,
-                order=order,
             )
         else:
             whole = jnp.concatenate(blocks, axis=0)
@@ -671,7 +637,6 @@
             taken = [whole[low + i * group : low + (i + 1) * group] for i in range(3)]
         return [v.reshape(-1, D) for v in taken]
 
-    both = jnp.concatenate([tokens_in, out_grad], axis=0)
     x, a0, x_far, upper, e0 = call(
         start_kernel,
         [
@@ -681,7 +646,7 @@
             ((half, D), f32, STAY),
             ((half, D), bf16),
         ],
-        [tokens_in, out_grad, swap(both, "y"), shared_params],
+        [tokens_in, out_grad, both, shared_params],
         "start",
         0,
     )
@@ -761,9 +726,9 @@
         saved.append(state + (branch_two,))
 
     grads = None
-    sizes = [stop - start for _, start, stop in back_order] * 2 if in_pieces else [owners_all * capacity]
+    sizes = [capacity] * owners_all if in_pieces else [owners_all * capacity]
     buffers = [((size, HEAD, D), bf16, FAR) for size in sizes]
-    norm_sums, table_args = [], []
+    norm_sums, tables = [], [None] * LAYERS
     for level in reversed(range(LAYERS)):
         x_far, a0_far, a1_far, qkv, mixed, logs, w_head, branch = saved[level][:8]
         x_mid_far, c0_far, c1_far, u, slope, w1, w2 = saved[level][8:15]
@@ -797,13 +762,18 @@
             count=len(buffers),
             capacity=capacity,
         )
+        waiting = [grads[0]]
+        if level + 1 < LAYERS:
+            args = [after(above[0], ours)] + list(above[1:])
+            tables[level + 1] = call(table_kernel, [((PACKED, 128), f32)], args, "table", 3)[0]
+            waiting += [tables[level + 1], theirs_early]
         d_mid, e0, sums_two = call(
             join_back((level, 4), (level, 2)),
             [((half, D), f32), ((half, D), bf16), ((4, D), f32)],
             [
                 ours,
                 theirs,
-                after(x_mid_far, grads[0]),
+                after(x_mid_far, *waiting),
                 upper,
                 branch,
                 shared_params,
@@ -843,7 +813,7 @@
             count=len(buffers),
             capacity=capacity,
         )
-        table_args.append([d_qkv, d_b1, d_scores, hot, hot_t])
+        table_args = (d_qkv, d_b1, d_scores, hot, hot_t)
         if level > 0:
             x_far = after(x_far, grads[0])
             upper, e0, sums_one = call(
@@ -854,18 +824,17 @@
                 0,
                 )
             e1 = swap(e0, "core")
+            above = table_args
+            early = chip_sum(after(final_parts[0], e0), after(final_parts[1], e0))
+            theirs_early = swap(early[rows:], "y")
         else:
             if not in_pieces:
-                grads = [
-                    grads[0][p * capacity + start : p * capacity + stop]
-                    for x in range(2)
-                    for s, start, stop in back_order
-                    for p in [x * nz + s]
-                ]
-            scatter = ScatterSums(grads, back_order)
+                grads = jnp.split(grads[0], owners_all, axis=0)
+            args = [after(table_args[0], grads[0])] + list(table_args[1:])
+            tables[0] = call(table_kernel, [((PACKED, 128), f32)], args, "table", 3)[0]
+            ours = chip_sum(keep, after(send, grads[0]))
+            scatter = ScatterSums(grads)
             scatter.step()
-            last = scatter.part
-            ours = chip_sum(keep, after(send, last))
             input_grad, sums_one = call(
                 last_back_kernel,
                 [((rows, D), f32), ((2, D), f32)],
@@ -875,10 +844,8 @@
                 )
         norm_sums.append((sums_one, sums_two))
 
-    keep, send = after(final_parts, last)
-    ours = chip_sum(keep, send)
     final_branch = (
-        ours[:rows].astype(f32) + swap(ours[rows:], "y").astype(f32) + shared_params[LAYERS - 1, 7]
+        early[:rows].astype(f32) + theirs_early.astype(f32) + shared_params[LAYERS - 1, 7]
     )
     last_scale = shared_params[LAYERS - 1, 6]
     block_out = (x_mid[:rows] + last_scale * final_branch).astype(bf16)
@@ -886,28 +853,25 @@
     branch_sums = jnp.stack(
         [jnp.sum(own_grad * final_branch, axis=0), jnp.sum(last_scale * own_grad, axis=0)]
     )
-    shared_grads, packed = [], []
-    for sums, args in zip(norm_sums, table_args):
-        sums_one, sums_two = sums
+    shared_grads = []
+    for sums_one, sums_two in norm_sums:
         shared_grads = [sums_one[0:2], sums_two[2:4], sums_two[0:2], branch_sums] + shared_grads
         branch_sums = sums_one[2:4]
-        table = call(
-            table_kernel, [((PACKED, 128), f32)], [after(args[0], last)] + args[1:], "table", 3
-        )[0]
-        packed.insert(0, table)
 
     shared_part = jnp.concatenate(shared_grads, axis=0)
     shared_part = sum_over(sum_over(shared_part, "core"), "y")
-    small = jnp.concatenate([shared_part.reshape(-1, 128)] + packed, axis=0)
+    small = jnp.concatenate([shared_part.reshape(-1, 128)] + tables, axis=0)
+    small = small + scatter.along_x.send(small, "x", SWAP)
+    while len(scatter.parts) < scatter.count - 1:
+        scatter.step()
+    small = after(small, scatter.along_z.come[0])
+    step = 1
+    while step < nz:
+        come = lax.ppermute(small, "z", [(i, i ^ step) for i in range(nz)])
+        step *= 2
+        small = small + (come if step < nz else after(come, scatter.parts[-1]))
     scatter.step()
-    scatter.step()
-    small = small + scatter.along_x.send(small, "x", SWAP)
-    while scatter.next < len(back_order) - 1:
-        scatter.step()
-    small = sum_over(small, "z")
-    small = after(small, scatter.part)
-    scatter.step()
-    mine = scatter.result()
+    mine = scatter.parts[-1]
     lines = shared_part.size // 128
     shared_total = small[:lines].reshape(shared_params.shape)
     split_grads = []

time: 379 us -> 361 us (0.953)
  waiting for transfers between devices: 242 us -> 232 us
  local copies, waits for them, and re-layouts: 12.8 us -> 3.68 us
    ppermute x21 -> x15, waiting for transfers between devices: 164 us -> 140 us  [send(): self.come.append(lax.ppermute(v, axis, perm))]
    ppermute x0 -> x2, waiting for transfers between devices: none -> 14 us  [per_device(): come = lax.ppermute(small, 'z', [(i, i ^ step) for i in range(nz)])]
    ppermute x25, waiting for transfers between devices: 70.2 us -> 77.6 us  [swap(): return lax.ppermute(v, axis, [(0, 1), (1, 0)])]
    ppermute x4 -> x2, waiting for transfers between devices: 8.5 us -> 1.22 us  [sum_over(): v = v + lax.ppermute(v, axis, [(i, i ^ step) for i in range(size)])]
    unnamed x92 -> x46, local copies, waits for them, and re-layouts: 7.7 us -> 1.07 us
    ppermute x21 -> x15, starting transfers between devices: 16.5 us -> 21.2 us  [send(): self.come.append(lax.ppermute(v, axis, perm))]
    ppermute x4 -> x2, starting transfers between devices: 5.96 us -> 1.65 us  [sum_over(): v = v + lax.ppermute(v, axis, [(i, i ^ step) for i in range(size)])]
    convert_element_type x5 -> x4, other arithmetic: 8.51 us -> 8.71 us  [the longest x3 6.98 us: step(): part = part.astype(bf16)]
  transfers between devices with their start and end apart: 50 -> 44, of which waited for: 37 -> 34; matrix products, arithmetic and copies ran while one was open for 5% -> 4% of each run, Pallas kernels for 8% -> 9%
where the time goes in v1:
time: 361 us; the launch traced here: 358 us
  waiting for transfers between devices  232 us (64%)
  Pallas kernels  55.1 us (15%)
  starting transfers between devices  42.6 us (12%)
  other arithmetic  22.3 us (6%)
  local copies, waits for them, and re-layouts  3.68 us (1%)
    ppermute x15, waiting for transfers between devices, send(): self.come.append(lax.ppermute(v, axis, perm))  140 us
    ppermute x25, waiting for transfers between devices, swap(): return lax.ppermute(v, axis, [(0, 1), (1, 0)])  77.6 us
    pallas_call x25, Pallas kernels, call(): pl.pallas_call(functools.partial(kernel, **options), out_shape=shapes, in...  55.1 us
    ppermute x15, starting transfers between devices, send(): self.come.append(lax.ppermute(v, axis, perm))  21.2 us
    ppermute x25, starting transfers between devices, swap(): return lax.ppermute(v, axis, [(0, 1), (1, 0)])  17.3 us
    ppermute x2, waiting for transfers between devices, per_device(): come = lax.ppermute(small, 'z', [(i, i ^ step) for i in range(nz)])  14 us
  transfers between devices with their start and end apart: 44, of which 34 were waited for; matrix products, arithmetic and copies ran while one was open for 4% of the time, Pallas kernels for 9%

profile of v1, /device:TPU:0, one launch (start us, length us, event | category | flops | bytes accessed | tf_op | source)
XLA Modules:
  0.0 357.8 jit_solution(9511301808032253985)
XLA Ops:
  0.7 1.7 convert_element_type.139.refs_0_
  2.4 3.1 collective-permute-start.2
  7.1 1.6 collective-permute-start
  9.0 8.4 %collective-permute-done.near = bf16[256,768]{1,0:T(8,128)(2,1)S(1)} collective-permute-done((bf16[256,768]{1,0:T(8,128)(2,1)S(1)}, bf16[256,768]{1,0:T(8,128)(2,1)S(1)}, u32[]{:S(2)}, u32[]{:S(2)}) %collective-permute-start) | collective-permute-done | bytes 393248 | tf_op jit(solution)/shard_map/ppermute | solution.py:97
  17.4 2.6 collective-permute-start.3
  20.0 17.4 %collective-permute-done.2.refs_1_ = bf16[10,64,768]{2,1,0:T(8,128)(2,1)S(1)} collective-permute-done((bf16[10,64,768]{2,1,0:T(8,128)(2,1)S(1)}, bf16[10,64,768]{2,1,0:T(8,128)(2,1)S(1)}, u32[]{:S(2)}, u32[]{:S(2)}) %collective-permute-start.2) | collective-permute-done | bytes 983072 | tf_op jit(solution)/shard_map/ppermute | solution.py:107
  37.5 2.6 collective-permute-start.6
  40.4 21.3 %collective-permute-done.3.refs_2_ = bf16[10,64,768]{2,1,0:T(8,128)(2,1)} collective-permute-done((bf16[10,64,768]{2,1,0:T(8,128)(2,1)S(1)}, bf16[10,64,768]{2,1,0:T(8,128)(2,1)}, u32[]{:S(2)}, u32[]{:S(2)}) %collective-permute-start.3) | collective-permute-done | bytes 983072 | tf_op jit(solution)/shard_map/ppermute | solution.py:107
  64.6 18.6 %collective-permute-done.4.refs_3_ = bf16[10,64,768]{2,1,0:T(8,128)(2,1)} collective-permute-done((bf16[10,64,768]{2,1,0:T(8,128)(2,1)}, bf16[10,64,768]{2,1,0:T(8,128)(2,1)}, u32[]{:S(2)}, u32[]{:S(2)}) %collective-permute-start.4) | collective-permute-done | bytes 983072 | tf_op jit(solution)/shard_map/ppermute | solution.py:107
  85.0 6.0 %prepare.1 = (bf16[512,256]{1,0:T(8,128)(2,1)S(1)}, bf16[256,512]{1,0:T(8,128)(2,1)S(1)}, f32[3,512,512]{2,1,0:T(8,128)S(1)}, f32[3,512,512]{2,1,0:T(8,128)S(1)}) custom-call(f32[6,32,32]{2,1,0:T(8,128)S(1)} %pad.4.table, f32[6,3]{1,0:T(8,128)S(1)} %slice.176.ends, s32[512,1]{1,0:T(8,128)S(1)} %copy.63.code_c, s32[512,1]{1,0:T(8,128)S(1)} %copy.64.seg_c, ...), custom_call_target="tpu_custom_call" | custom-call | flops 6000000000 | bytes 1 | tf_op jit(solution)/shard_map/prepare/pallas_call | solution.py:81
  91.6 12.9 %collective-permute-done.8.refs_7_ = bf16[10,64,768]{2,1,0:T(8,128)(2,1)S(1)} collective-permute-done((bf16[10,64,768]{2,1,0:T(8,128)(2,1)}, bf16[10,64,768]{2,1,0:T(8,128)(2,1)S(1)}, u32[]{:S(2)}, u32[]{:S(2)}) %collective-permute-start.8) | collective-permute-done | bytes 983072 | tf_op jit(solution)/shard_map/ppermute | solution.py:107
  105.5 2.8 deal.2
  108.3 2.7 attention.2
  111.0 1.7 collective-permute-done.9
  112.8 1.6 collective-permute-start.10
  114.4 2.8 deal.3
  117.2 6.8 %collective-permute-done.10.theirs = bf16[256,768]{1,0:T(8,128)(2,1)S(1)} collective-permute-done((bf16[256,768]{1,0:T(8,128)(2,1)S(1)}, bf16[256,768]{1,0:T(8,128)(2,1)S(1)}, u32[]{:S(2)}, u32[]{:S(2)}) %collective-permute-start.10) | collective-permute-done | bytes 393248 | tf_op jit(solution)/shard_map/ppermute | solution.py:97
  124.5 1.7 collective-permute-done.11.c1
  126.2 2.2 hidden.2
  128.6 1.6 collective-permute-done.12
  130.3 1.6 collective-permute-start.13
  131.9 9.6 %collective-permute-done.13.theirs = bf16[256,768]{1,0:T(8,128)(2,1)S(1)} collective-permute-done((bf16[256,768]{1,0:T(8,128)(2,1)S(1)}, bf16[256,768]{1,0:T(8,128)(2,1)S(1)}, u32[]{:S(2)}, u32[]{:S(2)}) %collective-permute-start.13) | collective-permute-done | bytes 393248 | tf_op jit(solution)/shard_map/ppermute | solution.py:97
  142.0 1.7 collective-permute-done.14.a1
  143.7 2.7 attention.3
  146.6 1.6 collective-permute-done.15
  149.9 9.6 %collective-permute-done.16.theirs = bf16[256,768]{1,0:T(8,128)(2,1)S(1)} collective-permute-done((bf16[256,768]{1,0:T(8,128)(2,1)S(1)}, bf16[256,768]{1,0:T(8,128)(2,1)S(1)}, u32[]{:S(2)}, u32[]{:S(2)}) %collective-permute-start.16) | collective-permute-done | bytes 393248 | tf_op jit(solution)/shard_map/ppermute | solution.py:97
  161.7 2.4 hidden.3
  164.1 2.1 hidden_back.2
  166.4 1.6 collective-permute-done.19
  169.7 3.1 hidden_weights.2
  172.7 6.6 %collective-permute-done.20.theirs = bf16[256,768]{1,0:T(8,128)(2,1)S(1)} collective-permute-done((bf16[256,768]{1,0:T(8,128)(2,1)S(1)}, bf16[256,768]{1,0:T(8,128)(2,1)S(1)}, u32[]{:S(2)}, u32[]{:S(2)}) %collective-permute-start.20) | collective-permute-done | bytes 393248 | tf_op jit(solution)/shard_map/ppermute | solution.py:97
  180.1 1.7 collective-permute-done.21.e1
  181.8 4.0 %attention_back.2 = (bf16[512,576]{1,0:T(8,128)(2,1)S(1)}, bf16[3,512,512]{2,1,0:T(8,128)(2,1)S(1)}, bf16[256,768]{1,0:T(8,128)(2,1)S(1)}, bf16[256,768]{1,0:T(8...) custom-call(bf16[256,768]{1,0:T(8,128)(2,1)S(1)} %get-tuple-element.212.e0, ...), custom_call_target="tpu_custom_call" | custom-call | bytes 1 | tf_op jit(solution)/shard_map/attention_back/pallas_call | solution.py:81
  186.0 1.6 collective-permute-done.22
  189.3 2.4 attention_weights.2
  191.7 7.3 %collective-permute-done.23.theirs = bf16[256,768]{1,0:T(8,128)(2,1)S(1)} collective-permute-done((bf16[256,768]{1,0:T(8,128)(2,1)S(1)}, bf16[256,768]{1,0:T(8,128)(2,1)S(1)}, u32[]{:S(2)}, u32[]{:S(2)}) %collective-permute-start.23) | collective-permute-done | bytes 393248 | tf_op jit(solution)/shard_map/ppermute | solution.py:97
  201.4 2.1 hidden_back.3
  204.2 1.6 collective-permute-start.25
  207.4 2.8 table.2
  210.2 3.1 hidden_weights.3
  213.3 6.6 %collective-permute-done.28.theirs = bf16[256,768]{1,0:T(8,128)(2,1)S(1)} collective-permute-done((bf16[256,768]{1,0:T(8,128)(2,1)S(1)}, bf16[256,768]{1,0:T(8,128)(2,1)S(1)}, u32[]{:S(2)}, u32[]{:S(2)}) %collective-permute-start.28) | collective-permute-done | bytes 393248 | tf_op jit(solution)/shard_map/ppermute | solution.py:97
  220.7 1.7 collective-permute-done.29.e1
  222.4 4.0 %attention_back.3 = (bf16[512,576]{1,0:T(8,128)(2,1)S(1)}, bf16[3,512,512]{2,1,0:T(8,128)(2,1)S(1)}, bf16[256,768]{1,0:T(8,128)(2,1)S(1)}, bf16[256,768]{1,0:T(8...) custom-call(bf16[256,768]{1,0:T(8,128)(2,1)S(1)} %get-tuple-element.267.e0, ...), custom_call_target="tpu_custom_call" | custom-call | bytes 1 | tf_op jit(solution)/shard_map/attention_back/pallas_call | solution.py:81
  226.4 2.4 attention_weights.3
  229.0 1.7 collective-permute-start.32
  233.3 5.4 %collective-permute-done.31.theirs = bf16[128,768]{1,0:T(8,128)(2,1)S(1)} collective-permute-done((bf16[128,768]{1,0:T(8,128)(2,1)S(1)}, bf16[128,768]{1,0:T(8,128)(2,1)S(1)}, u32[]{:S(2)}, u32[]{:S(2)}) %collective-permute-start.31) | collective-permute-done | bytes 196640 | tf_op jit(solution)/shard_map/ppermute | solution.py:97
  242.7 3.0 table.3
  245.7 7.6 %collective-permute-done.32 = bf16[10,64,768]{2,1,0:T(8,128)(2,1)} collective-permute-done((bf16[10,64,768]{2,1,0:T(8,128)(2,1)}, bf16[10,64,768]{2,1,0:T(8,128)(2,1)}, u32[]{:S(2)}, u32[]{:S(2)}) %collective-permute-start.32) | collective-permute-done | bytes 983072 | tf_op jit(solution)/shard_map/ppermute | solution.py:107
  253.3 1.7 collective-permute-start.35
  255.0 2.9 collective-permute-done.35
  257.9 1.7 collective-permute-start.36
  259.6 1.7 add_convert_fusion.2
  261.7 18.6 %collective-permute-done.36 = bf16[10,64,768]{2,1,0:T(8,128)(2,1)} collective-permute-done((bf16[10,64,768]{2,1,0:T(8,128)(2,1)}, bf16[10,64,768]{2,1,0:T(8,128)(2,1)}, u32[]{:S(2)}, u32[]{:S(2)}) %collective-permute-start.36) | collective-permute-done | bytes 983072 | tf_op jit(solution)/shard_map/ppermute | solution.py:107
  280.3 1.7 collective-permute-start.38
  283.8 4.2 %collective-permute-done.42 = f32[192,128]{1,0:T(8,128)S(1)} collective-permute-done((f32[192,128]{1,0:T(8,128)S(1)}, f32[192,128]{1,0:T(8,128)S(1)}, u32[]{:S(2)}, u32[]{:S(2)}) %collective-permute-start.42) | collective-permute-done | bytes 98336 | tf_op jit(solution)/shard_map/ppermute | solution.py:870
  288.0 2.1 collective-permute-start.43
  290.1 2.8 add_convert_fusion.1
  294.0 7.8 %collective-permute-done.38 = bf16[10,64,768]{2,1,0:T(8,128)(2,1)} collective-permute-done((bf16[10,64,768]{2,1,0:T(8,128)(2,1)}, bf16[10,64,768]{2,1,0:T(8,128)(2,1)}, u32[]{:S(2)}, u32[]{:S(2)}) %collective-permute-start.38) | collective-permute-done | bytes 983072 | tf_op jit(solution)/shard_map/ppermute | solution.py:107
  301.8 2.4 add_convert_fusion
  304.2 9.8 %collective-permute-done.43 = f32[192,128]{1,0:T(8,128)S(1)} collective-permute-done((f32[192,128]{1,0:T(8,128)S(1)}, f32[192,128]{1,0:T(8,128)S(1)}, u32[]{:S(2)}, u32[]{:S(2)}) %collective-permute-start.43) | collective-permute-done | bytes 98336 | tf_op jit(solution)/shard_map/ppermute | solution.py:870
  318.2 18.2 %collective-permute-done.40 = bf16[10,64,768]{2,1,0:T(8,128)(2,1)} collective-permute-done((bf16[10,64,768]{2,1,0:T(8,128)(2,1)}, bf16[10,64,768]{2,1,0:T(8,128)(2,1)}, u32[]{:S(2)}, u32[]{:S(2)}) %collective-permute-start.40) | collective-permute-done | bytes 983072 | tf_op jit(solution)/shard_map/ppermute | solution.py:107
  336.3 12.5 %collective-permute-done.41 = bf16[10,64,768]{2,1,0:T(8,128)(2,1)S(1)} collective-permute-done((bf16[10,64,768]{2,1,0:T(8,128)(2,1)}, bf16[10,64,768]{2,1,0:T(8,128)(2,1)S(1)}, u32[]{:S(2)}, u32[]{:S(2)}) %collective-permute-start.41) | collective-permute-done | bytes 983072 | tf_op jit(solution)/shard_map/ppermute | solution.py:107
  348.8 6.3 %subtract_select_fusion = (f32[10,64,768]{2,1,0:T(8,128)}, f32[10,64,768]{2,1,0:T(8,128)S(1)}) fusion(f32[10,64,768]{2,1,0:T(8,128)} %param.19, pred[10]{0:T(512)(128)(4,1)S(1)} %compare_reduce_fusion.1, f32[10,64,768]{2,1,0:T(8,128)} %param.20, f32[10,64,768]{2,1,0:T(8,128)} %param.21, bf16[10,64,768]{2,1,0:T(8,128)(2,1)S(1)} %collective-permute-done.41, ...), kind=kLoop, calls=%fused_computation.3 | loop fusion | flops 11304960 | bytes 13762570 | tf_op jit(solution)/shard_map/jit(_where)/select_n | solution.py:916
  355.1 2.5 broadcast_select_fusion
  (193 shorter events, 37.6 us)
Async XLA Ops:
  0.6 6.4 %copy-start.2 = (bf16[128,768]{1,0:T(8,128)(2,1)S(1)}, bf16[128,768]{1,0:T(8,128)(2,1)}, u32[]{:S(2)}) copy-start(bf16[128,768]{1,0:T(8,128)(2,1)} %tokens.1) | copy-start | bytes 589828
  0.7 6.4 %copy-start.1 = (bf16[128,768]{1,0:T(8,128)(2,1)S(1)}, bf16[128,768]{1,0:T(8,128)(2,1)}, u32[]{:S(2)}) copy-start(bf16[128,768]{1,0:T(8,128)(2,1)} %grads.1) | copy-start | bytes 589828
  0.7 8.0 %copy-start.20 = (s32[1,6]{1,0:T(1,128)S(1)}, s32[1,6]{1,0:T(1,128)}, u32[]{:S(2)}) copy-start(s32[1,6]{1,0:T(1,128)} %param.17) | copy-start | bytes 76
  0.7 39.5 %copy-start.21 = (s32[72]{0:T(128)S(1)}, s32[72]{0:T(128)}, u32[]{:S(2)}) copy-start(s32[72]{0:T(128)} %param.18) | copy-start | bytes 868
  0.7 62.5 %copy-start.15 = (f32[2,1,3348]{2,1,0:T(1,128)S(1)}, f32[2,1,3348]{2,1,0:T(1,128)}, u32[]{:S(2)}) copy-start(f32[2,1,3348]{2,1,0:T(1,128)} %param.25) | copy-start | bytes 80356
  2.4 88.6 %copy-start.6 = (bf16[10,64,768]{2,1,0:T(8,128)(2,1)}, bf16[10,64,768]{2,1,0:T(8,128)(2,1)S(1)}, u32[]{:S(2)}) copy-start(bf16[10,64,768]{2,1,0:T(8,128)(2,1)S(1)} %convert_element_type.139.refs_0_) | copy-start | bytes 2949124
  2.4 35.0 %collective-permute-start.2 = (bf16[10,64,768]{2,1,0:T(8,128)(2,1)S(1)}, bf16[10,64,768]{2,1,0:T(8,128)(2,1)S(1)}, u32[]{:S(2)}, u32[]{:S(2)}) collective-permute-start(bf16[10,64,768]{2,1,0:T(8,128)(2,1)S(1)} %convert_element_type.139.refs_0_), channel_id=1, source_target_pairs={{0,8},{8,0},{16,24},{24,16},{1,9},{9,1},{17,25},{25,17},{2,10},{10... | collective-permute-start | bytes 2949128 | tf_op jit(solution)/shard_map/ppermute | solution.py:107
  5.5 31.9 %collective-permute-start.5 = (bf16[10,64,768]{2,1,0:T(8,128)(2,1)S(1)}, bf16[10,64,768]{2,1,0:T(8,128)(2,1)}, u32[]{:S(2)}, u32[]{:S(2)}) collective-permute-start(bf16[10,64,768]{2,1,0:T(8,128)(2,1)S(1)} %convert_element_type.139.refs_0_), channel_id=1, source_target_pairs={{0,4},{4,0},{1,5},{5,1},{2,6},{6,2},{3,7},{7,3},{8,12},{12,8},{9,1... | collective-permute-start | bytes 2949128 | tf_op jit(solution)/shard_map/ppermute | solution.py:107
  7.1 10.4 %collective-permute-start = (bf16[256,768]{1,0:T(8,128)(2,1)S(1)}, bf16[256,768]{1,0:T(8,128)(2,1)S(1)}, u32[]{:S(2)}, u32[]{:S(2)}) collective-permute-start(bf16[256,768]{1,0:T(8,128)(2,1)S(1)} %pad_maximum_fusion), channel_id=1, source_target_pairs={{0,2},{2,0},{1,3},{3,1},{4,6},{6,4},{5,7},{7,5},{8,10},{10,8},{9,1... | collective-permute-start | bytes 1179656 | tf_op jit(solution)/shard_map/ppermute | solution.py:97
  17.4 44.2 %collective-permute-start.3 = (bf16[10,64,768]{2,1,0:T(8,128)(2,1)S(1)}, bf16[10,64,768]{2,1,0:T(8,128)(2,1)}, u32[]{:S(2)}, u32[]{:S(2)}) collective-permute-start(bf16[10,64,768]{2,1,0:T(8,128)(2,1)S(1)} %convert_element_type.139.refs_0_), channel_id=1, source_target_pairs={{0,16},{8,24},{16,0},{24,8},{1,17},{9,25},{17,1},{25,9},{2,18},{10... | collective-permute-start | bytes 2949128 | tf_op jit(solution)/shard_map/ppermute | solution.py:107
  37.5 25.4 %copy-start.11 = (bf16[10,64,768]{2,1,0:T(8,128)(2,1)}, bf16[10,64,768]{2,1,0:T(8,128)(2,1)S(1)}, u32[]{:S(2)}) copy-start(bf16[10,64,768]{2,1,0:T(8,128)(2,1)S(1)} %collective-permute-done.2.refs_1_) | copy-start | bytes 2949124
  37.5 24.2 %collective-permute-start.6 = (bf16[10,64,768]{2,1,0:T(8,128)(2,1)S(1)}, bf16[10,64,768]{2,1,0:T(8,128)(2,1)S(1)}, u32[]{:S(2)}, u32[]{:S(2)}) collective-permute-start(bf16[10,64,768]{2,1,0:T(8,128)(2,1)S(1)} %collective-permute-done.2.refs_1_), channel_id=1, source_target_pairs={{0,4},{4,0},{1,5},{5,1},{2,6},{6,2},{3,7},{7,3},{8,12},{12,8},{9,1... | collective-permute-start | bytes 2949128 | tf_op jit(solution)/shard_map/ppermute | solution.py:107
  61.7 21.6 %collective-permute-start.4 = (bf16[10,64,768]{2,1,0:T(8,128)(2,1)}, bf16[10,64,768]{2,1,0:T(8,128)(2,1)}, u32[]{:S(2)}, u32[]{:S(2)}) collective-permute-start(bf16[10,64,768]{2,1,0:T(8,128)(2,1)} %collective-permute-done.3.refs_2_), channel_id=1, source_target_pairs={{0,8},{8,0},{16,24},{24,16},{1,9},{9,1},{17,25},{25,17},{2,10},{10... | collective-permute-start | bytes 2949128 | tf_op jit(solution)/shard_map/ppermute | solution.py:107
  61.7 21.9 %collective-permute-start.7 = (bf16[10,64,768]{2,1,0:T(8,128)(2,1)}, bf16[10,64,768]{2,1,0:T(8,128)(2,1)}, u32[]{:S(2)}, u32[]{:S(2)}) collective-permute-start(bf16[10,64,768]{2,1,0:T(8,128)(2,1)} %collective-permute-done.3.refs_2_), channel_id=1, source_target_pairs={{0,4},{4,0},{1,5},{5,1},{2,6},{6,2},{3,7},{7,3},{8,12},{12,8},{9,1... | collective-permute-start | bytes 2949128 | tf_op jit(solution)/shard_map/ppermute | solution.py:107
  83.6 21.0 %collective-permute-start.8 = (bf16[10,64,768]{2,1,0:T(8,128)(2,1)}, bf16[10,64,768]{2,1,0:T(8,128)(2,1)S(1)}, u32[]{:S(2)}, u32[]{:S(2)}) collective-permute-start(bf16[10,64,768]{2,1,0:T(8,128)(2,1)} %collective-permute-done.4.refs_3_), channel_id=1, source_target_pairs={{0,4},{4,0},{1,5},{5,1},{2,6},{6,2},{3,7},{7,3},{8,12},{12,8},{9,1... | collective-permute-start | bytes 2949128 | tf_op jit(solution)/shard_map/ppermute | solution.py:107
  85.0 6.0 %copy-start = (f32[2,8,768]{2,1,0:T(8,128)S(1)}, f32[2,8,768]{2,1,0:T(8,128)}, u32[]{:S(2)}) copy-start(f32[2,8,768]{2,1,0:T(8,128)} %shared.15) | copy-start | bytes 147460
  91.5 16.8 %collective-permute-start.1 = (bf16[256,768]{1,0:T(8,128)(2,1)S(1)}, bf16[256,768]{1,0:T(8,128)(2,1)S(1)}, u32[]{:S(2)}, u32[]{:S(2)}) collective-permute-start(bf16[256,768]{1,0:T(8,128)(2,1)S(1)} %get-tuple-element.165.a0), channel_id=1, source_target_pairs={{0,1},{1,0},{2,3},{3,2},{4,5},{5,4},{6,7},{7,6},{8,9},{9,8},{10,11... | collective-permute-start | bytes 1179656 | tf_op jit(solution)/shard_map/ppermute | solution.py:97
  110.9 1.8 collective-permute-start.9
  112.8 11.2 %collective-permute-start.10 = (bf16[256,768]{1,0:T(8,128)(2,1)S(1)}, bf16[256,768]{1,0:T(8,128)(2,1)S(1)}, u32[]{:S(2)}, u32[]{:S(2)}) collective-permute-start(bf16[256,768]{1,0:T(8,128)(2,1)S(1)} %add_convert_fusion.10.ours), channel_id=1, source_target_pairs={{0,2},{2,0},{1,3},{3,1},{4,6},{6,4},{5,7},{7,5},{8,10},{10,8},{9,1... | collective-permute-start | bytes 1179656 | tf_op jit(solution)/shard_map/ppermute | solution.py:97
  124.4 1.8 collective-permute-start.11
  128.4 1.8 collective-permute-start.12
  130.3 11.2 %collective-permute-start.13 = (bf16[256,768]{1,0:T(8,128)(2,1)S(1)}, bf16[256,768]{1,0:T(8,128)(2,1)S(1)}, u32[]{:S(2)}, u32[]{:S(2)}) collective-permute-start(bf16[256,768]{1,0:T(8,128)(2,1)S(1)} %add_convert_fusion.9.ours), channel_id=1, source_target_pairs={{0,2},{2,0},{1,3},{3,1},{4,6},{6,4},{5,7},{7,5},{8,10},{10,8},{9,1... | collective-permute-start | bytes 1179656 | tf_op jit(solution)/shard_map/ppermute | solution.py:97
  141.9 1.8 collective-permute-start.14
  146.4 1.8 collective-permute-start.15
  148.3 11.2 %collective-permute-start.16 = (bf16[256,768]{1,0:T(8,128)(2,1)S(1)}, bf16[256,768]{1,0:T(8,128)(2,1)S(1)}, u32[]{:S(2)}, u32[]{:S(2)}) collective-permute-start(bf16[256,768]{1,0:T(8,128)(2,1)S(1)} %add_convert_fusion.8.ours), channel_id=1, source_target_pairs={{0,2},{2,0},{1,3},{3,1},{4,6},{6,4},{5,7},{7,5},{8,10},{10,8},{9,1... | collective-permute-start | bytes 1179656 | tf_op jit(solution)/shard_map/ppermute | solution.py:97
  159.9 1.8 collective-permute-start.17
  160.0 4.1 %collective-permute-start.18 = (bf16[256,768]{1,0:T(8,128)(2,1)S(1)}, bf16[256,768]{1,0:T(8,128)(2,1)S(1)}, u32[]{:S(2)}, u32[]{:S(2)}) collective-permute-start(bf16[256,768]{1,0:T(8,128)(2,1)S(1)} %get-tuple-element.196.e0), channel_id=1, source_target_pairs={{0,1},{1,0},{2,3},{3,2},{4,5},{5,4},{6,7},{7,6},{8,9},{9,8},{10,11... | collective-permute-start | bytes 1179656 | tf_op jit(solution)/shard_map/ppermute | solution.py:97
  166.2 1.8 collective-permute-start.19
  168.1 11.2 %collective-permute-start.20 = (bf16[256,768]{1,0:T(8,128)(2,1)S(1)}, bf16[256,768]{1,0:T(8,128)(2,1)S(1)}, u32[]{:S(2)}, u32[]{:S(2)}) collective-permute-start(bf16[256,768]{1,0:T(8,128)(2,1)S(1)} %add_convert_fusion.7.ours), channel_id=1, source_target_pairs={{0,2},{2,0},{1,3},{3,1},{4,6},{6,4},{5,7},{7,5},{8,10},{10,8},{9,1... | collective-permute-start | bytes 1179656 | tf_op jit(solution)/shard_map/ppermute | solution.py:97
  180.0 1.8 collective-permute-start.21
  185.8 1.8 collective-permute-start.22
  187.7 11.2 %collective-permute-start.23 = (bf16[256,768]{1,0:T(8,128)(2,1)S(1)}, bf16[256,768]{1,0:T(8,128)(2,1)S(1)}, u32[]{:S(2)}, u32[]{:S(2)}) collective-permute-start(bf16[256,768]{1,0:T(8,128)(2,1)S(1)} %add_convert_fusion.6.ours), channel_id=1, source_target_pairs={{0,2},{2,0},{1,3},{3,1},{4,6},{6,4},{5,7},{7,5},{8,10},{10,8},{9,1... | collective-permute-start | bytes 1179656 | tf_op jit(solution)/shard_map/ppermute | solution.py:97
  199.6 1.8 collective-permute-start.26
  199.7 4.4 %collective-permute-start.24 = (bf16[256,768]{1,0:T(8,128)(2,1)S(1)}, bf16[256,768]{1,0:T(8,128)(2,1)S(1)}, u32[]{:S(2)}, u32[]{:S(2)}) collective-permute-start(bf16[256,768]{1,0:T(8,128)(2,1)S(1)} %get-tuple-element.239), channel_id=1, source_target_pairs={{0,1},{1,0},{2,3},{3,2},{4,5},{5,4},{6,7},{7,6},{8,9},{9,8},{10,11... | collective-permute-start | bytes 1179656 | tf_op jit(solution)/shard_map/ppermute | solution.py:97
  203.5 2.3 collective-permute-start.27
  204.2 9.0 %collective-permute-start.25 = (bf16[128,768]{1,0:T(8,128)(2,1)S(1)}, bf16[128,768]{1,0:T(8,128)(2,1)S(1)}, u32[]{:S(2)}, u32[]{:S(2)}) collective-permute-start(bf16[128,768]{1,0:T(8,128)(2,1)S(1)} %slice.181), channel_id=1, source_target_pairs={{0,2},{2,0},{1,3},{3,1},{4,6},{6,4},{5,7},{7,5},{8,10},{10,8},{9,1... | collective-permute-start | bytes 589832 | tf_op jit(solution)/shard_map/ppermute | solution.py:97
  205.9 14.0 %collective-permute-start.28 = (bf16[256,768]{1,0:T(8,128)(2,1)S(1)}, bf16[256,768]{1,0:T(8,128)(2,1)S(1)}, u32[]{:S(2)}, u32[]{:S(2)}) collective-permute-start(bf16[256,768]{1,0:T(8,128)(2,1)S(1)} %add_convert_fusion.4.ours), channel_id=1, source_target_pairs={{0,2},{2,0},{1,3},{3,1},{4,6},{6,4},{5,7},{7,5},{8,10},{10,8},{9,1... | collective-permute-start | bytes 1179656 | tf_op jit(solution)/shard_map/ppermute | solution.py:97
  220.6 1.8 collective-permute-start.29
  228.8 2.8 collective-permute-start.30
  229.0 24.4 %collective-permute-start.32 = (bf16[10,64,768]{2,1,0:T(8,128)(2,1)}, bf16[10,64,768]{2,1,0:T(8,128)(2,1)}, u32[]{:S(2)}, u32[]{:S(2)}) collective-permute-start(bf16[10,64,768]{2,1,0:T(8,128)(2,1)} %get-tuple-element.293), channel_id=1, source_target_pairs={{0,4},{4,0},{1,5},{5,1},{2,6},{6,2},{3,7},{7,3},{8,12},{12,8},{9,1... | collective-permute-start | bytes 2949128 | tf_op jit(solution)/shard_map/ppermute | solution.py:107
  231.7 7.0 %collective-permute-start.31 = (bf16[128,768]{1,0:T(8,128)(2,1)S(1)}, bf16[128,768]{1,0:T(8,128)(2,1)S(1)}, u32[]{:S(2)}, u32[]{:S(2)}) collective-permute-start(bf16[128,768]{1,0:T(8,128)(2,1)S(1)} %slice.182), channel_id=1, source_target_pairs={{0,2},{2,0},{1,3},{3,1},{4,6},{6,4},{5,7},{7,5},{8,10},{10,8},{9,1... | collective-permute-start | bytes 589832 | tf_op jit(solution)/shard_map/ppermute | solution.py:97
  239.8 1.3 collective-permute-start.33
  241.1 4.5 %collective-permute-start.34 = (f32[16,768]{1,0:T(8,128)S(1)}, f32[16,768]{1,0:T(8,128)S(1)}, u32[]{:S(2)}, u32[]{:S(2)}) collective-permute-start(f32[16,768]{1,0:T(8,128)S(1)} %add.265), channel_id=1, source_target_pairs={{0,2},{2,0},{1,3},{3,1},{4,6},{6,4},{5,7},{7,5},{8,10},{10,8},{9,1... | collective-permute-start | bytes 147464 | tf_op jit(solution)/shard_map/ppermute | solution.py:160
  245.7 44.5 %copy-start.4 = (bf16[10,64,768]{2,1,0:T(8,128)(2,1)S(1)}, bf16[10,64,768]{2,1,0:T(8,128)(2,1)}, u32[]{:S(2)}) copy-start(bf16[10,64,768]{2,1,0:T(8,128)(2,1)} %get-tuple-element.294) | copy-start | bytes 2949124
  253.3 4.6 %collective-permute-start.35 = (f32[192,128]{1,0:T(8,128)S(1)}, f32[192,128]{1,0:T(8,128)S(1)}, u32[]{:S(2)}, u32[]{:S(2)}) collective-permute-start(f32[192,128]{1,0:T(8,128)S(1)} %pad_maximum_fusion.1), channel_id=1, source_target_pairs={{0,4},{4,0},{1,5},{5,1},{2,6},{6,2},{3,7},{7,3},{8,12},{12,8},{9,1... | collective-permute-start | bytes 294920 | tf_op jit(solution)/shard_map/ppermute | solution.py:107
  257.9 22.4 %collective-permute-start.36 = (bf16[10,64,768]{2,1,0:T(8,128)(2,1)}, bf16[10,64,768]{2,1,0:T(8,128)(2,1)}, u32[]{:S(2)}, u32[]{:S(2)}) collective-permute-start(bf16[10,64,768]{2,1,0:T(8,128)(2,1)} %get-tuple-element.304), channel_id=1, source_target_pairs={{0,4},{4,0},{1,5},{5,1},{2,6},{6,2},{3,7},{7,3},{8,12},{12,8},{9,1... | collective-permute-start | bytes 2949128 | tf_op jit(solution)/shard_map/ppermute | solution.py:107
  261.4 22.0 %collective-permute-start.37 = (bf16[10,64,768]{2,1,0:T(8,128)(2,1)S(1)}, bf16[10,64,768]{2,1,0:T(8,128)(2,1)}, u32[]{:S(2)}, u32[]{:S(2)}) collective-permute-start(bf16[10,64,768]{2,1,0:T(8,128)(2,1)S(1)} %add_convert_fusion.2), channel_id=1, source_target_pairs={{0,8},{8,0},{16,24},{24,16},{1,9},{9,1},{17,25},{25,17},{2,10},{10... | collective-permute-start | bytes 2949128 | tf_op jit(solution)/shard_map/ppermute | solution.py:107
  280.3 21.5 %collective-permute-start.38 = (bf16[10,64,768]{2,1,0:T(8,128)(2,1)}, bf16[10,64,768]{2,1,0:T(8,128)(2,1)}, u32[]{:S(2)}, u32[]{:S(2)}) collective-permute-start(bf16[10,64,768]{2,1,0:T(8,128)(2,1)} %get-tuple-element.307), channel_id=1, source_target_pairs={{0,4},{4,0},{1,5},{5,1},{2,6},{6,2},{3,7},{7,3},{8,12},{12,8},{9,1... | collective-permute-start | bytes 2949128 | tf_op jit(solution)/shard_map/ppermute | solution.py:107
  283.4 4.6 %collective-permute-start.42 = (f32[192,128]{1,0:T(8,128)S(1)}, f32[192,128]{1,0:T(8,128)S(1)}, u32[]{:S(2)}, u32[]{:S(2)}) collective-permute-start(f32[192,128]{1,0:T(8,128)S(1)} %fusion.16), channel_id=1, source_target_pairs={{0,8},{8,0},{16,24},{24,16},{1,9},{9,1},{17,25},{25,17},{2,10},{10... | collective-permute-start | bytes 294920 | tf_op jit(solution)/shard_map/ppermute | solution.py:870
  288.0 13.8 %copy-start.3 = (bf16[10,64,768]{2,1,0:T(8,128)(2,1)S(1)}, bf16[10,64,768]{2,1,0:T(8,128)(2,1)}, u32[]{:S(2)}) copy-start(bf16[10,64,768]{2,1,0:T(8,128)(2,1)} %get-tuple-element.305) | copy-start | bytes 2949124
  288.0 26.0 %collective-permute-start.43 = (f32[192,128]{1,0:T(8,128)S(1)}, f32[192,128]{1,0:T(8,128)S(1)}, u32[]{:S(2)}, u32[]{:S(2)}) collective-permute-start(f32[192,128]{1,0:T(8,128)S(1)} %add.279), channel_id=1, source_target_pairs={{0,16},{8,24},{16,0},{24,8},{1,17},{9,25},{17,1},{25,9},{2,18},{10... | collective-permute-start | bytes 294920 | tf_op jit(solution)/shard_map/ppermute | solution.py:870
  293.0 22.2 %copy-start.7 = (bf16[10,64,768]{2,1,0:T(8,128)(2,1)S(1)}, bf16[10,64,768]{2,1,0:T(8,128)(2,1)}, u32[]{:S(2)}) copy-start(bf16[10,64,768]{2,1,0:T(8,128)(2,1)} %get-tuple-element.310) | copy-start | bytes 2949124
  293.0 23.0 %copy-start.16 = (f32[2,8,768]{2,1,0:T(8,128)S(1)}, f32[2,8,768]{2,1,0:T(8,128)}, u32[]{:S(2)}) copy-start(f32[2,8,768]{2,1,0:T(8,128)} %param.24) | copy-start | bytes 147460
  293.0 23.1 %copy-start.17 = (f32[2,8,768]{2,1,0:T(8,128)S(1)}, f32[2,8,768]{2,1,0:T(8,128)}, u32[]{:S(2)}) copy-start(f32[2,8,768]{2,1,0:T(8,128)} %param.23) | copy-start | bytes 147460
  293.0 24.4 %copy-start.18 = (f32[2,1,3348]{2,1,0:T(1,128)S(1)}, f32[2,1,3348]{2,1,0:T(1,128)}, u32[]{:S(2)}) copy-start(f32[2,1,3348]{2,1,0:T(1,128)} %param.27) | copy-start | bytes 80356
  293.0 24.4 %copy-start.19 = (f32[2,1,3348]{2,1,0:T(1,128)S(1)}, f32[2,1,3348]{2,1,0:T(1,128)}, u32[]{:S(2)}) copy-start(f32[2,1,3348]{2,1,0:T(1,128)} %param.26) | copy-start | bytes 80356
  293.0 55.8 %copy-start.5 = (bf16[10,64,768]{2,1,0:T(8,128)(2,1)S(1)}, bf16[10,64,768]{2,1,0:T(8,128)(2,1)}, u32[]{:S(2)}) copy-start(bf16[10,64,768]{2,1,0:T(8,128)(2,1)} %get-tuple-element.308) | copy-start | bytes 2949124
  293.0 43.3 %collective-permute-start.40 = (bf16[10,64,768]{2,1,0:T(8,128)(2,1)}, bf16[10,64,768]{2,1,0:T(8,128)(2,1)}, u32[]{:S(2)}, u32[]{:S(2)}) collective-permute-start(bf16[10,64,768]{2,1,0:T(8,128)(2,1)} %add_convert_fusion.1), channel_id=1, source_target_pairs={{0,16},{8,24},{16,0},{24,8},{1,17},{9,25},{17,1},{25,9},{2,18},{10... | collective-permute-start | bytes 2949128 | tf_op jit(solution)/shard_map/ppermute | solution.py:107
  315.2 39.9 %copy-start.14 = (f32[2,8,768]{2,1,0:T(8,128)}, f32[2,8,768]{2,1,0:T(8,128)S(1)}, u32[]{:S(2)}) copy-start(f32[2,8,768]{2,1,0:T(8,128)S(1)} %reshape.271) | copy-start | bytes 147460
  315.2 21.1 %collective-permute-start.39 = (bf16[10,64,768]{2,1,0:T(8,128)(2,1)S(1)}, bf16[10,64,768]{2,1,0:T(8,128)(2,1)S(1)}, u32[]{:S(2)}, u32[]{:S(2)}) collective-permute-start(bf16[10,64,768]{2,1,0:T(8,128)(2,1)S(1)} %copy-done.7), channel_id=1, source_target_pairs={{0,4},{4,0},{1,5},{5,1},{2,6},{6,2},{3,7},{7,3},{8,12},{12,8},{9,1... | collective-permute-start | bytes 2949128 | tf_op jit(solution)/shard_map/ppermute | solution.py:107
  316.0 32.8 %collective-permute-start.41 = (bf16[10,64,768]{2,1,0:T(8,128)(2,1)}, bf16[10,64,768]{2,1,0:T(8,128)(2,1)S(1)}, u32[]{:S(2)}, u32[]{:S(2)}) collective-permute-start(bf16[10,64,768]{2,1,0:T(8,128)(2,1)} %add_convert_fusion), channel_id=1, source_target_pairs={{0,8},{8,0},{16,24},{24,16},{1,9},{9,1},{17,25},{25,17},{2,10},{10... | collective-permute-start | bytes 2949128 | tf_op jit(solution)/shard_map/ppermute | solution.py:107
  318.2 36.9 %copy-start.8 = (f32[10,64,768]{2,1,0:T(8,128)S(1)}, f32[10,64,768]{2,1,0:T(8,128)}, u32[]{:S(2)}) copy-start(f32[10,64,768]{2,1,0:T(8,128)} %param.20) | copy-start | bytes 5898244
  318.2 36.9 %copy-start.9 = (f32[10,64,768]{2,1,0:T(8,128)S(1)}, f32[10,64,768]{2,1,0:T(8,128)}, u32[]{:S(2)}) copy-start(f32[10,64,768]{2,1,0:T(8,128)} %param.21) | copy-start | bytes 5898244
  355.1 2.6 copy-start.10
  (2 other events, 2.1 us)

commit v2 on v1

--- a/solution.py
+++ b/solution.py
@@ -127,25 +127,32 @@
 
 
 class ScatterSums:
-    def __init__(self, grads):
-        self.grads, self.count = grads, len(grads) // 2
+    def __init__(self, ours, theirs):
+        self.ours, self.theirs, self.count = ours, theirs, len(ours)
         self.along_z, self.along_x = Line(), Line()
-        self.come = [[] for _ in range(self.count)]
-        self.parts = []
+        self.come = [[] for _ in ours]
+        self.parts, self.all_parts = [], []
 
     def step(self):
         s = self.count - 1 - len(self.parts)
-        got = self.along_x.send(self.grads[self.count + s], "x", SWAP)
-        ours = self.grads[s]
-        if self.parts:
-            ours = after(ours, self.parts[-1])
-        part = sum(v.astype(f32) for v in [ours, got] + self.come[s])
+        sent = []
+        last = self.parts[-1:]
+        for ours, theirs in zip(self.ours[s], self.theirs[s]):
+            got = self.along_x.send(theirs, "x", SWAP)
+            if last:
+                ours = after(ours, *last)
+            come = self.come[s] if s else self.come[s][:-1]
+            part = sum(v.astype(f32) for v in [ours, got] + come)
+            if s:
+                part = part.astype(bf16)
+                perm = [(i, i ^ low_bit(s)) for i in range(self.count)]
+                if s == 1:
+                    self.along_z.ahead = 2
+                sent.append(self.along_z.send(part, "z", perm))
+            last = [part]
+            self.all_parts.append(part)
         if s:
-            part = part.astype(bf16)
-            perm = [(i, i ^ low_bit(s)) for i in range(self.count)]
-            if s == 1:
-                self.along_z.ahead = 2
-            self.come[s - low_bit(s)].append(self.along_z.send(part, "z", perm))
+            self.come[s - low_bit(s)].append(jnp.concatenate(sent, axis=0) if len(sent) > 1 else sent[0])
         self.parts.append(part)
 
 
@@ -510,6 +517,29 @@
     return (first_new, second_new, weight_new)
 
 
+def fetch_kernel(*refs):
+    count = len(refs) // 2
+    copies = [
+        pltpu.make_async_copy(refs[i], refs[count + i], refs[-1].at[i]) for i in range(count)
+    ]
+    for copy in copies:
+        copy.start()
+    for copy in copies:
+        copy.wait()
+
+
+def update_kernel(used, base, come, weight, first, second, *refs):
+    outs, scratch, semaphores = refs[:4], refs[4:8], refs[8]
+    for k in range(base.shape[0]):
+        grad = base[k] + come[k].astype(f32)
+        values = (grad,) + adam_step(weight[k], first[k], second[k], grad, rate_matrix, weight_decay)
+        for i, value in enumerate(values):
+            scratch[i][k] = jnp.where(used[k] > 0, value, 0.0)
+            pltpu.make_async_copy(scratch[i].at[k], outs[i].at[k], semaphores.at[i]).start()
+    for i in range(4):
+        pltpu.make_async_copy(scratch[i], outs[i], semaphores.at[i]).wait()
+
+
 def image_layout(row_lengths, count):
     endings = jnp.cumsum(row_lengths)
     openings = endings - row_lengths
@@ -571,7 +601,18 @@
     near_unit = jnp.sum(jnp.where(near_match, unit_ids, 0), axis=2)
     near_unit = jnp.where(jnp.any(near_match, axis=2), near_unit, slots.shape[0])
     in_pieces = owners_all == 8
-    near_ids = jnp.arange(owners_all * capacity, dtype=jnp.int32).reshape(owners_all, capacity, 1)
+    sizes = [owners_all * capacity]
+    near_ids = [[p * capacity + k for k in range(capacity)] for p in range(owners_all)]
+    if in_pieces:
+        cut = capacity // 2
+        sizes, near_ids = [], []
+        for p in range(owners_all):
+            ids = []
+            for size in [cut, capacity - cut] if p % nz == nz - 1 else [capacity]:
+                ids += [len(sizes) * capacity + k for k in range(size)]
+                sizes.append(size)
+            near_ids.append(ids)
+    near_ids = jnp.asarray(near_ids, jnp.int32)[:, :, None]
     near_slot = jnp.sum(jnp.where(near_match, near_ids, 0), axis=(0, 1))
 
     segment, position = image_layout(lengths[0], tokens)
@@ -726,7 +767,6 @@
         saved.append(state + (branch_two,))
 
     grads = None
-    sizes = [capacity] * owners_all if in_pieces else [owners_all * capacity]
     buffers = [((size, HEAD, D), bf16, FAR) for size in sizes]
     norm_sums, tables = [], [None] * LAYERS
     for level in reversed(range(LAYERS)):
@@ -830,15 +870,23 @@
         else:
             if not in_pieces:
                 grads = jnp.split(grads[0], owners_all, axis=0)
+                pieces = [[v] for v in grads]
+            else:
+                pieces = []
+                for v in grads:
+                    if pieces and v.shape[0] < capacity and len(pieces[-1]) == 1 and pieces[-1][0].shape[0] < capacity:
+                        pieces[-1].append(v)
+                    else:
+                        pieces.append([v])
             args = [after(table_args[0], grads[0])] + list(table_args[1:])
             tables[0] = call(table_kernel, [((PACKED, 128), f32)], args, "table", 3)[0]
             ours = chip_sum(keep, after(send, grads[0]))
-            scatter = ScatterSums(grads)
+            scatter = ScatterSums(pieces[:nz], pieces[nz:])
             scatter.step()
             input_grad, sums_one = call(
                 last_back_kernel,
                 [((rows, D), f32), ((2, D), f32)],
-                [ours, swap(ours[rows:], "y"), x_far, d_mid, shared_params],
+                [ours, swap(ours[rows:], "y"), after(x_far, scatter.all_parts[0]), d_mid, shared_params],
                 "last_back",
                 0,
                 )
@@ -862,16 +910,15 @@
     shared_part = sum_over(sum_over(shared_part, "core"), "y")
     small = jnp.concatenate([shared_part.reshape(-1, 128)] + tables, axis=0)
     small = small + scatter.along_x.send(small, "x", SWAP)
-    while len(scatter.parts) < scatter.count - 1:
+    scatter.step()
+    step = nz // 2
+    while step:
+        if step == 1:
+            small = after(small, scatter.along_x.come[2], scatter.parts[1])
+        small = small + lax.ppermute(small, "z", [(i, i ^ step) for i in range(nz)])
+        step //= 2
+    while len(scatter.parts) < scatter.count:
         scatter.step()
-    small = after(small, scatter.along_z.come[0])
-    step = 1
-    while step < nz:
-        come = lax.ppermute(small, "z", [(i, i ^ step) for i in range(nz)])
-        step *= 2
-        small = small + (come if step < nz else after(come, scatter.parts[-1]))
-    scatter.step()
-    mine = scatter.parts[-1]
     lines = shared_part.size // 128
     shared_total = small[:lines].reshape(shared_params.shape)
     split_grads = []
@@ -895,11 +942,25 @@
     split_total = jnp.stack(split_grads)[:, None, :]
 
     my_ids = (my_z * 2 + my_x) * capacity + jnp.arange(capacity, dtype=jnp.int32)
-    used = jnp.any(my_ids[:, None] == slots[None, :], axis=1)[:, None, None]
-    zeros = jnp.zeros_like(weight_store)
-    mine = jnp.where(used, mine, zeros)
-    matrix_first, matrix_second, matrix_weight = adam_step(
-        weight_store, first_store, second_store, mine, rate_matrix, weight_decay
+    used = jnp.any(my_ids[:, None] == slots[None, :], axis=1).astype(jnp.int32)
+    base, come = scatter.parts[-1], scatter.come[0][-1]
+    store = (weight_store.shape, f32)
+    state = call(
+        fetch_kernel,
+        [(*store, STAY)] * 3,
+        [(v, FAR) for v in after((weight_store, first_store, second_store), base)],
+        "fetch",
+        2,
+        scratch=[pltpu.SemaphoreType.DMA((3,))],
+    )
+    mine, matrix_first, matrix_second, matrix_weight = call(
+        update_kernel,
+        [(*store, FAR)] * 4,
+        [(used, SMEM), base, come] + list(state),
+        "update",
+        3,
+        scratch=[pltpu.VMEM(*store)] * 4 + [pltpu.SemaphoreType.DMA((4,))],
+        limit=24,
     )
     shared_moment, shared_square, shared_value = adam_step(
         shared_params, shared_first, shared_second, shared_total, rate_small, 0.0
@@ -911,9 +972,9 @@
         block_out,
         input_grad,
         mine,
-        jnp.where(used, matrix_first, zeros),
-        jnp.where(used, matrix_second, zeros),
-        jnp.where(used, matrix_weight, zeros),
+        matrix_first,
+        matrix_second,
+        matrix_weight,
         shared_total,
         shared_moment,
         shared_square,

time: 361 us -> 356 us (0.986)
  waiting for transfers between devices: 232 us -> 221 us
  Pallas kernels: 55.1 us -> 62.1 us
  other arithmetic: 22.3 us -> 16.6 us
  starting transfers between devices: 42.6 us -> 46.9 us
    select_n x2 -> x0, other arithmetic: 8.82 us -> none  [the longest x1 6.27 us: per_device(): jnp.where(used, matrix_weight, zeros)]
    pallas_call x25 -> x27, Pallas kernels: 55.1 us -> 62.1 us  [call(): pl.pallas_call(functools.partial(kernel, **options), out_shape=shapes, in...]
    ppermute x2, waiting for transfers between devices: 14 us -> 7.5 us  [per_device(): small = small + lax.ppermute(small, 'z', [(i, i ^ step) for i in range(nz)])]
    ppermute x25, waiting for transfers between devices: 77.6 us -> 73.1 us  [swap(): return lax.ppermute(v, axis, [(0, 1), (1, 0)])]
    ppermute x15 -> x17, starting transfers between devices: 21.2 us -> 24.3 us  [send(): self.come.append(lax.ppermute(v, axis, perm))]
    convert_element_type x3 -> x4, other arithmetic: 6.98 us -> 8.19 us  [step(): part = part.astype(bf16)]
    ppermute x15 -> x17, waiting for transfers between devices: 140 us -> 140 us  [send(): self.come.append(lax.ppermute(v, axis, perm))]
  transfers between devices with their start and end apart: 44 -> 46, of which waited for: 34 -> 34; matrix products, arithmetic and copies ran while one was open for 4% -> 4% of each run, Pallas kernels for 9% -> 10%
where the time goes in v2:
time: 356 us; the launch traced here: 352 us
  waiting for transfers between devices  221 us (62%)
  Pallas kernels  62.1 us (17%)
  starting transfers between devices  46.9 us (13%)
  other arithmetic  16.6 us (5%)
  local copies, waits for them, and re-layouts  3.68 us (1%)
    ppermute x17, waiting for transfers between devices, send(): self.come.append(lax.ppermute(v, axis, perm))  140 us
    ppermute x25, waiting for transfers between devices, swap(): return lax.ppermute(v, axis, [(0, 1), (1, 0)])  73.1 us
    pallas_call x27, Pallas kernels, call(): pl.pallas_call(functools.partial(kernel, **options), out_shape=shapes, in...  62.1 us
    ppermute x17, starting transfers between devices, send(): self.come.append(lax.ppermute(v, axis, perm))  24.3 us
    ppermute x25, starting transfers between devices, swap(): return lax.ppermute(v, axis, [(0, 1), (1, 0)])  16.6 us
    convert_element_type x4, other arithmetic, step(): part = part.astype(bf16)  8.19 us
    ppermute x2, waiting for transfers between devices, per_device(): small = small + lax.ppermute(small, 'z', [(i, i ^ step) for i in range(nz)])  7.5 us
  transfers between devices with their start and end apart: 46, of which 34 were waited for; matrix products, arithmetic and copies ran while one was open for 4% of the time, Pallas kernels for 10%

profile of v2, /device:TPU:0, one launch (start us, length us, event | category | flops | bytes accessed | tf_op | source)
XLA Modules:
  0.0 352.4 jit_solution(8465057373215271548)
XLA Ops:
  0.7 1.7 convert_element_type.148.refs_0_
  2.5 3.1 collective-permute-start.2
  7.1 1.6 collective-permute-start
  9.0 8.4 %collective-permute-done.near = bf16[256,768]{1,0:T(8,128)(2,1)S(1)} collective-permute-done((bf16[256,768]{1,0:T(8,128)(2,1)S(1)}, bf16[256,768]{1,0:T(8,128)(2,1)S(1)}, u32[]{:S(2)}, u32[]{:S(2)}) %collective-permute-start) | collective-permute-done | bytes 393248 | tf_op jit(solution)/shard_map/ppermute | solution.py:97
  17.4 2.6 collective-permute-start.3
  20.0 17.4 %collective-permute-done.2.refs_1_ = bf16[10,64,768]{2,1,0:T(8,128)(2,1)S(1)} collective-permute-done((bf16[10,64,768]{2,1,0:T(8,128)(2,1)S(1)}, bf16[10,64,768]{2,1,0:T(8,128)(2,1)S(1)}, u32[]{:S(2)}, u32[]{:S(2)}) %collective-permute-start.2) | collective-permute-done | bytes 983072 | tf_op jit(solution)/shard_map/ppermute | solution.py:107
  37.5 2.6 collective-permute-start.6
  40.4 21.3 %collective-permute-done.3.refs_2_ = bf16[10,64,768]{2,1,0:T(8,128)(2,1)} collective-permute-done((bf16[10,64,768]{2,1,0:T(8,128)(2,1)S(1)}, bf16[10,64,768]{2,1,0:T(8,128)(2,1)}, u32[]{:S(2)}, u32[]{:S(2)}) %collective-permute-start.3) | collective-permute-done | bytes 983072 | tf_op jit(solution)/shard_map/ppermute | solution.py:107
  64.6 18.6 %collective-permute-done.4.refs_3_ = bf16[10,64,768]{2,1,0:T(8,128)(2,1)} collective-permute-done((bf16[10,64,768]{2,1,0:T(8,128)(2,1)}, bf16[10,64,768]{2,1,0:T(8,128)(2,1)}, u32[]{:S(2)}, u32[]{:S(2)}) %collective-permute-start.4) | collective-permute-done | bytes 983072 | tf_op jit(solution)/shard_map/ppermute | solution.py:107
  85.1 5.9 %prepare.1 = (bf16[512,256]{1,0:T(8,128)(2,1)S(1)}, bf16[256,512]{1,0:T(8,128)(2,1)S(1)}, f32[3,512,512]{2,1,0:T(8,128)S(1)}, f32[3,512,512]{2,1,0:T(8,128)S(1)}) custom-call(f32[6,32,32]{2,1,0:T(8,128)S(1)} %pad.4.table, f32[6,3]{1,0:T(8,128)S(1)} %slice.176.ends, s32[512,1]{1,0:T(8,128)S(1)} %copy.70.code_c, s32[512,1]{1,0:T(8,128)S(1)} %copy.71.seg_c, ...), custom_call_target="tpu_custom_call" | custom-call | flops 6000000000 | bytes 1 | tf_op jit(solution)/shard_map/prepare/pallas_call | solution.py:81
  91.6 12.9 %collective-permute-done.8.refs_7_ = bf16[10,64,768]{2,1,0:T(8,128)(2,1)S(1)} collective-permute-done((bf16[10,64,768]{2,1,0:T(8,128)(2,1)}, bf16[10,64,768]{2,1,0:T(8,128)(2,1)S(1)}, u32[]{:S(2)}, u32[]{:S(2)}) %collective-permute-start.8) | collective-permute-done | bytes 983072 | tf_op jit(solution)/shard_map/ppermute | solution.py:107
  105.5 2.8 deal.2
  108.3 2.7 attention.2
  111.0 1.7 collective-permute-done.9
  114.4 2.8 deal.3
  117.3 6.8 %collective-permute-done.10.theirs = bf16[256,768]{1,0:T(8,128)(2,1)S(1)} collective-permute-done((bf16[256,768]{1,0:T(8,128)(2,1)S(1)}, bf16[256,768]{1,0:T(8,128)(2,1)S(1)}, u32[]{:S(2)}, u32[]{:S(2)}) %collective-permute-start.10) | collective-permute-done | bytes 393248 | tf_op jit(solution)/shard_map/ppermute | solution.py:97
  124.6 1.7 collective-permute-done.11.c1
  126.3 2.2 hidden.2
  130.3 1.6 collective-permute-start.13
  131.9 9.6 %collective-permute-done.13.theirs = bf16[256,768]{1,0:T(8,128)(2,1)S(1)} collective-permute-done((bf16[256,768]{1,0:T(8,128)(2,1)S(1)}, bf16[256,768]{1,0:T(8,128)(2,1)S(1)}, u32[]{:S(2)}, u32[]{:S(2)}) %collective-permute-start.13) | collective-permute-done | bytes 393248 | tf_op jit(solution)/shard_map/ppermute | solution.py:97
  142.0 1.7 collective-permute-done.14.a1
  143.7 2.7 attention.3
  148.3 1.6 collective-permute-start.16
  149.9 9.6 %collective-permute-done.16.theirs = bf16[256,768]{1,0:T(8,128)(2,1)S(1)} collective-permute-done((bf16[256,768]{1,0:T(8,128)(2,1)S(1)}, bf16[256,768]{1,0:T(8,128)(2,1)S(1)}, u32[]{:S(2)}, u32[]{:S(2)}) %collective-permute-start.16) | collective-permute-done | bytes 393248 | tf_op jit(solution)/shard_map/ppermute | solution.py:97
  161.7 2.4 hidden.3
  164.1 2.1 hidden_back.2
  168.1 1.6 collective-permute-start.20
  169.7 3.1 hidden_weights.2
  172.8 6.5 %collective-permute-done.20.theirs = bf16[256,768]{1,0:T(8,128)(2,1)S(1)} collective-permute-done((bf16[256,768]{1,0:T(8,128)(2,1)S(1)}, bf16[256,768]{1,0:T(8,128)(2,1)S(1)}, u32[]{:S(2)}, u32[]{:S(2)}) %collective-permute-start.20) | collective-permute-done | bytes 393248 | tf_op jit(solution)/shard_map/ppermute | solution.py:97
  180.1 1.7 collective-permute-done.21.e1
  181.8 4.0 %attention_back.2 = (bf16[512,576]{1,0:T(8,128)(2,1)S(1)}, bf16[3,512,512]{2,1,0:T(8,128)(2,1)S(1)}, bf16[256,768]{1,0:T(8,128)(2,1)S(1)}, bf16[256,768]{1,0:T(8...) custom-call(bf16[256,768]{1,0:T(8,128)(2,1)S(1)} %get-tuple-element.233.e0, ...), custom_call_target="tpu_custom_call" | custom-call | bytes 1 | tf_op jit(solution)/shard_map/attention_back/pallas_call | solution.py:81
  186.0 1.6 collective-permute-done.22
  189.3 2.4 attention_weights.2
  191.7 7.3 %collective-permute-done.23.theirs = bf16[256,768]{1,0:T(8,128)(2,1)S(1)} collective-permute-done((bf16[256,768]{1,0:T(8,128)(2,1)S(1)}, bf16[256,768]{1,0:T(8,128)(2,1)S(1)}, u32[]{:S(2)}, u32[]{:S(2)}) %collective-permute-start.23) | collective-permute-done | bytes 393248 | tf_op jit(solution)/shard_map/ppermute | solution.py:97
  201.4 2.5 hidden_back.3
  204.3 1.6 collective-permute-start.25
  207.4 2.8 table.2
  210.2 3.1 hidden_weights.3
  213.3 6.6 %collective-permute-done.28.theirs = bf16[256,768]{1,0:T(8,128)(2,1)S(1)} collective-permute-done((bf16[256,768]{1,0:T(8,128)(2,1)S(1)}, bf16[256,768]{1,0:T(8,128)(2,1)S(1)}, u32[]{:S(2)}, u32[]{:S(2)}) %collective-permute-start.28) | collective-permute-done | bytes 393248 | tf_op jit(solution)/shard_map/ppermute | solution.py:97
  220.8 1.7 collective-permute-done.29.e1
  222.4 4.0 %attention_back.3 = (bf16[512,576]{1,0:T(8,128)(2,1)S(1)}, bf16[3,512,512]{2,1,0:T(8,128)(2,1)S(1)}, bf16[256,768]{1,0:T(8,128)(2,1)S(1)}, bf16[256,768]{1,0:T(8...) custom-call(bf16[256,768]{1,0:T(8,128)(2,1)S(1)} %get-tuple-element.292.e0, ...), custom_call_target="tpu_custom_call" | custom-call | bytes 1 | tf_op jit(solution)/shard_map/attention_back/pallas_call | solution.py:81
  226.5 2.4 attention_weights.3
  228.8 1.8 collective-permute-start.32
  234.0 8.3 %collective-permute-done.32 = bf16[5,64,768]{2,1,0:T(8,128)(2,1)S(1)} collective-permute-done((bf16[5,64,768]{2,1,0:T(8,128)(2,1)}, bf16[5,64,768]{2,1,0:T(8,128)(2,1)S(1)}, u32[]{:S(2)}, u32[]{:S(2)}) %collective-permute-start.32) | collective-permute-done | bytes 491552 | tf_op jit(solution)/shard_map/ppermute | solution.py:107
  242.4 1.7 collective-permute-start.33
  249.1 3.0 table.3
  252.1 3.0 collective-permute-done.33
  255.1 1.7 collective-permute-start.36
  257.0 2.7 collective-permute-done.36
  259.7 1.7 collective-permute-start.37
  261.4 2.1 add_convert_fusion.2
  263.5 4.7 %collective-permute-done.38 = bf16[5,64,768]{2,1,0:T(8,128)(2,1)S(1)} collective-permute-done((bf16[5,64,768]{2,1,0:T(8,128)(2,1)}, bf16[5,64,768]{2,1,0:T(8,128)(2,1)S(1)}, u32[]{:S(2)}, u32[]{:S(2)}) %collective-permute-start.38) | collective-permute-done | bytes 491552 | tf_op jit(solution)/shard_map/ppermute | solution.py:107
  268.6 2.8 collective-permute-start.44
  271.4 7.5 %collective-permute-done.44 = f32[192,128]{1,0:T(8,128)S(1)} collective-permute-done((f32[192,128]{1,0:T(8,128)S(1)}, f32[192,128]{1,0:T(8,128)S(1)}, u32[]{:S(2)}, u32[]{:S(2)}) %collective-permute-start.44) | collective-permute-done | bytes 98336 | tf_op jit(solution)/shard_map/ppermute | solution.py:918
  279.0 2.2 collective-permute-done.39
  281.1 2.8 add_convert_fusion.1
  287.0 1.7 collective-permute-start.42
  289.8 17.9 %collective-permute-done.40 = bf16[10,64,768]{2,1,0:T(8,128)(2,1)} collective-permute-done((bf16[10,64,768]{2,1,0:T(8,128)(2,1)}, bf16[10,64,768]{2,1,0:T(8,128)(2,1)}, u32[]{:S(2)}, u32[]{:S(2)}) %collective-permute-start.40) | collective-permute-done | bytes 983072 | tf_op jit(solution)/shard_map/ppermute | solution.py:107
  310.0 2.4 add_convert_fusion
  313.8 14.8 %collective-permute-done.42 = bf16[10,64,768]{2,1,0:T(8,128)(2,1)} collective-permute-done((bf16[10,64,768]{2,1,0:T(8,128)(2,1)}, bf16[10,64,768]{2,1,0:T(8,128)(2,1)}, u32[]{:S(2)}, u32[]{:S(2)}) %collective-permute-start.42) | collective-permute-done | bytes 983072 | tf_op jit(solution)/shard_map/ppermute | solution.py:107
  328.6 1.9 convert_add_fusion.base
  330.4 2.8 fetch.1
  333.2 15.3 %collective-permute-done.43.come = bf16[10,64,768]{2,1,0:T(8,128)(2,1)S(1)} collective-permute-done((bf16[10,64,768]{2,1,0:T(8,128)(2,1)}, bf16[10,64,768]{2,1,0:T(8,128)(2,1)S(1)}, u32[]{:S(2)}, u32[]{:S(2)}) %collective-permute-start.43) | collective-permute-done | bytes 983072 | tf_op jit(solution)/shard_map/ppermute | solution.py:107
  348.5 3.7 %update.1 = (f32[10,64,768]{2,1,0:T(8,128)}, f32[10,64,768]{2,1,0:T(8,128)}, f32[10,64,768]{2,1,0:T(8,128)}, f32[10,64,768]{2,1,0:T(8,128)}) custom-call(s32[10]{0:T(128)S(1)} %convert_element_type.179.used, f32[10,64,768]{2,1,0:T(8,128)S(1)} %convert_add_fusion.base, bf16[10,64,768]{2,1,0:T(8,128)(2,1)S(1)} %collective-permute-done.43.come, ...), custom_call_target="tpu_custom_call" | custom-call | flops 3000000000 | bytes 1 | tf_op jit(solution)/shard_map/update/pallas_call | solution.py:81
  (200 shorter events, 43.2 us)
Async XLA Ops:
  0.6 63.0 %copy-start.19 = (s32[8,10]{0,1:T(8,128)S(1)}, s32[8,10]{0,1:T(8,128)}, u32[]{:S(2)}) copy-start(s32[8,10]{0,1:T(8,128)} %constant.120.clone) | copy-start | bytes 964
  0.7 6.4 %copy-start.2 = (bf16[128,768]{1,0:T(8,128)(2,1)S(1)}, bf16[128,768]{1,0:T(8,128)(2,1)}, u32[]{:S(2)}) copy-start(bf16[128,768]{1,0:T(8,128)(2,1)} %tokens.1) | copy-start | bytes 589828
  0.7 8.0 %copy-start.20 = (s32[1,6]{1,0:T(1,128)S(1)}, s32[1,6]{1,0:T(1,128)}, u32[]{:S(2)}) copy-start(s32[1,6]{1,0:T(1,128)} %param.18) | copy-start | bytes 76
  0.7 39.5 %copy-start.21 = (s32[72]{0:T(128)S(1)}, s32[72]{0:T(128)}, u32[]{:S(2)}) copy-start(s32[72]{0:T(128)} %param.19) | copy-start | bytes 868
  0.7 62.5 %copy-start.14 = (f32[2,1,3348]{2,1,0:T(1,128)S(1)}, f32[2,1,3348]{2,1,0:T(1,128)}, u32[]{:S(2)}) copy-start(f32[2,1,3348]{2,1,0:T(1,128)} %param.26) | copy-start | bytes 80356
  2.4 88.6 %copy-start.6 = (bf16[10,64,768]{2,1,0:T(8,128)(2,1)}, bf16[10,64,768]{2,1,0:T(8,128)(2,1)S(1)}, u32[]{:S(2)}) copy-start(bf16[10,64,768]{2,1,0:T(8,128)(2,1)S(1)} %convert_element_type.148.refs_0_) | copy-start | bytes 2949124
  2.5 35.0 %collective-permute-start.2 = (bf16[10,64,768]{2,1,0:T(8,128)(2,1)S(1)}, bf16[10,64,768]{2,1,0:T(8,128)(2,1)S(1)}, u32[]{:S(2)}, u32[]{:S(2)}) collective-permute-start(bf16[10,64,768]{2,1,0:T(8,128)(2,1)S(1)} %convert_element_type.148.refs_0_), channel_id=1, source_target_pairs={{0,8},{8,0},{16,24},{24,16},{1,9},{9,1},{17,25},{25,17},{2,10},{10... | collective-permute-start | bytes 2949128 | tf_op jit(solution)/shard_map/ppermute | solution.py:107
  5.6 31.9 %collective-permute-start.5 = (bf16[10,64,768]{2,1,0:T(8,128)(2,1)S(1)}, bf16[10,64,768]{2,1,0:T(8,128)(2,1)}, u32[]{:S(2)}, u32[]{:S(2)}) collective-permute-start(bf16[10,64,768]{2,1,0:T(8,128)(2,1)S(1)} %convert_element_type.148.refs_0_), channel_id=1, source_target_pairs={{0,4},{4,0},{1,5},{5,1},{2,6},{6,2},{3,7},{7,3},{8,12},{12,8},{9,1... | collective-permute-start | bytes 2949128 | tf_op jit(solution)/shard_map/ppermute | solution.py:107
  7.1 10.4 %collective-permute-start = (bf16[256,768]{1,0:T(8,128)(2,1)S(1)}, bf16[256,768]{1,0:T(8,128)(2,1)S(1)}, u32[]{:S(2)}, u32[]{:S(2)}) collective-permute-start(bf16[256,768]{1,0:T(8,128)(2,1)S(1)} %pad_maximum_fusion), channel_id=1, source_target_pairs={{0,2},{2,0},{1,3},{3,1},{4,6},{6,4},{5,7},{7,5},{8,10},{10,8},{9,1... | collective-permute-start | bytes 1179656 | tf_op jit(solution)/shard_map/ppermute | solution.py:97
  17.4 44.2 %collective-permute-start.3 = (bf16[10,64,768]{2,1,0:T(8,128)(2,1)S(1)}, bf16[10,64,768]{2,1,0:T(8,128)(2,1)}, u32[]{:S(2)}, u32[]{:S(2)}) collective-permute-start(bf16[10,64,768]{2,1,0:T(8,128)(2,1)S(1)} %convert_element_type.148.refs_0_), channel_id=1, source_target_pairs={{0,16},{8,24},{16,0},{24,8},{1,17},{9,25},{17,1},{25,9},{2,18},{10... | collective-permute-start | bytes 2949128 | tf_op jit(solution)/shard_map/ppermute | solution.py:107
  37.5 25.4 %copy-start.9 = (bf16[10,64,768]{2,1,0:T(8,128)(2,1)}, bf16[10,64,768]{2,1,0:T(8,128)(2,1)S(1)}, u32[]{:S(2)}) copy-start(bf16[10,64,768]{2,1,0:T(8,128)(2,1)S(1)} %collective-permute-done.2.refs_1_) | copy-start | bytes 2949124
  37.5 24.2 %collective-permute-start.6 = (bf16[10,64,768]{2,1,0:T(8,128)(2,1)S(1)}, bf16[10,64,768]{2,1,0:T(8,128)(2,1)S(1)}, u32[]{:S(2)}, u32[]{:S(2)}) collective-permute-start(bf16[10,64,768]{2,1,0:T(8,128)(2,1)S(1)} %collective-permute-done.2.refs_1_), channel_id=1, source_target_pairs={{0,4},{4,0},{1,5},{5,1},{2,6},{6,2},{3,7},{7,3},{8,12},{12,8},{9,1... | collective-permute-start | bytes 2949128 | tf_op jit(solution)/shard_map/ppermute | solution.py:107
  61.7 21.6 %collective-permute-start.4 = (bf16[10,64,768]{2,1,0:T(8,128)(2,1)}, bf16[10,64,768]{2,1,0:T(8,128)(2,1)}, u32[]{:S(2)}, u32[]{:S(2)}) collective-permute-start(bf16[10,64,768]{2,1,0:T(8,128)(2,1)} %collective-permute-done.3.refs_2_), channel_id=1, source_target_pairs={{0,8},{8,0},{16,24},{24,16},{1,9},{9,1},{17,25},{25,17},{2,10},{10... | collective-permute-start | bytes 2949128 | tf_op jit(solution)/shard_map/ppermute | solution.py:107
  61.7 21.9 %collective-permute-start.7 = (bf16[10,64,768]{2,1,0:T(8,128)(2,1)}, bf16[10,64,768]{2,1,0:T(8,128)(2,1)}, u32[]{:S(2)}, u32[]{:S(2)}) collective-permute-start(bf16[10,64,768]{2,1,0:T(8,128)(2,1)} %collective-permute-done.3.refs_2_), channel_id=1, source_target_pairs={{0,4},{4,0},{1,5},{5,1},{2,6},{6,2},{3,7},{7,3},{8,12},{12,8},{9,1... | collective-permute-start | bytes 2949128 | tf_op jit(solution)/shard_map/ppermute | solution.py:107
  83.6 21.0 %collective-permute-start.8 = (bf16[10,64,768]{2,1,0:T(8,128)(2,1)}, bf16[10,64,768]{2,1,0:T(8,128)(2,1)S(1)}, u32[]{:S(2)}, u32[]{:S(2)}) collective-permute-start(bf16[10,64,768]{2,1,0:T(8,128)(2,1)} %collective-permute-done.4.refs_3_), channel_id=1, source_target_pairs={{0,4},{4,0},{1,5},{5,1},{2,6},{6,2},{3,7},{7,3},{8,12},{12,8},{9,1... | collective-permute-start | bytes 2949128 | tf_op jit(solution)/shard_map/ppermute | solution.py:107
  91.5 16.8 %collective-permute-start.1 = (bf16[256,768]{1,0:T(8,128)(2,1)S(1)}, bf16[256,768]{1,0:T(8,128)(2,1)S(1)}, u32[]{:S(2)}, u32[]{:S(2)}) collective-permute-start(bf16[256,768]{1,0:T(8,128)(2,1)S(1)} %get-tuple-element.186.a0), channel_id=1, source_target_pairs={{0,1},{1,0},{2,3},{3,2},{4,5},{5,4},{6,7},{7,6},{8,9},{9,8},{10,11... | collective-permute-start | bytes 1179656 | tf_op jit(solution)/shard_map/ppermute | solution.py:97
  111.0 1.8 collective-permute-start.9
  112.8 11.2 %collective-permute-start.10 = (bf16[256,768]{1,0:T(8,128)(2,1)S(1)}, bf16[256,768]{1,0:T(8,128)(2,1)S(1)}, u32[]{:S(2)}, u32[]{:S(2)}) collective-permute-start(bf16[256,768]{1,0:T(8,128)(2,1)S(1)} %add_convert_fusion.11.ours), channel_id=1, source_target_pairs={{0,2},{2,0},{1,3},{3,1},{4,6},{6,4},{5,7},{7,5},{8,10},{10,8},{9,1... | collective-permute-start | bytes 1179656 | tf_op jit(solution)/shard_map/ppermute | solution.py:97
  124.5 1.8 collective-permute-start.11
  128.4 1.8 collective-permute-start.12
  130.3 11.2 %collective-permute-start.13 = (bf16[256,768]{1,0:T(8,128)(2,1)S(1)}, bf16[256,768]{1,0:T(8,128)(2,1)S(1)}, u32[]{:S(2)}, u32[]{:S(2)}) collective-permute-start(bf16[256,768]{1,0:T(8,128)(2,1)S(1)} %add_convert_fusion.10.ours), channel_id=1, source_target_pairs={{0,2},{2,0},{1,3},{3,1},{4,6},{6,4},{5,7},{7,5},{8,10},{10,8},{9,1... | collective-permute-start | bytes 1179656 | tf_op jit(solution)/shard_map/ppermute | solution.py:97
  142.0 1.8 collective-permute-start.14
  146.4 1.8 collective-permute-start.15
  148.3 11.2 %collective-permute-start.16 = (bf16[256,768]{1,0:T(8,128)(2,1)S(1)}, bf16[256,768]{1,0:T(8,128)(2,1)S(1)}, u32[]{:S(2)}, u32[]{:S(2)}) collective-permute-start(bf16[256,768]{1,0:T(8,128)(2,1)S(1)} %add_convert_fusion.9.ours), channel_id=1, source_target_pairs={{0,2},{2,0},{1,3},{3,1},{4,6},{6,4},{5,7},{7,5},{8,10},{10,8},{9,1... | collective-permute-start | bytes 1179656 | tf_op jit(solution)/shard_map/ppermute | solution.py:97
  159.9 1.8 collective-permute-start.17
  160.0 4.1 %collective-permute-start.18 = (bf16[256,768]{1,0:T(8,128)(2,1)S(1)}, bf16[256,768]{1,0:T(8,128)(2,1)S(1)}, u32[]{:S(2)}, u32[]{:S(2)}) collective-permute-start(bf16[256,768]{1,0:T(8,128)(2,1)S(1)} %get-tuple-element.217.e0), channel_id=1, source_target_pairs={{0,1},{1,0},{2,3},{3,2},{4,5},{5,4},{6,7},{7,6},{8,9},{9,8},{10,11... | collective-permute-start | bytes 1179656 | tf_op jit(solution)/shard_map/ppermute | solution.py:97
  166.2 1.8 collective-permute-start.19
  168.1 11.2 %collective-permute-start.20 = (bf16[256,768]{1,0:T(8,128)(2,1)S(1)}, bf16[256,768]{1,0:T(8,128)(2,1)S(1)}, u32[]{:S(2)}, u32[]{:S(2)}) collective-permute-start(bf16[256,768]{1,0:T(8,128)(2,1)S(1)} %add_convert_fusion.8.ours), channel_id=1, source_target_pairs={{0,2},{2,0},{1,3},{3,1},{4,6},{6,4},{5,7},{7,5},{8,10},{10,8},{9,1... | collective-permute-start | bytes 1179656 | tf_op jit(solution)/shard_map/ppermute | solution.py:97
  180.0 1.8 collective-permute-start.21
  185.8 1.8 collective-permute-start.22
  187.7 11.2 %collective-permute-start.23 = (bf16[256,768]{1,0:T(8,128)(2,1)S(1)}, bf16[256,768]{1,0:T(8,128)(2,1)S(1)}, u32[]{:S(2)}, u32[]{:S(2)}) collective-permute-start(bf16[256,768]{1,0:T(8,128)(2,1)S(1)} %add_convert_fusion.7.ours), channel_id=1, source_target_pairs={{0,2},{2,0},{1,3},{3,1},{4,6},{6,4},{5,7},{7,5},{8,10},{10,8},{9,1... | collective-permute-start | bytes 1179656 | tf_op jit(solution)/shard_map/ppermute | solution.py:97
  199.6 1.8 collective-permute-start.26
  199.7 4.4 %collective-permute-start.24 = (bf16[256,768]{1,0:T(8,128)(2,1)S(1)}, bf16[256,768]{1,0:T(8,128)(2,1)S(1)}, u32[]{:S(2)}, u32[]{:S(2)}) collective-permute-start(bf16[256,768]{1,0:T(8,128)(2,1)S(1)} %get-tuple-element.262), channel_id=1, source_target_pairs={{0,1},{1,0},{2,3},{3,2},{4,5},{5,4},{6,7},{7,6},{8,9},{9,8},{10,11... | collective-permute-start | bytes 1179656 | tf_op jit(solution)/shard_map/ppermute | solution.py:97
  203.9 2.0 collective-permute-start.27
  204.3 9.0 %collective-permute-start.25 = (bf16[128,768]{1,0:T(8,128)(2,1)S(1)}, bf16[128,768]{1,0:T(8,128)(2,1)S(1)}, u32[]{:S(2)}, u32[]{:S(2)}) collective-permute-start(bf16[128,768]{1,0:T(8,128)(2,1)S(1)} %slice.181), channel_id=1, source_target_pairs={{0,2},{2,0},{1,3},{3,1},{4,6},{6,4},{5,7},{7,5},{8,10},{10,8},{9,1... | collective-permute-start | bytes 589832 | tf_op jit(solution)/shard_map/ppermute | solution.py:97
  206.0 14.0 %collective-permute-start.28 = (bf16[256,768]{1,0:T(8,128)(2,1)S(1)}, bf16[256,768]{1,0:T(8,128)(2,1)S(1)}, u32[]{:S(2)}, u32[]{:S(2)}) collective-permute-start(bf16[256,768]{1,0:T(8,128)(2,1)S(1)} %add_convert_fusion.5.ours), channel_id=1, source_target_pairs={{0,2},{2,0},{1,3},{3,1},{4,6},{6,4},{5,7},{7,5},{8,10},{10,8},{9,1... | collective-permute-start | bytes 1179656 | tf_op jit(solution)/shard_map/ppermute | solution.py:97
  220.7 1.8 collective-permute-start.29
  228.8 15.2 %copy-start.8 = (bf16[5,64,768]{2,1,0:T(8,128)(2,1)S(1)}, bf16[5,64,768]{2,1,0:T(8,128)(2,1)}, u32[]{:S(2)}) copy-start(bf16[5,64,768]{2,1,0:T(8,128)(2,1)} %get-tuple-element.315) | copy-start | bytes 1474564
  228.8 13.5 %collective-permute-start.32 = (bf16[5,64,768]{2,1,0:T(8,128)(2,1)}, bf16[5,64,768]{2,1,0:T(8,128)(2,1)S(1)}, u32[]{:S(2)}, u32[]{:S(2)}) collective-permute-start(bf16[5,64,768]{2,1,0:T(8,128)(2,1)} %get-tuple-element.316), channel_id=1, source_target_pairs={{0,4},{4,0},{1,5},{5,1},{2,6},{6,2},{3,7},{7,3},{8,12},{12,8},{9,1... | collective-permute-start | bytes 1474568 | tf_op jit(solution)/shard_map/ppermute | solution.py:107
  230.6 1.7 collective-permute-start.30
  232.5 12.5 %collective-permute-start.31 = (bf16[128,768]{1,0:T(8,128)(2,1)S(1)}, bf16[128,768]{1,0:T(8,128)(2,1)S(1)}, u32[]{:S(2)}, u32[]{:S(2)}) collective-permute-start(bf16[128,768]{1,0:T(8,128)(2,1)S(1)} %slice.182), channel_id=1, source_target_pairs={{0,2},{2,0},{1,3},{3,1},{4,6},{6,4},{5,7},{7,5},{8,10},{10,8},{9,1... | collective-permute-start | bytes 589832 | tf_op jit(solution)/shard_map/ppermute | solution.py:97
  242.4 12.7 %collective-permute-start.33 = (bf16[5,64,768]{2,1,0:T(8,128)(2,1)}, bf16[5,64,768]{2,1,0:T(8,128)(2,1)}, u32[]{:S(2)}, u32[]{:S(2)}) collective-permute-start(bf16[5,64,768]{2,1,0:T(8,128)(2,1)} %get-tuple-element.325), channel_id=1, source_target_pairs={{0,4},{4,0},{1,5},{5,1},{2,6},{6,2},{3,7},{7,3},{8,12},{12,8},{9,1... | collective-permute-start | bytes 1474568 | tf_op jit(solution)/shard_map/ppermute | solution.py:107
  246.2 1.3 collective-permute-start.34
  247.5 4.5 %collective-permute-start.35 = (f32[16,768]{1,0:T(8,128)S(1)}, f32[16,768]{1,0:T(8,128)S(1)}, u32[]{:S(2)}, u32[]{:S(2)}) collective-permute-start(f32[16,768]{1,0:T(8,128)S(1)} %add.245), channel_id=1, source_target_pairs={{0,2},{2,0},{1,3},{3,1},{4,6},{6,4},{5,7},{7,5},{8,10},{10,8},{9,1... | collective-permute-start | bytes 147464 | tf_op jit(solution)/shard_map/ppermute | solution.py:167
  252.0 29.1 %copy-start.5 = (bf16[10,64,768]{2,1,0:T(8,128)(2,1)S(1)}, bf16[10,64,768]{2,1,0:T(8,128)(2,1)}, u32[]{:S(2)}) copy-start(bf16[10,64,768]{2,1,0:T(8,128)(2,1)} %get-tuple-element.326) | copy-start | bytes 2949124
  255.1 4.6 %collective-permute-start.36 = (f32[192,128]{1,0:T(8,128)S(1)}, f32[192,128]{1,0:T(8,128)S(1)}, u32[]{:S(2)}, u32[]{:S(2)}) collective-permute-start(f32[192,128]{1,0:T(8,128)S(1)} %pad_maximum_fusion.1), channel_id=1, source_target_pairs={{0,4},{4,0},{1,5},{5,1},{2,6},{6,2},{3,7},{7,3},{8,12},{12,8},{9,1... | collective-permute-start | bytes 294920 | tf_op jit(solution)/shard_map/ppermute | solution.py:107
  256.8 11.4 %collective-permute-start.38 = (bf16[5,64,768]{2,1,0:T(8,128)(2,1)}, bf16[5,64,768]{2,1,0:T(8,128)(2,1)S(1)}, u32[]{:S(2)}, u32[]{:S(2)}) collective-permute-start(bf16[5,64,768]{2,1,0:T(8,128)(2,1)} %add_convert_fusion.3), channel_id=1, source_target_pairs={{0,8},{8,0},{16,24},{24,16},{1,9},{9,1},{17,25},{25,17},{2,10},{10... | collective-permute-start | bytes 1474568 | tf_op jit(solution)/shard_map/ppermute | solution.py:107
  259.7 21.4 %collective-permute-start.37 = (bf16[10,64,768]{2,1,0:T(8,128)(2,1)}, bf16[10,64,768]{2,1,0:T(8,128)(2,1)}, u32[]{:S(2)}, u32[]{:S(2)}) collective-permute-start(bf16[10,64,768]{2,1,0:T(8,128)(2,1)} %get-tuple-element.336), channel_id=1, source_target_pairs={{0,4},{4,0},{1,5},{5,1},{2,6},{6,2},{3,7},{7,3},{8,12},{12,8},{9,1... | collective-permute-start | bytes 2949128 | tf_op jit(solution)/shard_map/ppermute | solution.py:107
  268.3 10.6 %copy-start.12 = (bf16[5,64,768]{2,1,0:T(8,128)(2,1)}, bf16[5,64,768]{2,1,0:T(8,128)(2,1)S(1)}, u32[]{:S(2)}) copy-start(bf16[5,64,768]{2,1,0:T(8,128)(2,1)S(1)} %collective-permute-done.38) | copy-start | bytes 1474564
  268.3 12.8 %collective-permute-start.39 = (bf16[5,64,768]{2,1,0:T(8,128)(2,1)}, bf16[5,64,768]{2,1,0:T(8,128)(2,1)}, u32[]{:S(2)}, u32[]{:S(2)}) collective-permute-start(bf16[5,64,768]{2,1,0:T(8,128)(2,1)} %add_convert_fusion.2), channel_id=1, source_target_pairs={{0,8},{8,0},{16,24},{24,16},{1,9},{9,1},{17,25},{25,17},{2,10},{10... | collective-permute-start | bytes 1474568 | tf_op jit(solution)/shard_map/ppermute | solution.py:107
  268.6 10.3 %collective-permute-start.44 = (f32[192,128]{1,0:T(8,128)S(1)}, f32[192,128]{1,0:T(8,128)S(1)}, u32[]{:S(2)}, u32[]{:S(2)}) collective-permute-start(f32[192,128]{1,0:T(8,128)S(1)} %fusion.15), channel_id=1, source_target_pairs={{0,16},{8,24},{16,0},{24,8},{1,17},{9,25},{17,1},{25,9},{2,18},{10... | collective-permute-start | bytes 294920 | tf_op jit(solution)/shard_map/ppermute | solution.py:918
  278.9 28.8 %copy-start.7 = (bf16[10,64,768]{2,1,0:T(8,128)(2,1)S(1)}, bf16[10,64,768]{2,1,0:T(8,128)(2,1)}, u32[]{:S(2)}) copy-start(bf16[10,64,768]{2,1,0:T(8,128)(2,1)} %get-tuple-element.343) | copy-start | bytes 2949124
  278.9 30.2 %copy-start.17 = (f32[2,1,3348]{2,1,0:T(1,128)S(1)}, f32[2,1,3348]{2,1,0:T(1,128)}, u32[]{:S(2)}) copy-start(f32[2,1,3348]{2,1,0:T(1,128)} %param.28) | copy-start | bytes 80356
  278.9 30.2 %copy-start.18 = (f32[2,1,3348]{2,1,0:T(1,128)S(1)}, f32[2,1,3348]{2,1,0:T(1,128)}, u32[]{:S(2)}) copy-start(f32[2,1,3348]{2,1,0:T(1,128)} %param.27) | copy-start | bytes 80356
  278.9 31.1 %copy-start.4 = (bf16[10,64,768]{2,1,0:T(8,128)(2,1)S(1)}, bf16[10,64,768]{2,1,0:T(8,128)(2,1)}, u32[]{:S(2)}) copy-start(bf16[10,64,768]{2,1,0:T(8,128)(2,1)} %get-tuple-element.338) | copy-start | bytes 2949124
  283.9 4.8 %collective-permute-start.45 = (f32[192,128]{1,0:T(8,128)S(1)}, f32[192,128]{1,0:T(8,128)S(1)}, u32[]{:S(2)}, u32[]{:S(2)}) collective-permute-start(f32[192,128]{1,0:T(8,128)S(1)} %add.253), channel_id=1, source_target_pairs={{0,8},{8,0},{16,24},{24,16},{1,9},{9,1},{17,25},{25,17},{2,10},{10... | collective-permute-start | bytes 294920 | tf_op jit(solution)/shard_map/ppermute | solution.py:918
  285.5 22.2 %collective-permute-start.40 = (bf16[10,64,768]{2,1,0:T(8,128)(2,1)}, bf16[10,64,768]{2,1,0:T(8,128)(2,1)}, u32[]{:S(2)}, u32[]{:S(2)}) collective-permute-start(bf16[10,64,768]{2,1,0:T(8,128)(2,1)} %get-tuple-element.340), channel_id=1, source_target_pairs={{0,4},{4,0},{1,5},{5,1},{2,6},{6,2},{3,7},{7,3},{8,12},{12,8},{9,1... | collective-permute-start | bytes 2949128 | tf_op jit(solution)/shard_map/ppermute | solution.py:107
  287.0 41.6 %collective-permute-start.42 = (bf16[10,64,768]{2,1,0:T(8,128)(2,1)}, bf16[10,64,768]{2,1,0:T(8,128)(2,1)}, u32[]{:S(2)}, u32[]{:S(2)}) collective-permute-start(bf16[10,64,768]{2,1,0:T(8,128)(2,1)} %add_convert_fusion.1), channel_id=1, source_target_pairs={{0,16},{8,24},{16,0},{24,8},{1,17},{9,25},{17,1},{25,9},{2,18},{10... | collective-permute-start | bytes 2949128 | tf_op jit(solution)/shard_map/ppermute | solution.py:107
  289.3 23.8 %copy-start.15 = (f32[2,8,768]{2,1,0:T(8,128)S(1)}, f32[2,8,768]{2,1,0:T(8,128)}, u32[]{:S(2)}) copy-start(f32[2,8,768]{2,1,0:T(8,128)} %param.25) | copy-start | bytes 147460
  289.3 23.8 %copy-start.16 = (f32[2,8,768]{2,1,0:T(8,128)S(1)}, f32[2,8,768]{2,1,0:T(8,128)}, u32[]{:S(2)}) copy-start(f32[2,8,768]{2,1,0:T(8,128)} %param.24) | copy-start | bytes 147460
  289.8 38.8 %copy-start.3 = (bf16[10,64,768]{2,1,0:T(8,128)(2,1)S(1)}, bf16[10,64,768]{2,1,0:T(8,128)(2,1)}, u32[]{:S(2)}) copy-start(bf16[10,64,768]{2,1,0:T(8,128)(2,1)} %get-tuple-element.341) | copy-start | bytes 2949124
  307.7 20.8 %collective-permute-start.41 = (bf16[10,64,768]{2,1,0:T(8,128)(2,1)S(1)}, bf16[10,64,768]{2,1,0:T(8,128)(2,1)}, u32[]{:S(2)}, u32[]{:S(2)}) collective-permute-start(bf16[10,64,768]{2,1,0:T(8,128)(2,1)S(1)} %copy-done.7), channel_id=1, source_target_pairs={{0,4},{4,0},{1,5},{5,1},{2,6},{6,2},{3,7},{7,3},{8,12},{12,8},{9,1... | collective-permute-start | bytes 2949128 | tf_op jit(solution)/shard_map/ppermute | solution.py:107
  312.4 36.1 %collective-permute-start.43 = (bf16[10,64,768]{2,1,0:T(8,128)(2,1)}, bf16[10,64,768]{2,1,0:T(8,128)(2,1)S(1)}, u32[]{:S(2)}, u32[]{:S(2)}) collective-permute-start(bf16[10,64,768]{2,1,0:T(8,128)(2,1)} %add_convert_fusion), channel_id=1, source_target_pairs={{0,8},{8,0},{16,24},{24,16},{1,9},{9,1},{17,25},{25,17},{2,10},{10... | collective-permute-start | bytes 2949128 | tf_op jit(solution)/shard_map/ppermute | solution.py:107
  313.1 17.3 %copy-start.13 = (f32[2,8,768]{2,1,0:T(8,128)}, f32[2,8,768]{2,1,0:T(8,128)S(1)}, u32[]{:S(2)}) copy-start(f32[2,8,768]{2,1,0:T(8,128)S(1)} %reshape.251) | copy-start | bytes 147460
  (4 other events, 14.5 us)

commit v3 on v2

--- a/solution.py
+++ b/solution.py
@@ -111,48 +111,44 @@
 SWAP = [(0, 1), (1, 0)]
 
 
-def low_bit(s):
-    return s & -s
-
-
-def gather_stores(store, near):
+def ring(nz):
+    return list(range(0, nz, 2)) + list(range(1, nz, 2))[::-1]
+
+
+def ring_step(nz, back):
+    places = ring(nz)
+    pairs = [(places[i], places[(i + 1) % nz]) for i in range(nz)]
+    return [(b, a) for a, b in pairs] if back else pairs
+
+
+def gather_stores(store):
     nz = lax.axis_size("z")
-    along_z, along_x = Line(2), Line()
+    along_z, along_x = Line(), Line()
     blocks = [store]
-    for s in range(1, nz):
-        perm = [(i, i ^ low_bit(s)) for i in range(nz)]
-        sent = blocks[s - low_bit(s)]
-        blocks.append(along_z.send(after(sent, near) if s == 2 else sent, "z", perm))
+    for _ in range(1, nz):
+        blocks.append(along_z.send(blocks[-1], "z", ring_step(nz, False)))
     return blocks + [along_x.send(v, "x", SWAP) for v in blocks]
 
 
 class ScatterSums:
-    def __init__(self, ours, theirs):
-        self.ours, self.theirs, self.count = ours, theirs, len(ours)
+    def __init__(self, grads):
+        self.grads, self.count = grads, len(grads) // 2
         self.along_z, self.along_x = Line(), Line()
-        self.come = [[] for _ in ours]
-        self.parts, self.all_parts = [], []
+        self.come = None
+        self.parts = []
 
     def step(self):
         s = self.count - 1 - len(self.parts)
-        sent = []
-        last = self.parts[-1:]
-        for ours, theirs in zip(self.ours[s], self.theirs[s]):
-            got = self.along_x.send(theirs, "x", SWAP)
-            if last:
-                ours = after(ours, *last)
-            come = self.come[s] if s else self.come[s][:-1]
-            part = sum(v.astype(f32) for v in [ours, got] + come)
-            if s:
-                part = part.astype(bf16)
-                perm = [(i, i ^ low_bit(s)) for i in range(self.count)]
-                if s == 1:
-                    self.along_z.ahead = 2
-                sent.append(self.along_z.send(part, "z", perm))
-            last = [part]
-            self.all_parts.append(part)
+        got = self.along_x.send(self.grads[self.count + s], "x", SWAP)
+        ours = self.grads[s]
+        if self.parts:
+            ours = after(ours, self.parts[-1])
+        part = ours.astype(f32) + got.astype(f32)
         if s:
-            self.come[s - low_bit(s)].append(jnp.concatenate(sent, axis=0) if len(sent) > 1 else sent[0])
+            if self.come is not None:
+                part = part + self.come.astype(f32)
+            part = part.astype(bf16)
+            self.come = self.along_z.send(part, "z", ring_step(self.count, True))
         self.parts.append(part)
 
 
@@ -417,6 +413,39 @@
     d_b1[...] = jnp.concatenate(sums, axis=1)
 
 
+def hidden_turn_kernel(
+    c0, c1, e0, e1, b1, w1, w2, u, dz, c0_saved, c1_saved, e0_saved, e1_saved, d_b1, keep, send
+):
+    for source, saved in ((c0, c0_saved), (c1, c1_saved), (e0, e0_saved), (e1, e1_saved)):
+        saved[...] = source[...]
+    rows = c0.shape[0]
+    cols = w1.shape[0] // 2
+    sums = [None, None]
+    for i, (c, e, out) in ((1, (c1, e1, send)), (0, (c0, e0, keep))):
+        span = pl.ds(i * rows, rows)
+        total = None
+        for j in range(2):
+            lanes = slice(j * cols, (j + 1) * cols)
+            z = matmul_nt(c[...], w1[lanes, :]) + b1[:, lanes]
+            value, grade = gelu_parts(z)
+            u[span, lanes] = value.astype(bf16)
+            grad = matmul_nt(e[...], w2[lanes, :]) * grade
+            line = jnp.sum(grad, axis=0, keepdims=True)
+            sums[j] = line if sums[j] is None else sums[j] + line
+            grad = grad.astype(bf16)
+            dz[span, lanes] = grad
+            part = matmul(grad, w1[lanes, :])
+            total = part if total is None else total + part
+        out[...] = total.astype(bf16)
+    d_b1[...] = jnp.concatenate(sums, axis=1)
+
+
+def project_kernel(u, w2, keep, send):
+    rows = keep.shape[0]
+    keep[...] = matmul(u[:rows, :], w2[...]).astype(bf16)
+    send[...] = matmul(u[rows:, :], w2[...]).astype(bf16)
+
+
 def put_blocks(blocks, near_slot, first, outs, capacity, semaphore):
     for u in range(blocks.shape[0]):
         place = near_slot[first + u]
@@ -589,11 +618,16 @@
 
     slots = unit_slots(owners, capacity)
     both = swap(jnp.concatenate([tokens_in, out_grad], axis=0), "y")
-    blocks = gather_stores(weight_store.astype(bf16), both)
+    blocks = gather_stores(weight_store.astype(bf16))
 
     group = hidden // HEAD
     near_x = (my_x + jnp.arange(2, dtype=jnp.int32)) % 2
-    near_z = my_z ^ jnp.arange(nz, dtype=jnp.int32)
+    places = jnp.asarray(ring(nz), jnp.int32)
+    my_place = jnp.sum(jnp.where(places == my_z, jnp.arange(nz, dtype=jnp.int32), 0))
+    near_place = (my_place - jnp.arange(nz, dtype=jnp.int32)) % nz
+    near_z = jnp.sum(
+        jnp.where(near_place[:, None] == jnp.arange(nz, dtype=jnp.int32)[None, :], places[None, :], 0), axis=1
+    )
     owner_of = (near_z[None, :] * 2 + near_x[:, None]).reshape(-1)
     unit_ids = jnp.arange(slots.shape[0], dtype=jnp.int32)
     near_slots = owner_of[:, None] * capacity + jnp.arange(capacity, dtype=jnp.int32)[None, :]
@@ -601,18 +635,8 @@
     near_unit = jnp.sum(jnp.where(near_match, unit_ids, 0), axis=2)
     near_unit = jnp.where(jnp.any(near_match, axis=2), near_unit, slots.shape[0])
     in_pieces = owners_all == 8
-    sizes = [owners_all * capacity]
-    near_ids = [[p * capacity + k for k in range(capacity)] for p in range(owners_all)]
-    if in_pieces:
-        cut = capacity // 2
-        sizes, near_ids = [], []
-        for p in range(owners_all):
-            ids = []
-            for size in [cut, capacity - cut] if p % nz == nz - 1 else [capacity]:
-                ids += [len(sizes) * capacity + k for k in range(size)]
-                sizes.append(size)
-            near_ids.append(ids)
-    near_ids = jnp.asarray(near_ids, jnp.int32)[:, :, None]
+    sizes = [capacity] * owners_all if in_pieces else [owners_all * capacity]
+    near_ids = jnp.arange(owners_all * capacity, dtype=jnp.int32).reshape(owners_all, capacity, 1)
     near_slot = jnp.sum(jnp.where(near_match, near_ids, 0), axis=(0, 1))
 
     segment, position = image_layout(lengths[0], tokens)
@@ -740,20 +764,32 @@
             e1 = swap(e0, "core")
         x_mid, c0, branch, x_mid_far = joined(level, 0, ours, theirs, x)
         c1 = swap(c0, "core")
-        u, slope, c0_far, c1_far, keep, send = call(
-            hidden_kernel,
-            [
-                ((tokens, hidden), bf16, STAY),
-                ((tokens, hidden), f32, STAY),
-                ((half, D), bf16, STAY),
-                ((half, D), bf16, STAY),
-                ((half, D), bf16),
-                ((half, D), bf16),
-            ],
-            [c0, c1, bias_1[level : level + 1], w1, w2],
-            "hidden",
-            0,
-        )
+        if level + 1 < LAYERS:
+            u, slope, c0_far, c1_far, keep, send = call(
+                hidden_kernel,
+                [
+                    ((tokens, hidden), bf16, STAY),
+                    ((tokens, hidden), f32, STAY),
+                    ((half, D), bf16, STAY),
+                    ((half, D), bf16, STAY),
+                    ((half, D), bf16),
+                    ((half, D), bf16),
+                ],
+                [c0, c1, bias_1[level : level + 1], w1, w2],
+                "hidden",
+                0,
+            )
+        else:
+            u, dz, c0_far, c1_far, e0_far, e1_far, d_b1, keep, send = call(
+                hidden_turn_kernel,
+                [((tokens, hidden), bf16, STAY)] * 2
+                + [((half, D), bf16, STAY)] * 4
+                + [((1, hidden), f32), ((half, D), bf16), ((half, D), bf16)],
+                [c0, c1, e0, e1, bias_1[level : level + 1], w1, w2],
+                "hidden_turn",
+                0,
+            )
+            slope = None
         state = (x_far, a0_far, a1_far, qkv, mixed, logs, w_head, branch)
         state += (x_mid_far, c0_far, c1_far, u, slope, w1, w2)
         if level + 1 < LAYERS:
@@ -762,7 +798,6 @@
             x, a0, branch_two, x_far = joined(level, 1, ours, theirs, x_mid)
             a1 = swap(a0, "core")
         else:
-            final_parts = (keep, send)
             branch_two = None
         saved.append(state + (branch_two,))
 
@@ -772,20 +807,21 @@
     for level in reversed(range(LAYERS)):
         x_far, a0_far, a1_far, qkv, mixed, logs, w_head, branch = saved[level][:8]
         x_mid_far, c0_far, c1_far, u, slope, w1, w2 = saved[level][8:15]
-        dz, e0_far, e1_far, d_b1, keep, send = call(
-            hidden_back_kernel,
-            [
-                ((tokens, hidden), bf16, STAY),
-                ((half, D), bf16, STAY),
-                ((half, D), bf16, STAY),
-                ((1, hidden), f32),
-                ((half, D), bf16),
-                ((half, D), bf16),
-            ],
-            [e0, e1, w1, w2, slope],
-            "hidden_back",
-            0,
-        )
+        if level + 1 < LAYERS:
+            dz, e0_far, e1_far, d_b1, keep, send = call(
+                hidden_back_kernel,
+                [
+                    ((tokens, hidden), bf16, STAY),
+                    ((half, D), bf16, STAY),
+                    ((half, D), bf16, STAY),
+                    ((1, hidden), f32),
+                    ((half, D), bf16),
+                    ((half, D), bf16),
+                ],
+                [e0, e1, w1, w2, slope],
+                "hidden_back",
+                0,
+            )
         ours = chip_sum(keep, send)
         theirs = swap(ours, "y")
         first = 3 * group * level
@@ -865,28 +901,27 @@
                 )
             e1 = swap(e0, "core")
             above = table_args
+            final_parts = call(
+                project_kernel,
+                [((half, D), bf16), ((half, D), bf16)],
+                [after(u, ours), w2],
+                "project",
+                1,
+            )
             early = chip_sum(after(final_parts[0], e0), after(final_parts[1], e0))
             theirs_early = swap(early[rows:], "y")
         else:
             if not in_pieces:
                 grads = jnp.split(grads[0], owners_all, axis=0)
-                pieces = [[v] for v in grads]
-            else:
-                pieces = []
-                for v in grads:
-                    if pieces and v.shape[0] < capacity and len(pieces[-1]) == 1 and pieces[-1][0].shape[0] < capacity:
-                        pieces[-1].append(v)
-                    else:
-                        pieces.append([v])
             args = [after(table_args[0], grads[0])] + list(table_args[1:])
             tables[0] = call(table_kernel, [((PACKED, 128), f32)], args, "table", 3)[0]
             ours = chip_sum(keep, after(send, grads[0]))
-            scatter = ScatterSums(pieces[:nz], pieces[nz:])
+            scatter = ScatterSums(grads)
             scatter.step()
             input_grad, sums_one = call(
                 last_back_kernel,
                 [((rows, D), f32), ((2, D), f32)],
-                [ours, swap(ours[rows:], "y"), after(x_far, scatter.all_parts[0]), d_mid, shared_params],
+                [ours, swap(ours[rows:], "y"), x_far, d_mid, shared_params],
                 "last_back",
                 0,
                 )
@@ -909,12 +944,12 @@
     shared_part = jnp.concatenate(shared_grads, axis=0)
     shared_part = sum_over(sum_over(shared_part, "core"), "y")
     small = jnp.concatenate([shared_part.reshape(-1, 128)] + tables, axis=0)
+    small = after(small, scatter.parts[0])
+    scatter.step()
     small = small + scatter.along_x.send(small, "x", SWAP)
-    scatter.step()
+    small = after(small, scatter.parts[1])
     step = nz // 2
     while step:
-        if step == 1:
-            small = after(small, scatter.along_x.come[2], scatter.parts[1])
         small = small + lax.ppermute(small, "z", [(i, i ^ step) for i in range(nz)])
         step //= 2
     while len(scatter.parts) < scatter.count:
@@ -943,7 +978,7 @@
 
     my_ids = (my_z * 2 + my_x) * capacity + jnp.arange(capacity, dtype=jnp.int32)
     used = jnp.any(my_ids[:, None] == slots[None, :], axis=1).astype(jnp.int32)
-    base, come = scatter.parts[-1], scatter.come[0][-1]
+    base, come = scatter.parts[-1], scatter.come
     store = (weight_store.shape, f32)
     state = call(
         fetch_kernel,

time: 356 us -> 335 us (0.941)
  waiting for transfers between devices: 221 us -> 196 us
  local copies, waits for them, and re-layouts: 3.68 us -> 10.1 us
    ppermute x17 -> x15, waiting for transfers between devices: 140 us -> 102 us  [send(): self.come.append(lax.ppermute(v, axis, perm))]
    ppermute x2, waiting for transfers between devices: 7.5 us -> 25.5 us  [per_device(): small = small + lax.ppermute(small, 'z', [(i, i ^ step) for i in range(nz)])]
    ppermute x25, waiting for transfers between devices: 73.1 us -> 67.6 us  [swap(): return lax.ppermute(v, axis, [(0, 1), (1, 0)])]
    unnamed x46 -> x72, local copies, waits for them, and re-layouts: 1.08 us -> 6.05 us
    ppermute x2, starting transfers between devices: 4.25 us -> 0.44 us  [per_device(): small = small + lax.ppermute(small, 'z', [(i, i ^ step) for i in range(nz)])]
    convert_element_type x4 -> x3, other arithmetic: 8.19 us -> 7.42 us  [step(): part = part.astype(bf16)]
    ppermute x17 -> x15, starting transfers between devices: 24.3 us -> 25.1 us  [send(): self.come.append(lax.ppermute(v, axis, perm))]
  transfers between devices with their start and end apart: 46 -> 44, of which waited for: 34 -> 30; matrix products, arithmetic and copies ran while one was open for 4% -> 6% of each run, Pallas kernels for 10% -> 10%
where the time goes in v3:
time: 335 us; the launch traced here: 331 us
  waiting for transfers between devices  196 us (59%)
  Pallas kernels  63 us (19%)
  starting transfers between devices  43.4 us (13%)
  other arithmetic  16.4 us (5%)
  local copies, waits for them, and re-layouts  10.1 us (3%)
    ppermute x15, waiting for transfers between devices, send(): self.come.append(lax.ppermute(v, axis, perm))  102 us
    ppermute x25, waiting for transfers between devices, swap(): return lax.ppermute(v, axis, [(0, 1), (1, 0)])  67.6 us
    pallas_call x27, Pallas kernels, call(): pl.pallas_call(functools.partial(kernel, **options), out_shape=shapes, in...  63 us
    ppermute x2, waiting for transfers between devices, per_device(): small = small + lax.ppermute(small, 'z', [(i, i ^ step) for i in range(nz)])  25.5 us
    ppermute x15, starting transfers between devices, send(): self.come.append(lax.ppermute(v, axis, perm))  25.1 us
    ppermute x25, starting transfers between devices, swap(): return lax.ppermute(v, axis, [(0, 1), (1, 0)])  16.3 us
    convert_element_type x3, other arithmetic, step(): part = part.astype(bf16)  7.42 us
  transfers between devices with their start and end apart: 44, of which 30 were waited for; matrix products, arithmetic and copies ran while one was open for 6% of the time, Pallas kernels for 10%

profile of v3, /device:TPU:0, one launch (start us, length us, event | category | flops | bytes accessed | tf_op | source)
XLA Modules:
  0.0 331.3 jit_solution(17484162905202229195)
XLA Ops:
  0.7 1.7 convert_element_type.139.refs_0_
  2.5 4.1 %collective-permute-start.2 = (bf16[10,64,768]{2,1,0:T(8,128)(2,1)S(1)}, bf16[10,64,768]{2,1,0:T(8,128)(2,1)S(1)}, u32[]{:S(2)}, u32[]{:S(2)}) collective-permute-start(bf16[10,64,768]{2,1,0:T(8,128)(2,1)S(1)} %convert_element_type.139.refs_0_), channel_id=1, source_target_pairs={{0,16},{16,24},{24,8},{8,0},{1,17},{17,25},{25,9},{9,1},{2,18},{18... | collective-permute-start | bytes 2949128 | tf_op jit(solution)/shard_map/ppermute | solution.py:107
  12.4 15.2 %collective-permute-done.2.refs_1_ = bf16[10,64,768]{2,1,0:T(8,128)(2,1)S(1)} collective-permute-done((bf16[10,64,768]{2,1,0:T(8,128)(2,1)S(1)}, bf16[10,64,768]{2,1,0:T(8,128)(2,1)S(1)}, u32[]{:S(2)}, u32[]{:S(2)}) %collective-permute-start.2) | collective-permute-done | bytes 983072 | tf_op jit(solution)/shard_map/ppermute | solution.py:107
  27.6 3.4 %collective-permute-start.3 = (bf16[10,64,768]{2,1,0:T(8,128)(2,1)S(1)}, bf16[10,64,768]{2,1,0:T(8,128)(2,1)}, u32[]{:S(2)}, u32[]{:S(2)}) collective-permute-start(bf16[10,64,768]{2,1,0:T(8,128)(2,1)S(1)} %collective-permute-done.2.refs_1_), channel_id=1, source_target_pairs={{0,16},{16,24},{24,8},{8,0},{1,17},{17,25},{25,9},{9,1},{2,18},{18... | collective-permute-start | bytes 2949128 | tf_op jit(solution)/shard_map/ppermute | solution.py:107
  32.9 18.2 %collective-permute-done.3.refs_2_ = bf16[10,64,768]{2,1,0:T(8,128)(2,1)} collective-permute-done((bf16[10,64,768]{2,1,0:T(8,128)(2,1)S(1)}, bf16[10,64,768]{2,1,0:T(8,128)(2,1)}, u32[]{:S(2)}, u32[]{:S(2)}) %collective-permute-start.3) | collective-permute-done | bytes 983072 | tf_op jit(solution)/shard_map/ppermute | solution.py:107
  51.1 3.5 %collective-permute-start.4 = (bf16[10,64,768]{2,1,0:T(8,128)(2,1)}, bf16[10,64,768]{2,1,0:T(8,128)(2,1)}, u32[]{:S(2)}, u32[]{:S(2)}) collective-permute-start(bf16[10,64,768]{2,1,0:T(8,128)(2,1)} %collective-permute-done.3.refs_2_), channel_id=1, source_target_pairs={{0,16},{16,24},{24,8},{8,0},{1,17},{17,25},{25,9},{9,1},{2,18},{18... | collective-permute-start | bytes 2949128 | tf_op jit(solution)/shard_map/ppermute | solution.py:107
  60.3 5.9 %prepare.1 = (bf16[512,256]{1,0:T(8,128)(2,1)S(1)}, bf16[256,512]{1,0:T(8,128)(2,1)S(1)}, f32[3,512,512]{2,1,0:T(8,128)S(1)}, f32[3,512,512]{2,1,0:T(8,128)S(1)}) custom-call(f32[6,32,32]{2,1,0:T(8,128)S(1)} %pad.4.table, f32[6,3]{1,0:T(8,128)S(1)} %slice.176.ends, s32[512,1]{1,0:T(8,128)S(1)} %copy-done.8, s32[512,1]{1,0:T(8,128)S(1)} %copy-done.9, ...), custom_call_target="tpu_custom_call" | custom-call | flops 6000000000 | bytes 1 | tf_op jit(solution)/shard_map/prepare/pallas_call | solution.py:81
  66.3 1.6 copy-done
  69.3 4.8 %collective-permute-done.4.refs_3_ = bf16[10,64,768]{2,1,0:T(8,128)(2,1)} collective-permute-done((bf16[10,64,768]{2,1,0:T(8,128)(2,1)}, bf16[10,64,768]{2,1,0:T(8,128)(2,1)}, u32[]{:S(2)}, u32[]{:S(2)}) %collective-permute-start.4) | collective-permute-done | bytes 983072 | tf_op jit(solution)/shard_map/ppermute | solution.py:107
  74.1 2.4 collective-permute-done.7.refs_6_
  81.1 16.3 %collective-permute-done.8.refs_7_ = bf16[10,64,768]{2,1,0:T(8,128)(2,1)} collective-permute-done((bf16[10,64,768]{2,1,0:T(8,128)(2,1)}, bf16[10,64,768]{2,1,0:T(8,128)(2,1)}, u32[]{:S(2)}, u32[]{:S(2)}) %collective-permute-start.8) | collective-permute-done | bytes 983072 | tf_op jit(solution)/shard_map/ppermute | solution.py:107
  97.4 2.8 deal.2
  100.2 2.8 attention.2
  103.0 1.7 collective-permute-done.9
  104.8 1.6 collective-permute-start.10
  106.4 2.8 deal.3
  109.2 6.8 %collective-permute-done.10.theirs = bf16[256,768]{1,0:T(8,128)(2,1)S(1)} collective-permute-done((bf16[256,768]{1,0:T(8,128)(2,1)S(1)}, bf16[256,768]{1,0:T(8,128)(2,1)S(1)}, u32[]{:S(2)}, u32[]{:S(2)}) %collective-permute-start.10) | collective-permute-done | bytes 393248 | tf_op jit(solution)/shard_map/ppermute | solution.py:97
  116.6 1.7 collective-permute-done.11.c1
  118.3 2.2 hidden.1
  120.7 1.6 collective-permute-done.12
  122.4 1.6 collective-permute-start.13
  123.9 9.6 %collective-permute-done.13.theirs = bf16[256,768]{1,0:T(8,128)(2,1)S(1)} collective-permute-done((bf16[256,768]{1,0:T(8,128)(2,1)S(1)}, bf16[256,768]{1,0:T(8,128)(2,1)S(1)}, u32[]{:S(2)}, u32[]{:S(2)}) %collective-permute-start.13) | collective-permute-done | bytes 393248 | tf_op jit(solution)/shard_map/ppermute | solution.py:97
  134.1 1.7 collective-permute-done.14.a1
  135.8 2.8 attention.3
  138.7 1.6 collective-permute-done.15
  140.4 1.6 collective-permute-start.16
  142.0 9.6 %collective-permute-done.16.theirs = bf16[256,768]{1,0:T(8,128)(2,1)S(1)} collective-permute-done((bf16[256,768]{1,0:T(8,128)(2,1)S(1)}, bf16[256,768]{1,0:T(8,128)(2,1)S(1)}, u32[]{:S(2)}, u32[]{:S(2)}) %collective-permute-start.16) | collective-permute-done | bytes 393248 | tf_op jit(solution)/shard_map/ppermute | solution.py:97
  152.1 1.7 collective-permute-done.17.c1
  153.8 3.2 hidden_turn.1
  157.3 1.6 collective-permute-done.19
  158.9 1.6 collective-permute-start.20
  160.5 3.1 hidden_weights.2
  163.6 6.6 %collective-permute-done.20.theirs = bf16[256,768]{1,0:T(8,128)(2,1)S(1)} collective-permute-done((bf16[256,768]{1,0:T(8,128)(2,1)S(1)}, bf16[256,768]{1,0:T(8,128)(2,1)S(1)}, u32[]{:S(2)}, u32[]{:S(2)}) %collective-permute-start.20) | collective-permute-done | bytes 393248 | tf_op jit(solution)/shard_map/ppermute | solution.py:97
  171.0 1.7 collective-permute-done.21.e1
  172.7 4.1 %attention_back.2 = (bf16[512,576]{1,0:T(8,128)(2,1)S(1)}, bf16[3,512,512]{2,1,0:T(8,128)(2,1)S(1)}, bf16[256,768]{1,0:T(8,128)(2,1)S(1)}, bf16[256,768]{1,0:T(8...) custom-call(bf16[256,768]{1,0:T(8,128)(2,1)S(1)} %get-tuple-element.220.e0, ...), custom_call_target="tpu_custom_call" | custom-call | bytes 1 | tf_op jit(solution)/shard_map/attention_back/pallas_call | solution.py:81
  177.0 1.6 collective-permute-done.22
  178.7 1.6 collective-permute-start.23
  180.3 2.4 attention_weights.2
  182.7 7.3 %collective-permute-done.23.theirs = bf16[256,768]{1,0:T(8,128)(2,1)S(1)} collective-permute-done((bf16[256,768]{1,0:T(8,128)(2,1)S(1)}, bf16[256,768]{1,0:T(8,128)(2,1)S(1)}, u32[]{:S(2)}, u32[]{:S(2)}) %collective-permute-start.23) | collective-permute-done | bytes 393248 | tf_op jit(solution)/shard_map/ppermute | solution.py:97
  192.5 2.5 hidden_back.1
  195.3 1.6 collective-permute-start.25
  198.5 2.8 table.2
  201.3 3.1 hidden_weights.3
  204.4 6.6 %collective-permute-done.28.theirs = bf16[256,768]{1,0:T(8,128)(2,1)S(1)} collective-permute-done((bf16[256,768]{1,0:T(8,128)(2,1)S(1)}, bf16[256,768]{1,0:T(8,128)(2,1)S(1)}, u32[]{:S(2)}, u32[]{:S(2)}) %collective-permute-start.28) | collective-permute-done | bytes 393248 | tf_op jit(solution)/shard_map/ppermute | solution.py:97
  211.8 1.7 collective-permute-done.29.e1
  213.5 4.1 %attention_back.3 = (bf16[512,576]{1,0:T(8,128)(2,1)S(1)}, bf16[3,512,512]{2,1,0:T(8,128)(2,1)S(1)}, bf16[256,768]{1,0:T(8,128)(2,1)S(1)}, bf16[256,768]{1,0:T(8...) custom-call(bf16[256,768]{1,0:T(8,128)(2,1)S(1)} %get-tuple-element.277.e0, ...), custom_call_target="tpu_custom_call" | custom-call | bytes 1 | tf_op jit(solution)/shard_map/attention_back/pallas_call | solution.py:81
  217.7 2.4 attention_weights.3
  220.1 1.6 collective-permute-start.32
  221.8 22.4 %collective-permute-done.32 = bf16[10,64,768]{2,1,0:T(8,128)(2,1)S(1)} collective-permute-done((bf16[10,64,768]{2,1,0:T(8,128)(2,1)}, bf16[10,64,768]{2,1,0:T(8,128)(2,1)S(1)}, u32[]{:S(2)}, u32[]{:S(2)}) %collective-permute-start.32) | collective-permute-done | bytes 983072 | tf_op jit(solution)/shard_map/ppermute | solution.py:107
  245.6 2.4 add_convert_fusion.2
  249.4 1.6 collective-permute-start.31
  251.0 4.1 %collective-permute-done.31.theirs = bf16[128,768]{1,0:T(8,128)(2,1)S(1)} collective-permute-done((bf16[128,768]{1,0:T(8,128)(2,1)S(1)}, bf16[128,768]{1,0:T(8,128)(2,1)S(1)}, u32[]{:S(2)}, u32[]{:S(2)}) %collective-permute-start.31) | collective-permute-done | bytes 196640 | tf_op jit(solution)/shard_map/ppermute | solution.py:97
  257.7 1.6 collective-permute-start.36
  259.3 2.8 table.3
  262.1 5.3 %collective-permute-done.33 = bf16[10,64,768]{2,1,0:T(8,128)(2,1)} collective-permute-done((bf16[10,64,768]{2,1,0:T(8,128)(2,1)}, bf16[10,64,768]{2,1,0:T(8,128)(2,1)}, u32[]{:S(2)}, u32[]{:S(2)}) %collective-permute-start.33) | collective-permute-done | bytes 983072 | tf_op jit(solution)/shard_map/ppermute | solution.py:107
  268.9 3.2 collective-permute-done.34
  272.1 3.1 add_convert_fusion.1
  275.6 5.2 %collective-permute-done.42 = f32[192,128]{1,0:T(8,128)S(1)} collective-permute-done((f32[192,128]{1,0:T(8,128)S(1)}, f32[192,128]{1,0:T(8,128)S(1)}, u32[]{:S(2)}, u32[]{:S(2)}) %collective-permute-start.42) | collective-permute-done | bytes 98336 | tf_op jit(solution)/shard_map/ppermute | solution.py:953
  281.2 2.1 collective-permute-start.39
  283.8 20.2 %collective-permute-done.43 = f32[192,128]{1,0:T(8,128)S(1)} collective-permute-done((f32[192,128]{1,0:T(8,128)S(1)}, f32[192,128]{1,0:T(8,128)S(1)}, u32[]{:S(2)}, u32[]{:S(2)}) %collective-permute-start.43) | collective-permute-done | bytes 98336 | tf_op jit(solution)/shard_map/ppermute | solution.py:953
  306.6 1.9 add_convert_fusion
  309.9 14.4 %collective-permute-done.40 = bf16[10,64,768]{2,1,0:T(8,128)(2,1)S(1)} collective-permute-done((bf16[10,64,768]{2,1,0:T(8,128)(2,1)S(1)}, bf16[10,64,768]{2,1,0:T(8,128)(2,1)S(1)}, u32[]{:S(2)}, u32[]{:S(2)}) %collective-permute-start.40) | collective-permute-done | bytes 983072 | tf_op jit(solution)/shard_map/ppermute | solution.py:107
  324.5 2.8 fetch.1
  327.3 3.7 %update.1 = (f32[10,64,768]{2,1,0:T(8,128)}, f32[10,64,768]{2,1,0:T(8,128)}, f32[10,64,768]{2,1,0:T(8,128)}, f32[10,64,768]{2,1,0:T(8,128)}) custom-call(s32[10]{0:T(128)S(1)} %convert_element_type.167.used, f32[10,64,768]{2,1,0:T(8,128)S(1)} %convert_add_fusion.base, bf16[10,64,768]{2,1,0:T(8,128)(2,1)S(1)} %collective-permute-done.41.come, ...), custom_call_target="tpu_custom_call" | custom-call | flops 3000000000 | bytes 1 | tf_op jit(solution)/shard_map/update/pallas_call | solution.py:81
  (224 shorter events, 40.2 us)
Async XLA Ops:
  0.6 10.2 %copy-start.34 = (s32[4]{0:T(128)S(1)}, s32[4]{0:T(128)}, u32[]{:S(2)}) copy-start(s32[4]{0:T(128)} %constant.135.clone) | copy-start | bytes 52
  0.7 7.4 %copy-start.3 = (bf16[128,768]{1,0:T(8,128)(2,1)S(1)}, bf16[128,768]{1,0:T(8,128)(2,1)}, u32[]{:S(2)}) copy-start(bf16[128,768]{1,0:T(8,128)(2,1)} %grads.1) | copy-start | bytes 589828
  0.7 9.7 %copy-start.27 = (f32[2,1,3348]{2,1,0:T(1,128)S(1)}, f32[2,1,3348]{2,1,0:T(1,128)}, u32[]{:S(2)}) copy-start(f32[2,1,3348]{2,1,0:T(1,128)} %param.26) | copy-start | bytes 80356
  0.7 10.0 %copy-start.32 = (s32[1,6]{1,0:T(1,128)S(1)}, s32[1,6]{1,0:T(1,128)}, u32[]{:S(2)}) copy-start(s32[1,6]{1,0:T(1,128)} %param.18) | copy-start | bytes 76
  0.7 31.8 %copy-start.33 = (s32[72]{0:T(128)S(1)}, s32[72]{0:T(128)}, u32[]{:S(2)}) copy-start(s32[72]{0:T(128)} %param.19) | copy-start | bytes 868
  2.5 55.9 %copy-start.20 = (bf16[10,64,768]{2,1,0:T(8,128)(2,1)}, bf16[10,64,768]{2,1,0:T(8,128)(2,1)S(1)}, u32[]{:S(2)}) copy-start(bf16[10,64,768]{2,1,0:T(8,128)(2,1)S(1)} %convert_element_type.139.refs_0_) | copy-start | bytes 2949124
  2.5 25.1 %collective-permute-start.2 = (bf16[10,64,768]{2,1,0:T(8,128)(2,1)S(1)}, bf16[10,64,768]{2,1,0:T(8,128)(2,1)S(1)}, u32[]{:S(2)}, u32[]{:S(2)}) collective-permute-start(bf16[10,64,768]{2,1,0:T(8,128)(2,1)S(1)} %convert_element_type.139.refs_0_), channel_id=1, source_target_pairs={{0,16},{16,24},{24,8},{8,0},{1,17},{17,25},{25,9},{9,1},{2,18},{18... | collective-permute-start | bytes 2949128 | tf_op jit(solution)/shard_map/ppermute | solution.py:107
  6.6 24.4 %collective-permute-start.5 = (bf16[10,64,768]{2,1,0:T(8,128)(2,1)S(1)}, bf16[10,64,768]{2,1,0:T(8,128)(2,1)S(1)}, u32[]{:S(2)}, u32[]{:S(2)}) collective-permute-start(bf16[10,64,768]{2,1,0:T(8,128)(2,1)S(1)} %convert_element_type.139.refs_0_), channel_id=1, source_target_pairs={{0,4},{4,0},{1,5},{5,1},{2,6},{6,2},{3,7},{7,3},{8,12},{12,8},{9,1... | collective-permute-start | bytes 2949128 | tf_op jit(solution)/shard_map/ppermute | solution.py:107
  8.8 69.7 %collective-permute-start = (bf16[256,768]{1,0:T(8,128)(2,1)}, bf16[256,768]{1,0:T(8,128)(2,1)}, u32[]{:S(2)}, u32[]{:S(2)}) collective-permute-start(bf16[256,768]{1,0:T(8,128)(2,1)} %pad_maximum_fusion), channel_id=1, source_target_pairs={{0,2},{2,0},{1,3},{3,1},{4,6},{6,4},{5,7},{7,5},{8,10},{10,8},{9,1... | collective-permute-start | bytes 1179656 | tf_op jit(solution)/shard_map/ppermute | solution.py:97
  27.6 30.8 %copy-start.23 = (bf16[10,64,768]{2,1,0:T(8,128)(2,1)}, bf16[10,64,768]{2,1,0:T(8,128)(2,1)S(1)}, u32[]{:S(2)}) copy-start(bf16[10,64,768]{2,1,0:T(8,128)(2,1)S(1)} %collective-permute-done.2.refs_1_) | copy-start | bytes 2949124
  27.6 23.5 %collective-permute-start.3 = (bf16[10,64,768]{2,1,0:T(8,128)(2,1)S(1)}, bf16[10,64,768]{2,1,0:T(8,128)(2,1)}, u32[]{:S(2)}, u32[]{:S(2)}) collective-permute-start(bf16[10,64,768]{2,1,0:T(8,128)(2,1)S(1)} %collective-permute-done.2.refs_1_), channel_id=1, source_target_pairs={{0,16},{16,24},{24,8},{8,0},{1,17},{17,25},{25,9},{9,1},{2,18},{18... | collective-permute-start | bytes 2949128 | tf_op jit(solution)/shard_map/ppermute | solution.py:107
  31.0 27.4 %copy-start.24 = (bf16[10,64,768]{2,1,0:T(8,128)(2,1)}, bf16[10,64,768]{2,1,0:T(8,128)(2,1)S(1)}, u32[]{:S(2)}) copy-start(bf16[10,64,768]{2,1,0:T(8,128)(2,1)S(1)} %collective-permute-done.5.refs_4_) | copy-start | bytes 2949124
  31.0 23.6 %collective-permute-start.6 = (bf16[10,64,768]{2,1,0:T(8,128)(2,1)S(1)}, bf16[10,64,768]{2,1,0:T(8,128)(2,1)S(1)}, u32[]{:S(2)}, u32[]{:S(2)}) collective-permute-start(bf16[10,64,768]{2,1,0:T(8,128)(2,1)S(1)} %collective-permute-done.2.refs_1_), channel_id=1, source_target_pairs={{0,4},{4,0},{1,5},{5,1},{2,6},{6,2},{3,7},{7,3},{8,12},{12,8},{9,1... | collective-permute-start | bytes 2949128 | tf_op jit(solution)/shard_map/ppermute | solution.py:107
  51.1 23.0 %collective-permute-start.4 = (bf16[10,64,768]{2,1,0:T(8,128)(2,1)}, bf16[10,64,768]{2,1,0:T(8,128)(2,1)}, u32[]{:S(2)}, u32[]{:S(2)}) collective-permute-start(bf16[10,64,768]{2,1,0:T(8,128)(2,1)} %collective-permute-done.3.refs_2_), channel_id=1, source_target_pairs={{0,16},{16,24},{24,8},{8,0},{1,17},{17,25},{25,9},{9,1},{2,18},{18... | collective-permute-start | bytes 2949128 | tf_op jit(solution)/shard_map/ppermute | solution.py:107
  54.6 21.9 %collective-permute-start.7 = (bf16[10,64,768]{2,1,0:T(8,128)(2,1)}, bf16[10,64,768]{2,1,0:T(8,128)(2,1)}, u32[]{:S(2)}, u32[]{:S(2)}) collective-permute-start(bf16[10,64,768]{2,1,0:T(8,128)(2,1)} %collective-permute-done.3.refs_2_), channel_id=1, source_target_pairs={{0,4},{4,0},{1,5},{5,1},{2,6},{6,2},{3,7},{7,3},{8,12},{12,8},{9,1... | collective-permute-start | bytes 2949128 | tf_op jit(solution)/shard_map/ppermute | solution.py:107
  60.3 18.3 %copy-start.2 = (f32[2,8,768]{2,1,0:T(8,128)S(1)}, f32[2,8,768]{2,1,0:T(8,128)}, u32[]{:S(2)}) copy-start(f32[2,8,768]{2,1,0:T(8,128)} %shared.15) | copy-start | bytes 147460
  76.5 20.9 %collective-permute-start.8 = (bf16[10,64,768]{2,1,0:T(8,128)(2,1)}, bf16[10,64,768]{2,1,0:T(8,128)(2,1)}, u32[]{:S(2)}, u32[]{:S(2)}) collective-permute-start(bf16[10,64,768]{2,1,0:T(8,128)(2,1)} %collective-permute-done.4.refs_3_), channel_id=1, source_target_pairs={{0,4},{4,0},{1,5},{5,1},{2,6},{6,2},{3,7},{7,3},{8,12},{12,8},{9,1... | collective-permute-start | bytes 2949128 | tf_op jit(solution)/shard_map/ppermute | solution.py:107
  81.0 19.2 %collective-permute-start.1 = (bf16[256,768]{1,0:T(8,128)(2,1)S(1)}, bf16[256,768]{1,0:T(8,128)(2,1)S(1)}, u32[]{:S(2)}, u32[]{:S(2)}) collective-permute-start(bf16[256,768]{1,0:T(8,128)(2,1)S(1)} %get-tuple-element.175.a0), channel_id=1, source_target_pairs={{0,1},{1,0},{2,3},{3,2},{4,5},{5,4},{6,7},{7,6},{8,9},{9,8},{10,11... | collective-permute-start | bytes 1179656 | tf_op jit(solution)/shard_map/ppermute | solution.py:97
  103.0 1.8 collective-permute-start.9
  104.8 11.2 %collective-permute-start.10 = (bf16[256,768]{1,0:T(8,128)(2,1)S(1)}, bf16[256,768]{1,0:T(8,128)(2,1)S(1)}, u32[]{:S(2)}, u32[]{:S(2)}) collective-permute-start(bf16[256,768]{1,0:T(8,128)(2,1)S(1)} %add_convert_fusion.10.ours), channel_id=1, source_target_pairs={{0,2},{2,0},{1,3},{3,1},{4,6},{6,4},{5,7},{7,5},{8,10},{10,8},{9,1... | collective-permute-start | bytes 1179656 | tf_op jit(solution)/shard_map/ppermute | solution.py:97
  116.5 1.8 collective-permute-start.11
  118.3 17.5 %copy-start.1 = (f32[3,512,512]{2,1,0:T(8,128)S(1)}, f32[3,512,512]{2,1,0:T(8,128)}, u32[]{:S(2)}) copy-start(f32[3,512,512]{2,1,0:T(8,128)} %copy-done) | copy-start | bytes 9437188
  120.5 1.8 collective-permute-start.12
  122.4 11.2 %collective-permute-start.13 = (bf16[256,768]{1,0:T(8,128)(2,1)S(1)}, bf16[256,768]{1,0:T(8,128)(2,1)S(1)}, u32[]{:S(2)}, u32[]{:S(2)}) collective-permute-start(bf16[256,768]{1,0:T(8,128)(2,1)S(1)} %add_convert_fusion.9.ours), channel_id=1, source_target_pairs={{0,2},{2,0},{1,3},{3,1},{4,6},{6,4},{5,7},{7,5},{8,10},{10,8},{9,1... | collective-permute-start | bytes 1179656 | tf_op jit(solution)/shard_map/ppermute | solution.py:97
  134.0 1.8 collective-permute-start.14
  138.5 1.8 collective-permute-start.15
  140.4 11.2 %collective-permute-start.16 = (bf16[256,768]{1,0:T(8,128)(2,1)S(1)}, bf16[256,768]{1,0:T(8,128)(2,1)S(1)}, u32[]{:S(2)}, u32[]{:S(2)}) collective-permute-start(bf16[256,768]{1,0:T(8,128)(2,1)S(1)} %add_convert_fusion.8.ours), channel_id=1, source_target_pairs={{0,2},{2,0},{1,3},{3,1},{4,6},{6,4},{5,7},{7,5},{8,10},{10,8},{9,1... | collective-permute-start | bytes 1179656 | tf_op jit(solution)/shard_map/ppermute | solution.py:97
  142.0 10.1 %collective-permute-start.18 = (bf16[256,768]{1,0:T(8,128)(2,1)S(1)}, bf16[256,768]{1,0:T(8,128)(2,1)S(1)}, u32[]{:S(2)}, u32[]{:S(2)}) collective-permute-start(bf16[256,768]{1,0:T(8,128)(2,1)S(1)} %get-tuple-element.205.e0), channel_id=1, source_target_pairs={{0,1},{1,0},{2,3},{3,2},{4,5},{5,4},{6,7},{7,6},{8,9},{9,8},{10,11... | collective-permute-start | bytes 1179656 | tf_op jit(solution)/shard_map/ppermute | solution.py:97
  152.0 1.8 collective-permute-start.17
  157.1 1.8 collective-permute-start.19
  158.9 11.2 %collective-permute-start.20 = (bf16[256,768]{1,0:T(8,128)(2,1)S(1)}, bf16[256,768]{1,0:T(8,128)(2,1)S(1)}, u32[]{:S(2)}, u32[]{:S(2)}) collective-permute-start(bf16[256,768]{1,0:T(8,128)(2,1)S(1)} %add_convert_fusion.7.ours), channel_id=1, source_target_pairs={{0,2},{2,0},{1,3},{3,1},{4,6},{6,4},{5,7},{7,5},{8,10},{10,8},{9,1... | collective-permute-start | bytes 1179656 | tf_op jit(solution)/shard_map/ppermute | solution.py:97
  170.9 1.8 collective-permute-start.21
  176.8 1.8 collective-permute-start.22
  178.7 11.2 %collective-permute-start.23 = (bf16[256,768]{1,0:T(8,128)(2,1)S(1)}, bf16[256,768]{1,0:T(8,128)(2,1)S(1)}, u32[]{:S(2)}, u32[]{:S(2)}) collective-permute-start(bf16[256,768]{1,0:T(8,128)(2,1)S(1)} %add_convert_fusion.6.ours), channel_id=1, source_target_pairs={{0,2},{2,0},{1,3},{3,1},{4,6},{6,4},{5,7},{7,5},{8,10},{10,8},{9,1... | collective-permute-start | bytes 1179656 | tf_op jit(solution)/shard_map/ppermute | solution.py:97
  190.7 1.8 collective-permute-start.26
  191.5 3.6 %collective-permute-start.24 = (bf16[256,768]{1,0:T(8,128)(2,1)S(1)}, bf16[256,768]{1,0:T(8,128)(2,1)S(1)}, u32[]{:S(2)}, u32[]{:S(2)}) collective-permute-start(bf16[256,768]{1,0:T(8,128)(2,1)S(1)} %get-tuple-element.249), channel_id=1, source_target_pairs={{0,1},{1,0},{2,3},{3,2},{4,5},{5,4},{6,7},{7,6},{8,9},{9,8},{10,11... | collective-permute-start | bytes 1179656 | tf_op jit(solution)/shard_map/ppermute | solution.py:97
  195.0 1.9 collective-permute-start.27
  195.3 9.1 %collective-permute-start.25 = (bf16[128,768]{1,0:T(8,128)(2,1)S(1)}, bf16[128,768]{1,0:T(8,128)(2,1)S(1)}, u32[]{:S(2)}, u32[]{:S(2)}) collective-permute-start(bf16[128,768]{1,0:T(8,128)(2,1)S(1)} %slice.181), channel_id=1, source_target_pairs={{0,2},{2,0},{1,3},{3,1},{4,6},{6,4},{5,7},{7,5},{8,10},{10,8},{9,1... | collective-permute-start | bytes 589832 | tf_op jit(solution)/shard_map/ppermute | solution.py:97
  197.0 14.0 %collective-permute-start.28 = (bf16[256,768]{1,0:T(8,128)(2,1)S(1)}, bf16[256,768]{1,0:T(8,128)(2,1)S(1)}, u32[]{:S(2)}, u32[]{:S(2)}) collective-permute-start(bf16[256,768]{1,0:T(8,128)(2,1)S(1)} %add_convert_fusion.4.ours), channel_id=1, source_target_pairs={{0,2},{2,0},{1,3},{3,1},{4,6},{6,4},{5,7},{7,5},{8,10},{10,8},{9,1... | collective-permute-start | bytes 1179656 | tf_op jit(solution)/shard_map/ppermute | solution.py:97
  211.7 1.8 collective-permute-start.29
  220.1 24.1 %collective-permute-start.32 = (bf16[10,64,768]{2,1,0:T(8,128)(2,1)}, bf16[10,64,768]{2,1,0:T(8,128)(2,1)S(1)}, u32[]{:S(2)}, u32[]{:S(2)}) collective-permute-start(bf16[10,64,768]{2,1,0:T(8,128)(2,1)} %get-tuple-element.303), channel_id=1, source_target_pairs={{0,4},{4,0},{1,5},{5,1},{2,6},{6,2},{3,7},{7,3},{8,12},{12,8},{9,1... | collective-permute-start | bytes 2949128 | tf_op jit(solution)/shard_map/ppermute | solution.py:107
  221.7 27.6 %collective-permute-start.30 = (bf16[256,768]{1,0:T(8,128)(2,1)S(1)}, bf16[256,768]{1,0:T(8,128)(2,1)S(1)}, u32[]{:S(2)}, u32[]{:S(2)}) collective-permute-start(bf16[256,768]{1,0:T(8,128)(2,1)S(1)} %get-tuple-element.296), channel_id=1, source_target_pairs={{0,1},{1,0},{2,3},{3,2},{4,5},{5,4},{6,7},{7,6},{8,9},{9,8},{10,11... | collective-permute-start | bytes 1179656 | tf_op jit(solution)/shard_map/ppermute | solution.py:97
  244.1 23.3 %collective-permute-start.33 = (bf16[10,64,768]{2,1,0:T(8,128)(2,1)}, bf16[10,64,768]{2,1,0:T(8,128)(2,1)}, u32[]{:S(2)}, u32[]{:S(2)}) collective-permute-start(bf16[10,64,768]{2,1,0:T(8,128)(2,1)} %get-tuple-element.306), channel_id=1, source_target_pairs={{0,4},{4,0},{1,5},{5,1},{2,6},{6,2},{3,7},{7,3},{8,12},{12,8},{9,1... | collective-permute-start | bytes 2949128 | tf_op jit(solution)/shard_map/ppermute | solution.py:107
  248.1 24.0 %collective-permute-start.34 = (bf16[10,64,768]{2,1,0:T(8,128)(2,1)}, bf16[10,64,768]{2,1,0:T(8,128)(2,1)}, u32[]{:S(2)}, u32[]{:S(2)}) collective-permute-start(bf16[10,64,768]{2,1,0:T(8,128)(2,1)} %add_convert_fusion.2), channel_id=1, source_target_pairs={{16,0},{24,16},{8,24},{0,8},{17,1},{25,17},{9,25},{1,9},{18,2},{26... | collective-permute-start | bytes 2949128 | tf_op jit(solution)/shard_map/ppermute | solution.py:107
  249.3 10.0 %copy-start.7 = (bf16[512,576]{1,0:T(8,128)(2,1)S(1)}, bf16[512,576]{1,0:T(8,128)(2,1)}, u32[]{:S(2)}) copy-start(bf16[512,576]{1,0:T(8,128)(2,1)} %copy-done.6) | copy-start | bytes 1769476
  249.3 10.0 %copy-start.11 = (bf16[3,512,512]{2,1,0:T(8,128)(2,1)S(1)}, bf16[3,512,512]{2,1,0:T(8,128)(2,1)}, u32[]{:S(2)}) copy-start(bf16[3,512,512]{2,1,0:T(8,128)(2,1)} %copy-done.10) | copy-start | bytes 4718596
  249.3 10.0 %copy-start.14 = (bf16[512,256]{1,0:T(8,128)(2,1)S(1)}, bf16[512,256]{1,0:T(8,128)(2,1)}, u32[]{:S(2)}) copy-start(bf16[512,256]{1,0:T(8,128)(2,1)} %copy-done.12) | copy-start | bytes 786436
  249.3 10.0 %copy-start.17 = (bf16[256,512]{1,0:T(8,128)(2,1)S(1)}, bf16[256,512]{1,0:T(8,128)(2,1)}, u32[]{:S(2)}) copy-start(bf16[256,512]{1,0:T(8,128)(2,1)} %copy-done.15) | copy-start | bytes 786436
  249.4 5.7 %collective-permute-start.31 = (bf16[128,768]{1,0:T(8,128)(2,1)S(1)}, bf16[128,768]{1,0:T(8,128)(2,1)S(1)}, u32[]{:S(2)}, u32[]{:S(2)}) collective-permute-start(bf16[128,768]{1,0:T(8,128)(2,1)S(1)} %slice.182), channel_id=1, source_target_pairs={{0,2},{2,0},{1,3},{3,1},{4,6},{6,4},{5,7},{7,5},{8,10},{10,8},{9,1... | collective-permute-start | bytes 589832 | tf_op jit(solution)/shard_map/ppermute | solution.py:97
  256.3 1.3 collective-permute-start.35
  257.7 4.4 %collective-permute-start.36 = (f32[16,768]{1,0:T(8,128)S(1)}, f32[16,768]{1,0:T(8,128)S(1)}, u32[]{:S(2)}, u32[]{:S(2)}) collective-permute-start(f32[16,768]{1,0:T(8,128)S(1)} %add.260), channel_id=1, source_target_pairs={{0,2},{2,0},{1,3},{3,1},{4,6},{6,4},{5,7},{7,5},{8,10},{10,8},{9,1... | collective-permute-start | bytes 147464 | tf_op jit(solution)/shard_map/ppermute | solution.py:163
  262.1 21.1 %copy-start.22 = (bf16[10,64,768]{2,1,0:T(8,128)(2,1)S(1)}, bf16[10,64,768]{2,1,0:T(8,128)(2,1)}, u32[]{:S(2)}) copy-start(bf16[10,64,768]{2,1,0:T(8,128)(2,1)} %get-tuple-element.318) | copy-start | bytes 2949124
  267.4 7.8 %collective-permute-start.37 = (f32[192,128]{1,0:T(8,128)S(1)}, f32[192,128]{1,0:T(8,128)S(1)}, u32[]{:S(2)}, u32[]{:S(2)}) collective-permute-start(f32[192,128]{1,0:T(8,128)S(1)} %pad_maximum_fusion.1), channel_id=1, source_target_pairs={{0,4},{4,0},{1,5},{5,1},{2,6},{6,2},{3,7},{7,3},{8,12},{12,8},{9,1... | collective-permute-start | bytes 294920 | tf_op jit(solution)/shard_map/ppermute | solution.py:107
  275.2 29.9 %copy-start.30 = (f32[2,1,3348]{2,1,0:T(1,128)S(1)}, f32[2,1,3348]{2,1,0:T(1,128)}, u32[]{:S(2)}) copy-start(f32[2,1,3348]{2,1,0:T(1,128)} %param.28) | copy-start | bytes 80356
  275.2 29.9 %copy-start.31 = (f32[2,1,3348]{2,1,0:T(1,128)S(1)}, f32[2,1,3348]{2,1,0:T(1,128)}, u32[]{:S(2)}) copy-start(f32[2,1,3348]{2,1,0:T(1,128)} %param.27) | copy-start | bytes 80356
  275.2 30.8 %copy-start.21 = (bf16[10,64,768]{2,1,0:T(8,128)(2,1)S(1)}, bf16[10,64,768]{2,1,0:T(8,128)(2,1)}, u32[]{:S(2)}) copy-start(bf16[10,64,768]{2,1,0:T(8,128)(2,1)} %get-tuple-element.322) | copy-start | bytes 2949124
  275.2 31.4 %copy-start.19 = (bf16[10,64,768]{2,1,0:T(8,128)(2,1)S(1)}, bf16[10,64,768]{2,1,0:T(8,128)(2,1)}, u32[]{:S(2)}) copy-start(bf16[10,64,768]{2,1,0:T(8,128)(2,1)} %get-tuple-element.307) | copy-start | bytes 2949124
  275.3 5.6 %collective-permute-start.42 = (f32[192,128]{1,0:T(8,128)S(1)}, f32[192,128]{1,0:T(8,128)S(1)}, u32[]{:S(2)}, u32[]{:S(2)}) collective-permute-start(f32[192,128]{1,0:T(8,128)S(1)} %add.265), channel_id=1, source_target_pairs={{0,16},{8,24},{16,0},{24,8},{1,17},{9,25},{17,1},{25,9},{2,18},{10... | collective-permute-start | bytes 294920 | tf_op jit(solution)/shard_map/ppermute | solution.py:953
  280.9 23.1 %collective-permute-start.43 = (f32[192,128]{1,0:T(8,128)S(1)}, f32[192,128]{1,0:T(8,128)S(1)}, u32[]{:S(2)}, u32[]{:S(2)}) collective-permute-start(f32[192,128]{1,0:T(8,128)S(1)} %add.266), channel_id=1, source_target_pairs={{0,8},{8,0},{16,24},{24,16},{1,9},{9,1},{17,25},{25,17},{2,10},{10... | collective-permute-start | bytes 294920 | tf_op jit(solution)/shard_map/ppermute | solution.py:953
  281.2 25.5 %collective-permute-start.39 = (bf16[10,64,768]{2,1,0:T(8,128)(2,1)}, bf16[10,64,768]{2,1,0:T(8,128)(2,1)}, u32[]{:S(2)}, u32[]{:S(2)}) collective-permute-start(bf16[10,64,768]{2,1,0:T(8,128)(2,1)} %add_convert_fusion.1), channel_id=1, source_target_pairs={{16,0},{24,16},{8,24},{0,8},{17,1},{25,17},{9,25},{1,9},{18,2},{26... | collective-permute-start | bytes 2949128 | tf_op jit(solution)/shard_map/ppermute | solution.py:107
  283.2 22.8 %collective-permute-start.38 = (bf16[10,64,768]{2,1,0:T(8,128)(2,1)S(1)}, bf16[10,64,768]{2,1,0:T(8,128)(2,1)}, u32[]{:S(2)}, u32[]{:S(2)}) collective-permute-start(bf16[10,64,768]{2,1,0:T(8,128)(2,1)S(1)} %copy-done.22), channel_id=1, source_target_pairs={{0,4},{4,0},{1,5},{5,1},{2,6},{6,2},{3,7},{7,3},{8,12},{12,8},{9,1... | collective-permute-start | bytes 2949128 | tf_op jit(solution)/shard_map/ppermute | solution.py:107
  306.0 18.3 %copy-start.18 = (bf16[10,64,768]{2,1,0:T(8,128)(2,1)S(1)}, bf16[10,64,768]{2,1,0:T(8,128)(2,1)}, u32[]{:S(2)}) copy-start(bf16[10,64,768]{2,1,0:T(8,128)(2,1)} %get-tuple-element.320) | copy-start | bytes 2949124
  306.0 18.3 %collective-permute-start.40 = (bf16[10,64,768]{2,1,0:T(8,128)(2,1)S(1)}, bf16[10,64,768]{2,1,0:T(8,128)(2,1)S(1)}, u32[]{:S(2)}, u32[]{:S(2)}) collective-permute-start(bf16[10,64,768]{2,1,0:T(8,128)(2,1)S(1)} %copy-done.21), channel_id=1, source_target_pairs={{0,4},{4,0},{1,5},{5,1},{2,6},{6,2},{3,7},{7,3},{8,12},{12,8},{9,1... | collective-permute-start | bytes 2949128 | tf_op jit(solution)/shard_map/ppermute | solution.py:107
  308.5 18.8 %collective-permute-start.41 = (bf16[10,64,768]{2,1,0:T(8,128)(2,1)S(1)}, bf16[10,64,768]{2,1,0:T(8,128)(2,1)S(1)}, u32[]{:S(2)}, u32[]{:S(2)}) collective-permute-start(bf16[10,64,768]{2,1,0:T(8,128)(2,1)S(1)} %add_convert_fusion), channel_id=1, source_target_pairs={{16,0},{24,16},{8,24},{0,8},{17,1},{25,17},{9,25},{1,9},{18,2},{26... | collective-permute-start | bytes 2949128 | tf_op jit(solution)/shard_map/ppermute | solution.py:107
  (15 other events, 37.2 us)
